TPU v7x, 256 devices: a whole 4x4x8 slice. The times are simulated.
256 devices in a mesh: gx: 16 (over z, core), gy: 4 (over x), gz: 4 (over y).
Axes of the slice: x: 4, y: 4, z: 8, core: 2. Of those that a mesh axis runs over, the one named last changes fastest.
Arguments:
- velocity: float32 [3, 64, 128, 2048], P(None, 'gz', 'gy', 'gx'), may hold values from 0.2 to 1.5
- adjoint: float32 [3, 64, 128, 2048], P(None, 'gz', 'gy', 'gx'), may hold values from -6 to 6
- pressure: float32 [64, 128, 2048], P('gz', 'gy', 'gx'), may hold values from -6 to 6
- viscosity: float32 [64, 128, 2048], P('gz', 'gy', 'gx'), may hold values from 0.02 to 0.2
- disk_cells: int32 [131072], P(('gx', 'gy', 'gz')), may hold values from 0 to 65535, as said below
- disk_turbine: int32 [131072], P(('gx', 'gy', 'gz')), may hold values from 0 to 1023, as said below
- disk_weight: float32 [131072], P(('gx', 'gy', 'gz')), may hold values from 0.01 to 0.03
- disk_dweight: float32 [2, 131072], P(None, ('gx', 'gy', 'gz')), may hold values from -0.75 to 0.75
- yaw: float32 [1024], P(('gx', 'gy', 'gz')), may hold values from -0.5 to 0.5
- thrust_coef: float32 [1024], P(('gx', 'gy', 'gz')), may hold values from 0.6 to 0.9
- owner_slot: int32 [1024], replicated, may hold values from 0 to 1023, each once
Outputs:
- velocity_next: float32 [3, 64, 128, 2048], P(None, 'gz', 'gy', 'gx')
- adjoint_next: float32 [3, 64, 128, 2048], P(None, 'gz', 'gy', 'gx')
- pressure_next: float32 [64, 128, 2048], P('gz', 'gy', 'gx')
- yaw_grad: float32 [1024], P(('gx', 'gy', 'gz'))
- position_grad: float32 [2, 1024], P(None, ('gx', 'gy', 'gz'))
Inputs may be any that keep to these rules, and one draw needn't show every extreme that they name: `disk_cells`: a cell of the entry's own device tile. `disk_turbine`: every turbine has entries; turbine t belongs to the column of tiles number t // (4 * 4), numbered bx * 4 + by, and its entries lie on the tiles of that column or of the columns just before and after it streamwise.
All inputs are finite; a program needn't handle non-finite values.
Results may differ from a plain program's by a relative error of at most 0.00027.
Values sent between devices are 32-bit elements; how exact they have to be, the bound alone decides.
No kernel may reach another device: no remote copies, remote signals or barrier semaphores. Data moves between devices by JAX's collectives and lax.ppermute only.
A program may use at most 64 MiB of HBM per device.

v0:
```python
import functools

import jax
import jax.numpy as jnp
from jax import lax
from jax.experimental import pallas as pl
from jax.experimental.pallas import tpu as pltpu
from jax.sharding import PartitionSpec as P

SWEEPS = 8
DT = 0.2
F32 = jnp.float32
BF16 = jnp.bfloat16
CZ, CY, CX = 16, 32, 128
KJ = CZ * CY
H = 8
EZ, EY = CZ + 2 * H, CY + 2 * H
SZ = CZ + 2
TILES = EY // H
PADR = 8
PER = 16
WIN = 64
YAW = 112
NN = (((1,), (0,)), ((), ()))
NT = (((1,), (1,)), ((), ()))
TN = (((0,), (0,)), ((), ()))


def iota(shape, dim):
    return lax.broadcasted_iota(jnp.int32, shape, dim)


def pieces(x, count):
    parts = []
    for _ in range(count):
        head = x.astype(BF16)
        parts.append(head)
        x = x - head.astype(F32)
    return parts


def dots(left, right, dims):
    total = None
    for a in left:
        for b in right:
            term = lax.dot_general(a, b, dims, preferred_element_type=F32)
            total = term if total is None else total + term
    return total


def onehot(mask):
    return jnp.where(mask, 1.0, 0.0).astype(BF16)


def roll(x, shift, axis):
    return pltpu.roll(x, shift % x.shape[axis], axis)


def entry_onehots(cells):
    row = lax.shift_right_logical(cells, 7)
    lane = jnp.bitwise_and(cells, CX - 1)
    count = cells.shape[1]
    rows = onehot(iota((KJ, count), 0) == row)
    lanes = iota((CX, count), 0) == lane
    return rows, lanes


def window_lane(turbine, bx, n_gy):
    column_x = lax.shift_right_logical(turbine, 4) // n_gy
    return WIN + (column_x - bx + 1) * PER + jnp.bitwise_and(turbine, PER - 1)


def lookup(table_ref, turbine):
    count = turbine.shape[1]
    table = table_ref[...]
    owner = lax.shift_right_logical(table, 2).astype(F32)
    which = jnp.bitwise_and(table, 3).astype(F32)
    rows = table.shape[0]
    high = lax.shift_right_logical(turbine, 7)
    low = onehot(iota((CX, count), 0) == jnp.bitwise_and(turbine, CX - 1))
    keep = iota((rows, count), 0) == high
    out = []
    for part in (owner, which):
        picked = dots([part.astype(BF16)], [low], NN)
        picked = jnp.sum(jnp.where(keep, picked, 0.0), axis=0, keepdims=True)
        out.append(picked.astype(jnp.int32))
    return out


def entry_kernel(
    n_dev, n_gy, pos_ref, yaw_ref, ct_ref, vel_hbm, adj_hbm, visc_hbm, cells_ref, turb_ref, weight_ref, dweight_ref, owner_ref,
    pay_ref, xr_ref, xl_ref, yr_ref, yl_ref, zr_ref, zl_ref, fld_ref, index_ref, scale_ref, table_ref, out_ref, sems,
):
    order = (0, 3, 4, 1, 2, 5, 6)
    copies = {}
    for f in order:
        hbm = vel_hbm.at[f] if f < 3 else adj_hbm.at[f - 3] if f < 6 else visc_hbm
        copies[f] = pltpu.make_async_copy(hbm, fld_ref.at[f], sems.at[f])
        copies[f].start()
    bx = pos_ref[0]
    cells, turbine, weight = cells_ref[...], turb_ref[...], weight_ref[...]
    index_ref[0:1, :] = cells
    index_ref[1:2, :] = turbine
    scale_ref[...] = weight
    table_ref[...] = owner_ref[...]
    count = cells.shape[1]
    rows, lanes = entry_onehots(cells)
    owner, which = lookup(owner_ref, turbine)
    to_owner = onehot(iota((n_dev, count), 0) == owner)
    in_window = onehot(iota((CX, count), 0) == window_lane(turbine, bx, n_gy))

    columns = []
    for f in order[:3]:
        copies[f].wait()
        columns += pieces(fld_ref[f].reshape(KJ, CX), 2)
    at_row = dots([jnp.concatenate(columns, axis=1)], [rows], TN)
    gathered = []
    for k in range(3):
        both = at_row[2 * k * CX:(2 * k + 1) * CX] + at_row[(2 * k + 1) * CX:(2 * k + 2) * CX]
        gathered.append(jnp.sum(jnp.where(lanes, both, 0.0), axis=0, keepdims=True))
    factors = [weight, dweight_ref[0:1, :], dweight_ref[1:2, :]]
    values = [f * g for f in factors for g in gathered]

    sub = iota((PER, count), 0)
    stacked = jnp.zeros((PER, count), F32)
    for v, value in enumerate(values):
        stacked = jnp.where(sub == v, value, stacked)
    per_slot = jnp.concatenate(
        [jnp.where(which == i, stacked, 0.0) for i in range(4)] + [jnp.zeros((CX - 4 * PER, count), F32)], axis=0
    )
    payload = dots([to_owner], pieces(per_slot, 2), NT)

    speed = jnp.broadcast_to(values[0], (8, count))
    shared = dots(pieces(speed, 2), [in_window], NT)[0:1, :]
    lane = iota((1, CX), 1)
    for i in range(4):
        shared = jnp.where(lane == YAW + i, yaw_ref[i], shared)
        shared = jnp.where(lane == YAW + 4 + i, ct_ref[i], shared)
    out_ref[...] = payload + shared
    leaving = pltpu.make_async_copy(out_ref, pay_ref, sems.at[7])
    leaving.start()

    for f in order[3:]:
        copies[f].wait()
    lane = iota((H, CX), 1)
    for t in range(CY // H):
        at = slice(H * t, H * t + H)
        right = jnp.zeros((H, CX), F32)
        left = jnp.zeros((H, CX), F32)
        for f in range(6):
            for z in range(CZ):
                tile = fld_ref[f, z, at]
                spot = lane == f * CZ + z
                right = jnp.where(spot, roll(tile, f * CZ + z + 1, 1), right)
                left = jnp.where(spot, roll(tile, f * CZ + z, 1), left)
        xr_ref[at] = right
        xl_ref[at] = left
    for f in range(6):
        yr_ref[f * CZ:(f + 1) * CZ, :] = fld_ref[f, :, CY - 1, :]
        yl_ref[f * CZ:(f + 1) * CZ, :] = fld_ref[f, :, 0, :]
        zr_ref[f] = fld_ref[f, CZ - 1]
        zl_ref[f] = fld_ref[f, 0]
    leaving.wait()


def turbine_terms(speed, yaw, thrust_coef):
    cosine = jnp.cos(yaw)
    sine = jnp.sin(yaw)
    magnitude = jnp.abs(speed)
    force = 0.5 * thrust_coef * speed * magnitude * cosine * cosine
    weighting = 1.5 * thrust_coef * speed * magnitude * cosine * cosine * cosine
    return cosine, sine, magnitude, force, weighting


def owner_outputs(got, yaw_ref, ct_ref, yaw_out, pos_out):
    total = jnp.sum(got, axis=0, keepdims=True)
    total = jnp.broadcast_to(total, (8, CX))
    lane = iota((8, CX), 1)
    yaw = jnp.zeros((8, CX), F32)
    ct = jnp.zeros((8, CX), F32)
    for i in range(4):
        yaw = jnp.where(lane == i * PER, yaw_ref[i], yaw)
        ct = jnp.where(lane == i * PER, ct_ref[i], ct)

    def at(v):
        return roll(total, -v, 1)

    speed, dual_x, dual_y = total, at(1), at(2)
    cosine, sine, magnitude, force, weighting = turbine_terms(speed, yaw, ct)
    yaw_grad = -1.5 * ct * magnitude * magnitude * magnitude * cosine * cosine * sine + force * (
        sine * dual_x - cosine * dual_y
    )
    grads = [yaw_grad]
    for r in range(2):
        grads.append(weighting * at(3 + 3 * r) - force * cosine * at(4 + 3 * r) - force * sine * at(5 + 3 * r))
    packed = []
    for grad in grads:
        out = jnp.zeros((8, CX), F32)
        for i in range(4):
            out = jnp.where(lane == i, roll(grad, -(PER - 1) * i, 1), out)
        packed.append(out)
    yaw_out[...] = packed[0][0:1, 0:4]
    pos_out[0:1, :] = packed[1][0:1, 0:4]
    pos_out[1:2, :] = packed[2][0:1, 0:4]


def window_terms(got, n_dev, n_gx, n_gy, n_gz, bx, by, owner_ref):
    lane = iota((1, CX), 1)
    inside = jnp.logical_and(lane >= WIN, lane < WIN + 3 * PER)
    row = iota((n_dev, CX), 0)
    speed = jnp.zeros((1, CX), F32)
    for delta in range(-2, 3):
        base = ((bx + delta) * n_gy + by) * n_gz
        keep = jnp.logical_and(row >= base, row < base + n_gz)
        part = jnp.sum(jnp.where(keep, got, 0.0), axis=0, keepdims=True)
        part = jnp.broadcast_to(jnp.where(inside, part, 0.0), (8, CX))
        speed = speed + roll(part, delta * PER, 1)[0:1, :]
    speed = jnp.where(inside, speed, 0.0)

    table = owner_ref[...]
    sub = iota(table.shape, 0)
    slots = jnp.zeros((1, CX), jnp.int32)
    for j in range(3):
        column_x = jnp.clip(bx - 1 + j, 0, n_gx - 1)
        first = (column_x * n_gy + by) * PER
        picked = jnp.sum(jnp.where(sub == first // CX, table, 0), axis=0, keepdims=True)
        picked = jnp.broadcast_to(picked, (8, CX))
        moved = pltpu.roll(picked, jnp.bitwise_and(WIN + PER * j - first, CX - 1), 1)[0:1, :]
        here = jnp.logical_and(lane >= WIN + PER * j, lane < WIN + PER * (j + 1))
        slots = jnp.where(here, moved, slots)
    owner = onehot(iota((n_dev, CX), 0) == lax.shift_right_logical(slots, 2))
    which = jnp.bitwise_and(slots, 3)
    found = dots(pieces(got, 3), [owner], TN)
    yaw = jnp.zeros((1, CX), F32)
    ct = jnp.zeros((1, CX), F32)
    for i in range(4):
        yaw = jnp.where(which == i, found[YAW + i:YAW + i + 1, :], yaw)
        ct = jnp.where(which == i, found[YAW + 4 + i:YAW + 5 + i, :], ct)
    cosine, sine, magnitude, force, weighting = turbine_terms(speed, yaw, ct)
    keep = lambda x: jnp.where(inside, x, 0.0)
    return keep(force * cosine), keep(force * sine), keep(weighting)


def edges(pos_ref, dims):
    n_dev, n_gx, n_gy, n_gz = dims
    out = []
    for k, count in enumerate((n_gx, n_gy, n_gz)):
        out.append(jnp.where(pos_ref[k] > 0, 1.0, 0.0))
        out.append(jnp.where(pos_ref[k] < count - 1, 1.0, 0.0))
    return out


def tile_rows(t):
    return slice(H * t, H * t + H)


def south_of(ref, index, t, sub):
    if t > 0:
        return ref[index + (slice(H * t - 1, H * t + H - 1),)]
    return jnp.where(sub == 0, 0.0, roll(ref[index + (tile_rows(0),)], 1, 0))


def north_of(ref, index, t, sub):
    if t < CY // H - 1:
        return ref[index + (slice(H * t + 1, H * t + H + 1),)]
    return jnp.where(sub == H - 1, 0.0, roll(ref[index + (tile_rows(t),)], -1, 0))


def base_kernel(
    dims, pos_ref, fld_ref, index_ref, scale_ref, owner_ref, got_ref,
    pred_ref, dual_ref, field_ref,
):
    n_dev, n_gx, n_gy, n_gz = dims
    bx, by = pos_ref[0], pos_ref[1]
    terms = window_terms(got_ref[...], n_dev, n_gx, n_gy, n_gz, bx, by, owner_ref)
    cells, turbine, weight = index_ref[0:1, :], index_ref[1:2, :], scale_ref[...]
    count = cells.shape[1]
    rows, lanes = entry_onehots(cells)
    in_window = onehot(iota((CX, count), 0) == window_lane(turbine, bx, n_gy))
    stacked = jnp.concatenate([jnp.broadcast_to(t, (8, CX)) for t in terms], axis=0)
    per_entry = dots(pieces(stacked, 2), [in_window], NN)
    for c in range(3):
        value = per_entry[8 * c:8 * c + 1, :] * weight
        if c < 2:
            value = -value
        spread = jnp.where(lanes, value, 0.0)
        field_ref[c] = dots([rows], pieces(spread, 2), NT).reshape(CZ, CY, CX)

    lane = iota((H, CX), 1)
    sub = iota((H, CX), 0)
    zero = jnp.zeros((H, CX), F32)
    for t in range(CY // H):
        at = tile_rows(t)
        for f in range(6):
            out, comp = (pred_ref, f) if f < 3 else (dual_ref, f - 3)
            below, tile = zero, fld_ref[f, 0, at]
            for z in range(CZ):
                above = fld_ref[f, z + 1, at] if z < CZ - 1 else zero
                south, north = south_of(fld_ref, (f, z), t, sub), north_of(fld_ref, (f, z), t, sub)
                west = jnp.where(lane == 0, 0.0, roll(tile, 1, 1))
                east = jnp.where(lane == CX - 1, 0.0, roll(tile, -1, 1))
                lap = (above + below) + (north + south) + (east + west) - 6.0 * tile
                rate = fld_ref[6, z, at] * lap
                rate = rate + (west - tile if f < 3 else east - tile)
                if f < 2:
                    rate = rate + field_ref[f, z, at]
                if f == 3:
                    rate = rate + field_ref[2, z, at]
                out[comp, z, at] = tile + DT * rate
                below, tile = tile, above


def add_faces(f, first, out, given, fld_ref, bounds, xlo_ref, xhi_ref, ylo_ref, yhi_ref, zlo_ref, zhi_ref):
    lo_x, hi_x, lo_y, hi_y, lo_z, hi_z = bounds
    lane = iota((H, CX), 1)
    sub = iota((H, CX), 0)
    flow = f < 3
    comp = f - first
    for t in range(CY // H):
        at = tile_rows(t)
        face_lo, face_hi = xlo_ref[at] * lo_x, xhi_ref[at] * hi_x
        for z in range(CZ):
            spot = f * CZ + z
            west = jnp.where(lane == 0, roll(face_lo, -spot, 1), 0.0)
            east = jnp.where(lane == CX - 1, roll(face_hi, CX - 1 - spot, 1), 0.0)
            lap = west + east
            if t == 0:
                lap = lap + jnp.where(sub == 0, ylo_ref[spot:spot + 1, :] * lo_y, 0.0)
            if t == CY // H - 1:
                lap = lap + jnp.where(sub == H - 1, yhi_ref[spot:spot + 1, :] * hi_y, 0.0)
            if z == 0:
                lap = lap + zlo_ref[f, at] * lo_z
            if z == CZ - 1:
                lap = lap + zhi_ref[f, at] * hi_z
            out[comp, z, at] = given[comp, z, at] + DT * (fld_ref[6, z, at] * lap + (west if flow else east))


def fold_shift(z):
    return H + 16 * (z % 8)


def flow_kernel(
    dims, pos_ref, base_ref, fld_ref, xlo_ref, xhi_ref, ylo_ref, yhi_ref, zlo_ref, zhi_ref,
    pred_ref, dm_ref, ds_ref, xr_ref, xl_ref,
):
    bounds = edges(pos_ref, dims)
    for f in range(3):
        add_faces(f, 0, pred_ref, base_ref, fld_ref, bounds, xlo_ref, xhi_ref, ylo_ref, yhi_ref, zlo_ref, zhi_ref)
    lane = iota((H, CX), 1)
    sub = iota((H, CX), 0)
    zero = jnp.zeros((H, CX), F32)
    for r in range(EY // H):
        at = tile_rows(r)
        t = r - 1
        inside = 0 <= t < CY // H
        for k in range(SZ):
            z = k - 1
            main, side = zero, zero
            if inside and 0 <= z < CZ:
                own = tile_rows(t)
                p0 = pred_ref[0, z, own]
                west, east = roll(p0, 1, 1), roll(p0, -1, 1)
                div = jnp.where(lane == CX - 1, 0.0, east) - jnp.where(lane == 0, 0.0, west)
                div = div + (north_of(pred_ref, (1, z), t, sub) - south_of(pred_ref, (1, z), t, sub))
                if z < CZ - 1:
                    div = div + pred_ref[2, z + 1, own]
                if z > 0:
                    div = div - pred_ref[2, z - 1, own]
                main = 0.5 * div
                side = jnp.where(lane == CX - 1, 0.5 * east, jnp.where(lane == 0, -0.5 * west, 0.0))
            elif inside:
                main = 0.5 * pred_ref[2, 0, tile_rows(t)] if z < 0 else -0.5 * pred_ref[2, CZ - 1, tile_rows(t)]
            elif 0 <= z < CZ and t < 0:
                main = jnp.where(sub == H - 1, 0.5 * roll(pred_ref[1, z, 0:H], -1, 0), 0.0)
            elif 0 <= z < CZ:
                main = jnp.where(sub == 0, -0.5 * roll(pred_ref[1, z, CY - H:CY], 1, 0), 0.0)
            dm_ref[k, at] = main
            ds_ref[k, at] = side
    for r in range(EY // H):
        at = tile_rows(r)
        right, left = [zero] * 3, [zero] * 3
        for k in range(SZ):
            if not 0 < r < EY // H - 1 and not 0 < k < SZ - 1:
                continue
            main, side = dm_ref[k, at], ds_ref[k, at]
            g = k % 8
            mine = jnp.logical_and(lane >= 16 * g, lane < 16 * g + 16)
            right[k // 8] = jnp.where(mine, roll(jnp.where(lane < H, side, main), fold_shift(k), 1), right[k // 8])
            left[k // 8] = jnp.where(mine, roll(jnp.where(lane < H, main, side), fold_shift(k), 1), left[k // 8])
        for i in range(3):
            xr_ref[i, at] = right[i]
            xl_ref[i, at] = left[i]


def dual_kernel(
    dims, pos_ref, yaw_ref, ct_ref, base_ref, fld_ref, got_ref, xlo_ref, xhi_ref, ylo_ref, yhi_ref, zlo_ref, zhi_ref,
    dual_out, yaw_out, pos_out, dual_ref, sems,
):
    bounds = edges(pos_ref, dims)
    copies = []
    for f in range(3, 6):
        add_faces(f, 3, dual_ref, base_ref, fld_ref, bounds, xlo_ref, xhi_ref, ylo_ref, yhi_ref, zlo_ref, zhi_ref)
        copies.append(pltpu.make_async_copy(dual_ref.at[f - 3], dual_out.at[f - 3], sems.at[f - 3]))
        copies[-1].start()
    owner_outputs(got_ref[...], yaw_ref, ct_ref, yaw_out, pos_out)
    for copy in copies:
        copy.wait()


def x_kernel(dims, pos_ref, dm_ref, ds_ref, lo_ref, hi_ref, om_ref, os_ref, up_ref, down_ref):
    in_lo, in_hi = edges(pos_ref, dims)[0:2]
    lane = iota((H, CX), 1)
    head, tail = lane < H, lane >= CX - H
    zero = jnp.zeros((H, CX), F32)
    for r in range(EY // H):
        at = tile_rows(r)
        lows = [lo_ref[i, at] * in_lo for i in range(3)]
        highs = [hi_ref[i, at] * in_hi for i in range(3)]
        for z in range(SZ):
            lo = roll(lows[z // 8], -fold_shift(z), 1)
            hi = roll(highs[z // 8], -fold_shift(z), 1)
            om_ref[z, at] = dm_ref[z, at] + jnp.where(head, lo, jnp.where(tail, hi, 0.0))
            os_ref[z, at] = ds_ref[z, at] + jnp.where(tail, lo, jnp.where(head, hi, 0.0))
    for out, row, edge in ((up_ref, CY, H + CY), (down_ref, H, H - 1)):
        for i in range(3):
            fold = zero
            out[18 + i] = zero
            out[24 + i] = zero
            for g in range(min(8, SZ - 8 * i)):
                z = 8 * i + g
                out[z] = om_ref[z, row:row + H]
                mine = jnp.logical_and(lane >= 16 * g, lane < 16 * g + 16)
                fold = jnp.where(mine, roll(os_ref[z, row:row + H], fold_shift(z), 1), fold)
                out[18 + i, g:g + 1] = om_ref[z, edge:edge + 1]
                out[24 + i, g:g + 1] = os_ref[z, edge:edge + 1]
            out[21 + i] = fold


def y_kernel(dims, pos_ref, dm_ref, ds_ref, lo_ref, hi_ref, om_ref, os_ref, up_ref, down_ref):
    in_lo, in_hi = edges(pos_ref, dims)[2:4]
    lane = iota((H, CX), 1)
    sub = iota((H, CX), 0)
    ends = jnp.logical_or(lane < H, lane >= CX - H)
    zero = jnp.zeros((H, CX), F32)
    last = EY // H - 1
    for r in range(EY // H):
        at = tile_rows(r)
        up_fold, down_fold = zero, zero
        for z in range(SZ):
            tile, g = z // 8, z % 8
            main, side = dm_ref[z, at], ds_ref[z, at]
            if r == 0:
                main = main + lo_ref[z] * in_lo
                side = side + jnp.where(ends, roll(lo_ref[21 + tile], -fold_shift(z), 1) * in_lo, 0.0)
            if r == 1:
                main = main + jnp.where(sub == 0, lo_ref[18 + tile, g:g + 1, :] * in_lo, 0.0)
                side = side + jnp.where(sub == 0, lo_ref[24 + tile, g:g + 1, :] * in_lo, 0.0)
            if r == last - 1:
                main = main + jnp.where(sub == H - 1, hi_ref[18 + tile, g:g + 1, :] * in_hi, 0.0)
                side = side + jnp.where(sub == H - 1, hi_ref[24 + tile, g:g + 1, :] * in_hi, 0.0)
            if r == last:
                main = main + hi_ref[z] * in_hi
                side = side + jnp.where(ends, roll(hi_ref[21 + tile], -fold_shift(z), 1) * in_hi, 0.0)
            om_ref[z, at] = main
            os_ref[z, at] = side
            if z >= CZ - H + 1:
                i = z - (CZ - H + 1)
                up_ref[i, at] = main
                shift = 14 * i + 7 if i < H else 120
                mine = jnp.logical_and(lane >= 14 * i, lane < (14 * i + 14 if i < H else CX))
                up_fold = jnp.where(mine, roll(side, shift, 1), up_fold)
            if z <= H:
                i = z - 1 if z > 0 else H
                down_ref[i, at] = main
                shift = 14 * i + 7 if i < H else 120
                mine = jnp.logical_and(lane >= 14 * i, lane < (14 * i + 14 if i < H else CX))
                down_fold = jnp.where(mine, roll(side, shift, 1), down_fold)
        up_ref[H + 1, at] = up_fold
        down_ref[H + 1, at] = down_fold


def pre_planes(level):
    return (H + 1 + level, H + CZ - 1 - level) if level < SWEEPS - 1 else (0, 0)


def pre_index(level, z):
    return sum(CZ - 2 - 2 * i for i in range(level)) + z - pre_planes(level)[0]


PRE = sum(CZ - 2 - 2 * i for i in range(SWEEPS - 1))


def padded_rows(t, shift=0):
    return slice(PADR + H * t + shift, PADR + H * t + H + shift)


def coefficients(pos_ref, dims):
    lo_x, hi_x, lo_y, hi_y, lo_z, hi_z = edges(pos_ref, dims)
    lane = iota((H, CX), 1)
    low, high = jnp.where(lane >= CX - H, lo_x, 1.0), jnp.where(lane < H, hi_x, 1.0)
    main = [jnp.full((H, CX), 1.0 / 6.0, F32)] * TILES
    main[0] = main[0] * lo_y
    main[-1] = main[-1] * hi_y
    return main, [c * (low * high) for c in main]


def relax(planes, get, put, rhs, weights):
    lane = iota((H, CX), 1)
    first, last = lane == 0, lane == CX - 1
    z0 = planes[0]
    carry = [[get(k, z0 - 1 + i, padded_rows(t)) for k in range(2) for i in range(2)] for t in range(TILES)]
    for z in planes:
        main_weight, side_weight = weights(z)
        for t in range(TILES):
            below, main, side_below, side = carry[t]
            at, up, down = padded_rows(t), padded_rows(t, 1), padded_rows(t, -1)
            above, side_above = get(0, z + 1, at), get(1, z + 1, at)
            main_w, side_w = roll(main, 1, 1), roll(side, 1, 1)
            main_e, side_e = roll(main, -1, 1), roll(side, -1, 1)
            total = (above + below) + (get(0, z, up) + get(0, z, down))
            total = total + (jnp.where(first, side_w, main_w) + jnp.where(last, side_e, main_e))
            put(0, z, at, (total - rhs(0, z, tile_rows(t))) * main_weight[t])
            total = (side_above + side_below) + (get(1, z, up) + get(1, z, down))
            total = total + (jnp.where(first, main_w, side_w) + jnp.where(last, main_e, side_e))
            put(1, z, at, (total - rhs(1, z, tile_rows(t))) * side_weight[t])
            carry[t] = [main, above, side, side_above]


def inner_kernel(dims, pos_ref, dm_ref, ds_ref, pre_ref):
    main_coef, side_coef = coefficients(pos_ref, dims)
    scale = 1.0 / DT
    zero = jnp.zeros((H, CX), F32)
    for i in range(PRE):
        for part in range(2):
            pre_ref[i, part, 0:PADR] = zero
            pre_ref[i, part, PADR + EY:PADR + EY + PADR] = zero

    def rhs(part, z, rows):
        return (ds_ref if part else dm_ref)[z - H + 1, rows] * scale

    for z in range(*pre_planes(0)):
        for t in range(TILES):
            pre_ref[pre_index(0, z), 0, padded_rows(t)] = -rhs(0, z, tile_rows(t)) * main_coef[t]
            pre_ref[pre_index(0, z), 1, padded_rows(t)] = -rhs(1, z, tile_rows(t)) * side_coef[t]
    for level in range(1, SWEEPS - 1):
        def get(part, z, rows, level=level):
            return pre_ref[pre_index(level - 1, z), part, rows]

        def put(part, z, rows, value, level=level):
            pre_ref[pre_index(level, z), part, rows] = value

        relax(range(*pre_planes(level)), get, put, rhs, lambda z: (main_coef, side_coef))


def sweep_kernel(
    dims, pos_ref, dm_ref, ds_ref, pre_ref, lo_ref, hi_ref, pred_ref, pres_ref, vel_out, pres_out,
    b_ref, phi_ref, vel_buf, pres_buf, sems,
):
    lo_z, hi_z = edges(pos_ref, dims)[4:6]
    main_coef, side_coef = coefficients(pos_ref, dims)
    scale = 1.0 / DT
    lane = iota((H, CX), 1)
    first, last = lane == 0, lane == CX - 1
    zero = jnp.zeros((H, CX), F32)
    near = jnp.logical_or(lane < H - 1, lane >= CX - H + 1)
    ends = jnp.logical_or(lane < H, lane >= CX - H)
    lo_scale, hi_scale = lo_z * scale, hi_z * scale
    low_coef = [[c * lo_z for c in main_coef], [c * lo_z for c in side_coef]]
    high_coef = [[c * hi_z for c in main_coef], [c * hi_z for c in side_coef]]

    def weights(z):
        return low_coef if z < H else high_coef if z >= H + CZ else (main_coef, side_coef)

    outer = list(range(pre_planes(0)[0])) + list(range(pre_planes(0)[1], EZ))
    place = {z: i for i, z in enumerate(outer)}

    for z in range(EZ):
        for part in range(2):
            for buf in range(2):
                phi_ref[buf, part, z, 0:PADR] = zero
                phi_ref[buf, part, z, PADR + EY:PADR + EY + PADR] = zero
    for t in range(TILES):
        rows = tile_rows(t)
        folded = (lo_ref[H + 1, rows] * lo_scale, hi_ref[H + 1, rows] * hi_scale)
        for z in outer:
            low = z < EZ // 2
            halo, fold, factor = (lo_ref, folded[0], lo_scale) if low else (hi_ref, folded[1], hi_scale)
            if z < H or z >= H + CZ:
                g = z if low else z - H - CZ
                main = halo[g, rows] * factor
                side = jnp.where(near, roll(fold, -(14 * g + 7), 1), 0.0)
                if z in (H - 1, H + CZ):
                    k = 0 if low else SZ - 1
                    main = main + dm_ref[k, rows] * factor
                    side = side + ds_ref[k, rows] * factor
            else:
                main = dm_ref[z - H + 1, rows] * scale + halo[H, rows] * factor
                side = ds_ref[z - H + 1, rows] * scale + jnp.where(ends, roll(fold, -120, 1), 0.0)
            b_ref[0, place[z], rows] = main
            b_ref[1, place[z], rows] = side
            cm, cs = weights(z)
            phi_ref[0, 0, z, padded_rows(t)] = -main * cm[t]
            phi_ref[0, 1, z, padded_rows(t)] = -side * cs[t]

    def rhs(part, z, rows):
        if z in place:
            return b_ref[part, place[z], rows]
        return (ds_ref if part else dm_ref)[z - H + 1, rows] * scale

    def reader(level):
        known = range(*pre_planes(level))

        def get(part, z, rows):
            if z in known:
                return pre_ref[pre_index(level, z), part, rows]
            return phi_ref[level % 2, part, z, rows]

        return get

    for level in range(1, SWEEPS):
        lo, hi = pre_planes(level)

        def put(part, z, rows, value, level=level):
            phi_ref[level % 2, part, z, rows] = value

        runs = ((level, lo), (hi, EZ - level)) if hi > lo else ((level, EZ - level),)
        for run in runs:
            relax(range(*run), reader(level - 1), put, rhs, weights)

    get = reader(SWEEPS - 1)
    chunk = 4
    copies = []
    for c in range(CZ // chunk):
        for z in range(c * chunk, (c + 1) * chunk):
            for t in range(CY // H):
                rows = tile_rows(t)
                at, up, down = padded_rows(t + 1), padded_rows(t + 1, 1), padded_rows(t + 1, -1)
                main, side = get(0, z + H, at), get(1, z + H, at)
                west = jnp.where(first, roll(side, 1, 1), roll(main, 1, 1))
                east = jnp.where(last, roll(side, -1, 1), roll(main, -1, 1))
                half = DT * 0.5
                vel_buf[0, z, rows] = pred_ref[0, z, rows] - half * (east - west)
                vel_buf[1, z, rows] = pred_ref[1, z, rows] - half * (get(0, z + H, up) - get(0, z + H, down))
                vel_buf[2, z, rows] = pred_ref[2, z, rows] - half * (get(0, z + H + 1, at) - get(0, z + H - 1, at))
                pres_buf[z, rows] = pres_ref[z, rows] + main
        part = pl.ds(c * chunk, chunk)
        copies.append(pltpu.make_async_copy(vel_buf.at[:, part], vel_out.at[:, part], sems.at[2 * c]))
        copies.append(pltpu.make_async_copy(pres_buf.at[part], pres_out.at[part], sems.at[2 * c + 1]))
        for copy in copies[-2:]:
            copy.start()
    for copy in copies:
        copy.wait()


def swap(up, down, axis):
    count = lax.axis_size(axis)
    forward = [(i, (i + 1) % count) for i in range(count)]
    backward = [(j, i) for i, j in forward]
    return lax.ppermute(up, axis, forward), lax.ppermute(down, axis, backward)


def shape(*dims):
    return jax.ShapeDtypeStruct(dims, F32)


SMEM = pl.BlockSpec(memory_space=pltpu.SMEM)
VMEM = pl.BlockSpec(memory_space=pltpu.VMEM)


ANY = pl.BlockSpec(memory_space=pl.ANY)


def in_hbm(x):
    return pltpu.with_memory_space_constraint(x, pltpu.HBM)


def in_vmem(*dims, dtype=F32):
    return pltpu.VMEM(dims, dtype)


MIB = 1024 * 1024
ENTRY_LIMIT = 24


class Place:
    def __getitem__(self, k):
        return lax.axis_index(("gx", "gy", "gz")[k])


def call(kernel, scalars, arrays, outs, scratch=(), in_specs=None, out_specs=None, limit=24, cost=0):
    return pl.pallas_call(
        functools.partial(kernel, Place()),
        out_shape=outs,
        in_specs=[SMEM] * len(scalars) + list(in_specs or [VMEM] * len(arrays)),
        out_specs=out_specs or [VMEM] * len(outs),
        scratch_shapes=list(scratch),
        compiler_params=pltpu.CompilerParams(vmem_limit_bytes=limit * MIB),
        cost_estimate=pl.CostEstimate(flops=cost, bytes_accessed=cost // 64, transcendentals=0) if cost else None,
    )(*scalars, *arrays)


def shards(
    velocity, adjoint, pressure, viscosity, disk_cells, disk_turbine, disk_weight, disk_dweight, yaw, thrust_coef, owner_slot,
):
    axes = ("gx", "gy", "gz")
    n_gx, n_gy, n_gz = (lax.axis_size(a) for a in axes)
    n_dev = n_gx * n_gy * n_gz
    dims = (n_dev, n_gx, n_gy, n_gz)
    turbines = owner_slot.shape[0]
    if turbines % CX:
        owner_slot = jnp.pad(owner_slot, (0, CX - turbines % CX))
    owner = owner_slot.reshape(-1, CX)
    cells, turbine, weight = (a.reshape(1, -1) for a in (disk_cells, disk_turbine, disk_weight))

    payload, xr, xl, yr, yl, zr, zl, fields, index, scale, table = call(
        functools.partial(entry_kernel, n_dev, n_gy),
        (in_hbm(yaw), in_hbm(thrust_coef)),
        tuple(in_hbm(a) for a in (velocity, adjoint, viscosity, cells, turbine, weight, disk_dweight, owner)),
        (
            shape(n_dev, CX), in_vmem(CY, CX), in_vmem(CY, CX), in_vmem(6 * CZ, CX), in_vmem(6 * CZ, CX),
            in_vmem(6, CY, CX), in_vmem(6, CY, CX), in_vmem(7, CZ, CY, CX), in_vmem(2, cells.shape[1], dtype=jnp.int32),
            in_vmem(*weight.shape), in_vmem(*owner.shape, dtype=jnp.int32),
        ),
        (pltpu.VMEM((n_dev, CX), F32), pltpu.SemaphoreType.DMA((8,))),
        [ANY, ANY, ANY] + [VMEM] * 5,
        [ANY] + [VMEM] * 10,
        limit=ENTRY_LIMIT,
    )
    got = lax.all_to_all(payload, axes, 0, 0, tiled=True)
    xlo, xhi = swap(xr, xl, "gx")
    ylo, yhi = swap(yr, yl, "gy")
    xlo, zl = lax.optimization_barrier((xlo, zl))
    zlo, zhi = swap(zr, zl, "gz")
    faces = (xlo, xhi, ylo, yhi, zlo, zhi)

    pred_base, dual_base = call(
        functools.partial(base_kernel, dims),
        (),
        (fields, index, scale, table, got),
        (shape(3, CZ, CY, CX), shape(3, CZ, CY, CX)),
        (pltpu.VMEM((3, CZ, CY, CX), F32),),
        cost=1 << 30,
    )
    predicted, dm, ds, xr, xl = call(
        functools.partial(flow_kernel, dims),
        (),
        (pred_base, fields) + faces,
        (shape(3, CZ, CY, CX), shape(SZ, EY, CX), shape(SZ, EY, CX), shape(3, EY, CX), shape(3, EY, CX)),
    )
    adjoint_next, yaw_grad, position_grad = call(
        functools.partial(dual_kernel, dims),
        (in_hbm(yaw), in_hbm(thrust_coef)),
        (dual_base, fields, got) + faces,
        (shape(3, CZ, CY, CX), shape(1, 4), shape(2, 4)),
        (pltpu.VMEM((3, CZ, CY, CX), F32), pltpu.SemaphoreType.DMA((3,))),
        out_specs=[ANY, VMEM, VMEM],
        cost=1 << 30,
    )
    lo, hi = swap(xr, xl, "gx")
    dm, ds, up, down = call(
        functools.partial(x_kernel, dims), (), (dm, ds, lo, hi),
        (shape(SZ, EY, CX), shape(SZ, EY, CX), shape(27, H, CX), shape(27, H, CX)),
    )
    lo, hi = swap(up, down, "gy")
    lo, yaw_grad = lax.optimization_barrier((lo, yaw_grad))
    dm, ds, up, down = call(
        functools.partial(y_kernel, dims), (), (dm, ds, lo, hi),
        (shape(SZ, EY, CX), shape(SZ, EY, CX), shape(H + 2, EY, CX), shape(H + 2, EY, CX)),
    )
    lo, hi = swap(up, down, "gz")
    pre = call(
        functools.partial(inner_kernel, dims), (), (dm, ds), (shape(PRE, 2, EY + 2 * PADR, CX),), cost=1 << 30
    )[0]
    velocity_next, pressure_next = call(
        functools.partial(sweep_kernel, dims), (), (dm, ds, pre, lo, hi, predicted, pressure),
        (shape(3, CZ, CY, CX), shape(CZ, CY, CX)),
        (
            pltpu.VMEM((2, EZ - CZ + 2, EY, CX), F32), pltpu.VMEM((2, 2, EZ, EY + 2 * PADR, CX), F32),
            pltpu.VMEM((3, CZ, CY, CX), F32), pltpu.VMEM((CZ, CY, CX), F32), pltpu.SemaphoreType.DMA((8,)),
        ),
        out_specs=[ANY, ANY],
    )
    return velocity_next, adjoint_next, pressure_next, yaw_grad.reshape(-1), position_grad


def solution(mesh):
    axes = ("gx", "gy", "gz")
    grid = P(None, "gz", "gy", "gx")
    cell = P("gz", "gy", "gx")
    flat = P(axes)
    return jax.shard_map(
        shards,
        mesh=mesh,
        in_specs=(grid, grid, cell, cell, flat, flat, flat, P(None, axes), flat, flat, P()),
        out_specs=(grid, grid, cell, flat, P(None, axes)),
        check_vma=False,
    )
```

profile of v0, /device:TPU:24, one launch (start us, length us, event | category | flops | bytes accessed | tf_op | source)
XLA Modules:
  0.0 60.3 jit_solution(11926491459602259046)
XLA Ops:
  0.6 4.1 %shard_map.146 = (f32[256,128]{1,0:T(8,128)}, f32[32,128]{1,0:T(8,128)S(1)}, f32[32,128]{1,0:T(8,128)S(1)}, f32[96,128]{1,0:T(8,128)S(1)}, f32[96,128]{1,0:T(8,1...) custom-call(f32[4]{0:T(128)} %yaw_ref.3, ...), custom_call_target="tpu_custom_call" | custom-call | tf_op jit(solution)/shard_map/pallas_call | solution.py:691
  4.7 14.4 %all-to-all-start = ((f32[256,1,128]{2,1,0:T(1,128)}), f32[256,1,128]{2,1,0:T(1,128)S(1)}, u32[]{:S(2)}, u32[]{:S(2)}) async-start(f32[256,1,128]{2,1,0:T(1,128)} %bitcast.5), calls=%async_computation | async-start | bytes 262144 | tf_op jit(solution)/shard_map/all_to_all | solution.py:729
  19.1 0.2 collective-permute-start
  19.3 4.2 %collective-permute-start.1 = (f32[32,128]{1,0:T(8,128)S(1)}, f32[32,128]{1,0:T(8,128)S(1)}, u32[]{:S(2)}, u32[]{:S(2)}) collective-permute-start(f32[32,128]{1,0:T(8,128)S(1)} %get-tuple-element.49), channel_id=1, source_target_pairs={{16,0},{32,16},{48,32},{64,48},{80,64},{96,80},{112,96},{128,112},... | collective-permute-start | bytes 49160 | tf_op jit(solution)/shard_map/ppermute | solution.py:659
  23.5 1.5 %collective-permute-start.2 = (f32[96,128]{1,0:T(8,128)S(1)}, f32[96,128]{1,0:T(8,128)S(1)}, u32[]{:S(2)}, u32[]{:S(2)}) collective-permute-start(f32[96,128]{1,0:T(8,128)S(1)} %get-tuple-element.50), channel_id=1, source_target_pairs={{0,4},{4,8},{8,12},{12,0},{1,5},{5,9},{9,13},{13,1},{2,6},{6,10},{... | collective-permute-start | bytes 147464 | tf_op jit(solution)/shard_map/ppermute | solution.py:659
  25.0 1.8 %collective-permute-start.3 = (f32[96,128]{1,0:T(8,128)S(1)}, f32[96,128]{1,0:T(8,128)S(1)}, u32[]{:S(2)}, u32[]{:S(2)}) collective-permute-start(f32[96,128]{1,0:T(8,128)S(1)} %get-tuple-element.51), channel_id=1, source_target_pairs={{4,0},{8,4},{12,8},{0,12},{5,1},{9,5},{13,9},{1,13},{6,2},{10,6},{... | collective-permute-start | bytes 147464 | tf_op jit(solution)/shard_map/ppermute | solution.py:659
  26.7 0.7 %collective-permute-start.4 = (f32[6,32,128]{2,1,0:T(8,128)S(1)}, f32[6,32,128]{2,1,0:T(8,128)S(1)}, u32[]{:S(2)}, u32[]{:S(2)}) collective-permute-start(f32[6,32,128]{2,1,0:T(8,128)S(1)} %get-tuple-element.52), channel_id=1, source_target_pairs={{0,1},{1,2},{2,3},{3,0},{4,5},{5,6},{6,7},{7,4},{8,9},{9,10},{10,1... | collective-permute-start | bytes 294920 | tf_op jit(solution)/shard_map/ppermute | solution.py:659
  27.4 0.0 collective-permute-done.xlo_ref
  27.5 1.3 %collective-permute-start.5 = (f32[6,32,128]{2,1,0:T(8,128)S(1)}, f32[6,32,128]{2,1,0:T(8,128)S(1)}, u32[]{:S(2)}, u32[]{:S(2)}) collective-permute-start(f32[6,32,128]{2,1,0:T(8,128)S(1)} %get-tuple-element.53), channel_id=1, source_target_pairs={{1,0},{2,1},{3,2},{0,3},{5,4},{6,5},{7,6},{4,7},{9,8},{10,9},{11,1... | collective-permute-start | bytes 294920 | tf_op jit(solution)/shard_map/ppermute | solution.py:659
  28.8 2.0 %all-to-all-done = f32[256,1,128]{2,1,0:T(1,128)S(1)} async-done(((f32[256,1,128]{2,1,0:T(1,128)}), f32[256,1,128]{2,1,0:T(1,128)S(1)}, u32[]{:S(2)}, u32[]{:S(2)}) %all-to-all-start) | async-done | bytes 131104 | tf_op jit(solution)/shard_map/all_to_all | solution.py:729
  30.8 1.9 %shard_map.147 = (f32[3,16,32,128]{3,2,1,0:T(8,128)S(1)}, f32[3,16,32,128]{3,2,1,0:T(8,128)S(1)}) custom-call(f32[7,16,32,128]{3,2,1,0:T(8,128)S(1)} %get-tuple-element.40.fld_ref, s32[2,512]{1,0:T(2,128)S(1)} %get-tuple-element.41.index_ref, f32[1,512]{1,0:T(1,128)S(1)} %get-tuple-element.42.scale_ref, s32[8,128]{1,0:T(8,128)S(1)} %get-tuple-element.43.owner_ref, ...), custom_call_target="tpu_custom_call" | custom-call | flops 1073741824 | bytes 16777216 | tf_op jit(solution)/shard_map/pallas_call | solution.py:691
  32.7 0.0 collective-permute-done.1.xhi_ref
  32.7 0.0 collective-permute-done.2.ylo_ref
  32.7 0.0 collective-permute-done.3.yhi_ref
  32.7 0.0 collective-permute-done.4.zlo_ref
  32.7 0.5 collective-permute-done.5.zhi_ref
  33.3 0.8 %shard_map.148 = (f32[3,16,32,128]{3,2,1,0:T(8,128)S(1)}, f32[18,48,128]{2,1,0:T(8,128)S(1)}, f32[18,48,128]{2,1,0:T(8,128)S(1)}, f32[3,48,128]{2,1,0:T(8,128)S(1)}, f32[3,48,128]{2,1,0:T(8,128)S(1)}) custom-call(f32[3,16,32,128]{3,2,1,0:T(8,128)S(1)} %get-tuple-element.45.base_ref, f32[7,16,32,128]{3,2,1,0:T(8,128)S(1)} %get-tuple-element.40.fld_ref, ...), custom_call_target="tpu_custom_call" | custom-call | tf_op jit(solution)/shard_map/pallas_call | solution.py:691
  34.1 0.0 collective-permute-start.6
  34.1 2.9 %collective-permute-start.7 = (f32[3,48,128]{2,1,0:T(8,128)S(1)}, f32[3,48,128]{2,1,0:T(8,128)S(1)}, u32[]{:S(2)}, u32[]{:S(2)}) collective-permute-start(f32[3,48,128]{2,1,0:T(8,128)S(1)} %get-tuple-element.57), channel_id=1, source_target_pairs={{16,0},{32,16},{48,32},{64,48},{80,64},{96,80},{112,96},{128,112},... | collective-permute-start | bytes 221192 | tf_op jit(solution)/shard_map/ppermute | solution.py:659
  37.1 2.0 %collective-permute-done.6.lo_ref = f32[3,48,128]{2,1,0:T(8,128)S(1)} collective-permute-done((f32[3,48,128]{2,1,0:T(8,128)S(1)}, f32[3,48,128]{2,1,0:T(8,128)S(1)}, u32[]{:S(2)}, u32[]{:S(2)}) %collective-permute-start.6) | collective-permute-done | bytes 73760 | tf_op jit(solution)/shard_map/ppermute | solution.py:659
  39.1 0.0 collective-permute-done.7.hi_ref
  39.1 0.4 shard_map.149
  39.5 0.1 collective-permute-start.8
  39.7 3.2 %collective-permute-start.9 = (f32[27,8,128]{2,1,0:T(8,128)S(1)}, f32[27,8,128]{2,1,0:T(8,128)S(1)}, u32[]{:S(2)}, u32[]{:S(2)}) collective-permute-start(f32[27,8,128]{2,1,0:T(8,128)S(1)} %get-tuple-element.64), channel_id=1, source_target_pairs={{4,0},{8,4},{12,8},{0,12},{5,1},{9,5},{13,9},{1,13},{6,2},{10,6},{... | collective-permute-start | bytes 331784 | tf_op jit(solution)/shard_map/ppermute | solution.py:659
  42.8 2.5 %shard_map.150 = (f32[3,16,32,128]{3,2,1,0:T(8,128)}, f32[1,4]{1,0:T(1,128)}, f32[2,4]{1,0:T(2,128)}) custom-call(f32[4]{0:T(128)} %yaw_ref.3, f32[4]{0:T(128)} %ct_ref.3, f32[3,16,32,128]{3,2,1,0:T(8,128)S(1)} %get-tuple-element.61.base_ref, f32[7,16,32,128]{3,2,1,0:T(8,128)S(1)} %get-tuple-element.40.fld_ref, f32[256,128]{1,0:T(8,128)S(1)} %bitcast.10, ...), custom_call_target="tpu_custom_call" | custom-call | flops 1073741824 | bytes 16777216 | tf_op jit(solution)/shard_map/pallas_call | solution.py:691
  45.3 0.0 copy-start
  45.3 0.2 collective-permute-done.8.lo_ref
  45.6 0.0 collective-permute-done.9.hi_ref
  45.6 0.3 shard_map.151
  45.9 1.8 %collective-permute-start.10 = (f32[10,48,128]{2,1,0:T(8,128)S(1)}, f32[10,48,128]{2,1,0:T(8,128)S(1)}, u32[]{:S(2)}, u32[]{:S(2)}) collective-permute-start(f32[10,48,128]{2,1,0:T(8,128)S(1)} %get-tuple-element.67), channel_id=1, source_target_pairs={{0,1},{1,2},{2,3},{3,0},{4,5},{5,6},{6,7},{7,4},{8,9},{9,10},{10,1... | collective-permute-start | bytes 737288 | tf_op jit(solution)/shard_map/ppermute | solution.py:659
  47.6 0.5 collective-permute-start.11
  48.2 1.2 %shard_map.152.pre_ref = f32[56,2,64,128]{3,2,1,0:T(8,128)S(1)} custom-call(f32[18,48,128]{2,1,0:T(8,128)S(1)} %get-tuple-element.65.dm_ref, f32[18,48,128]{2,1,0:T(8,128)S(1)} %get-tuple-element.66.ds_ref), custom_call_target="tpu_custom_call" | custom-call | flops 1073741824 | bytes 16777216 | tf_op jit(solution)/shard_map/pallas_call | solution.py:691
  49.4 3.6 %collective-permute-done.10.lo_ref = f32[10,48,128]{2,1,0:T(8,128)S(1)} collective-permute-done((f32[10,48,128]{2,1,0:T(8,128)S(1)}, f32[10,48,128]{2,1,0:T(8,128)S(1)}, u32[]{:S(2)}, u32[]{:S(2)}) %collective-permute-start.10) | collective-permute-done | bytes 245792 | tf_op jit(solution)/shard_map/ppermute | solution.py:659
  52.9 2.7 %collective-permute-done.11.hi_ref = f32[10,48,128]{2,1,0:T(8,128)S(1)} collective-permute-done((f32[10,48,128]{2,1,0:T(8,128)S(1)}, f32[10,48,128]{2,1,0:T(8,128)S(1)}, u32[]{:S(2)}, u32[]{:S(2)}) %collective-permute-start.11) | collective-permute-done | bytes 245792 | tf_op jit(solution)/shard_map/ppermute | solution.py:659
  55.6 0.0 copy-done
  55.6 4.5 %shard_map.153 = (f32[3,16,32,128]{3,2,1,0:T(8,128)}, f32[16,32,128]{2,1,0:T(8,128)}) custom-call(f32[18,48,128]{2,1,0:T(8,128)S(1)} %get-tuple-element.65.dm_ref, f32[18,48,128]{2,1,0:T(8,128)S(1)} %get-tuple-element.66.ds_ref, f32[56,2,64,128]{3,2,1,0:T(8,128)S(1)} %shard_map.152.pre_ref, f32[10,48,128]{2,1,0:T(8,128)S(1)} %collective-permute-done.10.lo_ref, ...), custom_call_target="tpu_custom_call" | custom-call | tf_op jit(solution)/shard_map/pallas_call | solution.py:691
Async XLA Ops:
  4.7 26.1 %all-to-all-start = ((f32[256,1,128]{2,1,0:T(1,128)}), f32[256,1,128]{2,1,0:T(1,128)S(1)}, u32[]{:S(2)}, u32[]{:S(2)}) async-start(f32[256,1,128]{2,1,0:T(1,128)} %bitcast.5), calls=%async_computation | async-start | bytes 262144 | tf_op jit(solution)/shard_map/all_to_all | solution.py:729
  19.1 8.3 %collective-permute-start = (f32[32,128]{1,0:T(8,128)S(1)}, f32[32,128]{1,0:T(8,128)S(1)}, u32[]{:S(2)}, u32[]{:S(2)}) collective-permute-start(f32[32,128]{1,0:T(8,128)S(1)} %get-tuple-element.46), channel_id=1, source_target_pairs={{0,16},{16,32},{32,48},{48,64},{64,80},{80,96},{96,112},{112,128},... | collective-permute-start | bytes 49160 | tf_op jit(solution)/shard_map/ppermute | solution.py:659
  19.3 13.4 %collective-permute-start.1 = (f32[32,128]{1,0:T(8,128)S(1)}, f32[32,128]{1,0:T(8,128)S(1)}, u32[]{:S(2)}, u32[]{:S(2)}) collective-permute-start(f32[32,128]{1,0:T(8,128)S(1)} %get-tuple-element.49), channel_id=1, source_target_pairs={{16,0},{32,16},{48,32},{64,48},{80,64},{96,80},{112,96},{128,112},... | collective-permute-start | bytes 49160 | tf_op jit(solution)/shard_map/ppermute | solution.py:659
  23.5 9.2 %collective-permute-start.2 = (f32[96,128]{1,0:T(8,128)S(1)}, f32[96,128]{1,0:T(8,128)S(1)}, u32[]{:S(2)}, u32[]{:S(2)}) collective-permute-start(f32[96,128]{1,0:T(8,128)S(1)} %get-tuple-element.50), channel_id=1, source_target_pairs={{0,4},{4,8},{8,12},{12,0},{1,5},{5,9},{9,13},{13,1},{2,6},{6,10},{... | collective-permute-start | bytes 147464 | tf_op jit(solution)/shard_map/ppermute | solution.py:659
  25.0 7.7 %collective-permute-start.3 = (f32[96,128]{1,0:T(8,128)S(1)}, f32[96,128]{1,0:T(8,128)S(1)}, u32[]{:S(2)}, u32[]{:S(2)}) collective-permute-start(f32[96,128]{1,0:T(8,128)S(1)} %get-tuple-element.51), channel_id=1, source_target_pairs={{4,0},{8,4},{12,8},{0,12},{5,1},{9,5},{13,9},{1,13},{6,2},{10,6},{... | collective-permute-start | bytes 147464 | tf_op jit(solution)/shard_map/ppermute | solution.py:659
  26.7 6.0 %collective-permute-start.4 = (f32[6,32,128]{2,1,0:T(8,128)S(1)}, f32[6,32,128]{2,1,0:T(8,128)S(1)}, u32[]{:S(2)}, u32[]{:S(2)}) collective-permute-start(f32[6,32,128]{2,1,0:T(8,128)S(1)} %get-tuple-element.52), channel_id=1, source_target_pairs={{0,1},{1,2},{2,3},{3,0},{4,5},{5,6},{6,7},{7,4},{8,9},{9,10},{10,1... | collective-permute-start | bytes 294920 | tf_op jit(solution)/shard_map/ppermute | solution.py:659
  27.5 5.8 %collective-permute-start.5 = (f32[6,32,128]{2,1,0:T(8,128)S(1)}, f32[6,32,128]{2,1,0:T(8,128)S(1)}, u32[]{:S(2)}, u32[]{:S(2)}) collective-permute-start(f32[6,32,128]{2,1,0:T(8,128)S(1)} %get-tuple-element.53), channel_id=1, source_target_pairs={{1,0},{2,1},{3,2},{0,3},{5,4},{6,5},{7,6},{4,7},{9,8},{10,9},{11,1... | collective-permute-start | bytes 294920 | tf_op jit(solution)/shard_map/ppermute | solution.py:659
  34.1 5.0 %collective-permute-start.6 = (f32[3,48,128]{2,1,0:T(8,128)S(1)}, f32[3,48,128]{2,1,0:T(8,128)S(1)}, u32[]{:S(2)}, u32[]{:S(2)}) collective-permute-start(f32[3,48,128]{2,1,0:T(8,128)S(1)} %get-tuple-element.56), channel_id=1, source_target_pairs={{0,16},{16,32},{32,48},{48,64},{64,80},{80,96},{96,112},{112,128},... | collective-permute-start | bytes 221192 | tf_op jit(solution)/shard_map/ppermute | solution.py:659
  34.1 5.0 %collective-permute-start.7 = (f32[3,48,128]{2,1,0:T(8,128)S(1)}, f32[3,48,128]{2,1,0:T(8,128)S(1)}, u32[]{:S(2)}, u32[]{:S(2)}) collective-permute-start(f32[3,48,128]{2,1,0:T(8,128)S(1)} %get-tuple-element.57), channel_id=1, source_target_pairs={{16,0},{32,16},{48,32},{64,48},{80,64},{96,80},{112,96},{128,112},... | collective-permute-start | bytes 221192 | tf_op jit(solution)/shard_map/ppermute | solution.py:659
  39.5 6.0 %collective-permute-start.8 = (f32[27,8,128]{2,1,0:T(8,128)S(1)}, f32[27,8,128]{2,1,0:T(8,128)S(1)}, u32[]{:S(2)}, u32[]{:S(2)}) collective-permute-start(f32[27,8,128]{2,1,0:T(8,128)S(1)} %get-tuple-element.60), channel_id=1, source_target_pairs={{0,4},{4,8},{8,12},{12,0},{1,5},{5,9},{9,13},{13,1},{2,6},{6,10},{... | collective-permute-start | bytes 331784 | tf_op jit(solution)/shard_map/ppermute | solution.py:659
  39.7 5.9 %collective-permute-start.9 = (f32[27,8,128]{2,1,0:T(8,128)S(1)}, f32[27,8,128]{2,1,0:T(8,128)S(1)}, u32[]{:S(2)}, u32[]{:S(2)}) collective-permute-start(f32[27,8,128]{2,1,0:T(8,128)S(1)} %get-tuple-element.64), channel_id=1, source_target_pairs={{4,0},{8,4},{12,8},{0,12},{5,1},{9,5},{13,9},{1,13},{6,2},{10,6},{... | collective-permute-start | bytes 331784 | tf_op jit(solution)/shard_map/ppermute | solution.py:659
  45.3 10.3 %copy-start = (f32[16,32,128]{2,1,0:T(8,128)S(1)}, f32[16,32,128]{2,1,0:T(8,128)}, u32[]{:S(2)}) copy-start(f32[16,32,128]{2,1,0:T(8,128)} %pres_ref.1) | copy-start | bytes 786436
  45.9 7.0 %collective-permute-start.10 = (f32[10,48,128]{2,1,0:T(8,128)S(1)}, f32[10,48,128]{2,1,0:T(8,128)S(1)}, u32[]{:S(2)}, u32[]{:S(2)}) collective-permute-start(f32[10,48,128]{2,1,0:T(8,128)S(1)} %get-tuple-element.67), channel_id=1, source_target_pairs={{0,1},{1,2},{2,3},{3,0},{4,5},{5,6},{6,7},{7,4},{8,9},{9,10},{10,1... | collective-permute-start | bytes 737288 | tf_op jit(solution)/shard_map/ppermute | solution.py:659
  47.6 8.0 %collective-permute-start.11 = (f32[10,48,128]{2,1,0:T(8,128)S(1)}, f32[10,48,128]{2,1,0:T(8,128)S(1)}, u32[]{:S(2)}, u32[]{:S(2)}) collective-permute-start(f32[10,48,128]{2,1,0:T(8,128)S(1)} %get-tuple-element.68), channel_id=1, source_target_pairs={{1,0},{2,1},{3,2},{0,3},{5,4},{6,5},{7,6},{4,7},{9,8},{10,9},{11,1... | collective-permute-start | bytes 737288 | tf_op jit(solution)/shard_map/ppermute | solution.py:659
where the time goes:
time: 60.5 us; the launch traced here: 60.3 us
  starting transfers between devices  32.6 us (54%)
  Pallas kernels  15.7 us (26%)
  waiting for transfers between devices  11.1 us (18%)
  between operations  0.9 us (1%)
    ppermute x12, starting transfers between devices, swap(): return (lax.ppermute(up, axis, forward), lax.ppermute(down, axis, backward))  18.2 us
    pallas_call x8, Pallas kernels, call(): pl.pallas_call(functools.partial(kernel, Place()), out_shape=outs, in_spe...  15.7 us
    all_to_all x1, starting transfers between devices, shards(): got = lax.all_to_all(payload, axes, 0, 0, tiled=True)  14.4 us
    ppermute x12, waiting for transfers between devices, swap(): return (lax.ppermute(up, axis, forward), lax.ppermute(down, axis, backward))  9.06 us
    all_to_all x1, waiting for transfers between devices, shards(): got = lax.all_to_all(payload, axes, 0, 0, tiled=True)  2.04 us
  transfers between devices with their start and end apart: 13, of which 6 were waited for; matrix products, arithmetic and copies ran while one was open for 0% of the time, Pallas kernels for 9%

commit v1 on v0

--- a/solution.py
+++ b/solution.py
@@ -266,10 +266,7 @@
     return jnp.where(sub == H - 1, 0.0, roll(ref[index + (tile_rows(t),)], -1, 0))
 
 
-def base_kernel(
-    dims, pos_ref, fld_ref, index_ref, scale_ref, owner_ref, got_ref,
-    pred_ref, dual_ref, field_ref,
-):
+def force_kernel(dims, pos_ref, index_ref, scale_ref, owner_ref, got_ref, field_ref):
     n_dev, n_gx, n_gy, n_gz = dims
     bx, by = pos_ref[0], pos_ref[1]
     terms = window_terms(got_ref[...], n_dev, n_gx, n_gy, n_gz, bx, by, owner_ref)
@@ -286,6 +283,8 @@
         spread = jnp.where(lanes, value, 0.0)
         field_ref[c] = dots([rows], pieces(spread, 2), NT).reshape(CZ, CY, CX)
 
+
+def stencil_kernel(pos_ref, fld_ref, pred_ref, dual_ref):
     lane = iota((H, CX), 1)
     sub = iota((H, CX), 0)
     zero = jnp.zeros((H, CX), F32)
@@ -300,17 +299,12 @@
                 west = jnp.where(lane == 0, 0.0, roll(tile, 1, 1))
                 east = jnp.where(lane == CX - 1, 0.0, roll(tile, -1, 1))
                 lap = (above + below) + (north + south) + (east + west) - 6.0 * tile
-                rate = fld_ref[6, z, at] * lap
-                rate = rate + (west - tile if f < 3 else east - tile)
-                if f < 2:
-                    rate = rate + field_ref[f, z, at]
-                if f == 3:
-                    rate = rate + field_ref[2, z, at]
+                rate = fld_ref[6, z, at] * lap + (west - tile if f < 3 else east - tile)
                 out[comp, z, at] = tile + DT * rate
                 below, tile = tile, above
 
 
-def add_faces(f, first, out, given, fld_ref, bounds, xlo_ref, xhi_ref, ylo_ref, yhi_ref, zlo_ref, zhi_ref):
+def add_faces(f, first, out, given, field_ref, fld_ref, bounds, xlo_ref, xhi_ref, ylo_ref, yhi_ref, zlo_ref, zhi_ref):
     lo_x, hi_x, lo_y, hi_y, lo_z, hi_z = bounds
     lane = iota((H, CX), 1)
     sub = iota((H, CX), 0)
@@ -332,7 +326,12 @@
                 lap = lap + zlo_ref[f, at] * lo_z
             if z == CZ - 1:
                 lap = lap + zhi_ref[f, at] * hi_z
-            out[comp, z, at] = given[comp, z, at] + DT * (fld_ref[6, z, at] * lap + (west if flow else east))
+            rate = fld_ref[6, z, at] * lap + (west if flow else east)
+            if f < 2:
+                rate = rate + field_ref[f, z, at]
+            if f == 3:
+                rate = rate + field_ref[2, z, at]
+            out[comp, z, at] = given[comp, z, at] + DT * rate
 
 
 def fold_shift(z):
@@ -340,12 +339,12 @@
 
 
 def flow_kernel(
-    dims, pos_ref, base_ref, fld_ref, xlo_ref, xhi_ref, ylo_ref, yhi_ref, zlo_ref, zhi_ref,
+    dims, pos_ref, base_ref, field_ref, fld_ref, xlo_ref, xhi_ref, ylo_ref, yhi_ref, zlo_ref, zhi_ref,
     pred_ref, dm_ref, ds_ref, xr_ref, xl_ref,
 ):
     bounds = edges(pos_ref, dims)
     for f in range(3):
-        add_faces(f, 0, pred_ref, base_ref, fld_ref, bounds, xlo_ref, xhi_ref, ylo_ref, yhi_ref, zlo_ref, zhi_ref)
+        add_faces(f, 0, pred_ref, base_ref, field_ref, fld_ref, bounds, xlo_ref, xhi_ref, ylo_ref, yhi_ref, zlo_ref, zhi_ref)
     lane = iota((H, CX), 1)
     sub = iota((H, CX), 0)
     zero = jnp.zeros((H, CX), F32)
@@ -393,13 +392,13 @@
 
 
 def dual_kernel(
-    dims, pos_ref, yaw_ref, ct_ref, base_ref, fld_ref, got_ref, xlo_ref, xhi_ref, ylo_ref, yhi_ref, zlo_ref, zhi_ref,
+    dims, pos_ref, yaw_ref, ct_ref, base_ref, field_ref, fld_ref, got_ref, xlo_ref, xhi_ref, ylo_ref, yhi_ref, zlo_ref, zhi_ref,
     dual_out, yaw_out, pos_out, dual_ref, sems,
 ):
     bounds = edges(pos_ref, dims)
     copies = []
     for f in range(3, 6):
-        add_faces(f, 3, dual_ref, base_ref, fld_ref, bounds, xlo_ref, xhi_ref, ylo_ref, yhi_ref, zlo_ref, zhi_ref)
+        add_faces(f, 3, dual_ref, base_ref, field_ref, fld_ref, bounds, xlo_ref, xhi_ref, ylo_ref, yhi_ref, zlo_ref, zhi_ref)
         copies.append(pltpu.make_async_copy(dual_ref.at[f - 3], dual_out.at[f - 3], sems.at[f - 3]))
         copies[-1].start()
     owner_outputs(got_ref[...], yaw_ref, ct_ref, yaw_out, pos_out)
@@ -407,7 +406,9 @@
         copy.wait()
 
 
-def x_kernel(dims, pos_ref, dm_ref, ds_ref, lo_ref, hi_ref, om_ref, os_ref, up_ref, down_ref):
+def x_kernel(
+    dims, pos_ref, dm_ref, ds_ref, lo_ref, hi_ref, om_ref, os_ref, up_ref, down_ref, above_ref, below_ref
+):
     in_lo, in_hi = edges(pos_ref, dims)[0:2]
     lane = iota((H, CX), 1)
     head, tail = lane < H, lane >= CX - H
@@ -434,18 +435,41 @@
                 out[18 + i, g:g + 1] = om_ref[z, edge:edge + 1]
                 out[24 + i, g:g + 1] = os_ref[z, edge:edge + 1]
             out[21 + i] = fold
-
-
-def y_kernel(dims, pos_ref, dm_ref, ds_ref, lo_ref, hi_ref, om_ref, os_ref, up_ref, down_ref):
+    for out, plane in ((above_ref, up_plane), (below_ref, down_plane)):
+        for r in range(1, 1 + CY // H):
+            for i in range(H + 1):
+                out[i, tile_rows(r - 1)] = om_ref[plane(i), tile_rows(r)]
+            out[H + 1, tile_rows(r - 1)] = fold_planes(lambda i: os_ref[plane(i), tile_rows(r)])
+
+
+def up_plane(i):
+    return CZ - H + 1 + i
+
+
+def down_plane(i):
+    return i + 1 if i < H else 0
+
+
+def fold_planes(side):
+    lane = iota((H, CX), 1)
+    fold = jnp.zeros((H, CX), F32)
+    for i in range(H + 1):
+        mine = jnp.logical_and(lane >= 14 * i, lane < (14 * i + 14 if i < H else CX))
+        fold = jnp.where(mine, roll(side(i), 14 * i + 7 if i < H else 120, 1), fold)
+    return fold
+
+
+LATE = H + 1 + 2 + 3
+
+
+def y_kernel(dims, pos_ref, dm_ref, ds_ref, lo_ref, hi_ref, om_ref, os_ref, above_ref, below_ref):
     in_lo, in_hi = edges(pos_ref, dims)[2:4]
     lane = iota((H, CX), 1)
     sub = iota((H, CX), 0)
     ends = jnp.logical_or(lane < H, lane >= CX - H)
-    zero = jnp.zeros((H, CX), F32)
     last = EY // H - 1
     for r in range(EY // H):
         at = tile_rows(r)
-        up_fold, down_fold = zero, zero
         for z in range(SZ):
             tile, g = z // 8, z % 8
             main, side = dm_ref[z, at], ds_ref[z, at]
@@ -463,20 +487,29 @@
                 side = side + jnp.where(ends, roll(hi_ref[21 + tile], -fold_shift(z), 1) * in_hi, 0.0)
             om_ref[z, at] = main
             os_ref[z, at] = side
-            if z >= CZ - H + 1:
-                i = z - (CZ - H + 1)
-                up_ref[i, at] = main
-                shift = 14 * i + 7 if i < H else 120
-                mine = jnp.logical_and(lane >= 14 * i, lane < (14 * i + 14 if i < H else CX))
-                up_fold = jnp.where(mine, roll(side, shift, 1), up_fold)
-            if z <= H:
-                i = z - 1 if z > 0 else H
-                down_ref[i, at] = main
-                shift = 14 * i + 7 if i < H else 120
-                mine = jnp.logical_and(lane >= 14 * i, lane < (14 * i + 14 if i < H else CX))
-                down_fold = jnp.where(mine, roll(side, shift, 1), down_fold)
-        up_ref[H + 1, at] = up_fold
-        down_ref[H + 1, at] = down_fold
+    lower, upper = tile_rows(0), tile_rows(last)
+    for out, plane, depth in (
+        (above_ref, up_plane, lambda i: H - i),
+        (below_ref, down_plane, lambda i: i + 1),
+    ):
+        at_depth = {depth(i): plane(i) for i in range(H)}
+        for d in range(1, H):
+            out[d - 1] = jnp.where(sub >= d, om_ref[at_depth[d], lower], om_ref[at_depth[H - d], upper])
+        out[H - 1] = om_ref[plane(H), lower]
+        out[H] = om_ref[plane(H), upper]
+        out[H + 1] = fold_planes(lambda i: os_ref[plane(i), lower])
+        out[H + 2] = fold_planes(lambda i: os_ref[plane(i), upper])
+        out[H + 5] = jnp.zeros((H, CX), F32)
+        for given, factor, k in ((lo_ref, in_lo, 0), (hi_ref, in_hi, 1)):
+            for i in range(H + 1):
+                tile, g = plane(i) // 8, plane(i) % 8
+                row = given[18 + tile, g:g + 1, :] * factor
+                if i < H:
+                    out[H + 3 + k, i:i + 1] = row
+                else:
+                    out[H + 5, k:k + 1] = row
+            side = fold_planes(lambda i: jnp.broadcast_to(given[24 + plane(i) // 8, plane(i) % 8:plane(i) % 8 + 1, :], (H, CX)))
+            out[H + 5, 2 + k:3 + k] = side[0:1] * factor
 
 
 def pre_planes(level):
@@ -504,7 +537,12 @@
     return main, [c * (low * high) for c in main]
 
 
-def relax(planes, get, put, rhs, weights):
+def reached(level, z, t, part):
+    depth = max(0, H - z, z - H - CZ + 1)
+    return depth + (t in (0, TILES - 1)) + part <= SWEEPS - level
+
+
+def relax(level, planes, get, put, rhs, weights):
     lane = iota((H, CX), 1)
     first, last = lane == 0, lane == CX - 1
     z0 = planes[0]
@@ -517,12 +555,14 @@
             above, side_above = get(0, z + 1, at), get(1, z + 1, at)
             main_w, side_w = roll(main, 1, 1), roll(side, 1, 1)
             main_e, side_e = roll(main, -1, 1), roll(side, -1, 1)
-            total = (above + below) + (get(0, z, up) + get(0, z, down))
-            total = total + (jnp.where(first, side_w, main_w) + jnp.where(last, side_e, main_e))
-            put(0, z, at, (total - rhs(0, z, tile_rows(t))) * main_weight[t])
-            total = (side_above + side_below) + (get(1, z, up) + get(1, z, down))
-            total = total + (jnp.where(first, main_w, side_w) + jnp.where(last, main_e, side_e))
-            put(1, z, at, (total - rhs(1, z, tile_rows(t))) * side_weight[t])
+            if reached(level, z, t, 0):
+                total = (above + below) + (get(0, z, up) + get(0, z, down))
+                total = total + (jnp.where(first, side_w, main_w) + jnp.where(last, side_e, main_e))
+                put(0, z, at, (total - rhs(0, z, tile_rows(t))) * main_weight[t])
+            if reached(level, z, t, 1):
+                total = (side_above + side_below) + (get(1, z, up) + get(1, z, down))
+                total = total + (jnp.where(first, main_w, side_w) + jnp.where(last, main_e, side_e))
+                put(1, z, at, (total - rhs(1, z, tile_rows(t))) * side_weight[t])
             carry[t] = [main, above, side, side_above]
 
 
@@ -549,11 +589,11 @@
         def put(part, z, rows, value, level=level):
             pre_ref[pre_index(level, z), part, rows] = value
 
-        relax(range(*pre_planes(level)), get, put, rhs, lambda z: (main_coef, side_coef))
+        relax(level, range(*pre_planes(level)), get, put, rhs, lambda z: (main_coef, side_coef))
 
 
 def sweep_kernel(
-    dims, pos_ref, dm_ref, ds_ref, pre_ref, lo_ref, hi_ref, pred_ref, pres_ref, vel_out, pres_out,
+    dims, pos_ref, dm_ref, ds_ref, pre_ref, lo_ref, hi_ref, late_lo_ref, late_hi_ref, pred_ref, pres_ref, vel_out, pres_out,
     b_ref, phi_ref, vel_buf, pres_buf, sems,
 ):
     lo_z, hi_z = edges(pos_ref, dims)[4:6]
@@ -579,22 +619,50 @@
             for buf in range(2):
                 phi_ref[buf, part, z, 0:PADR] = zero
                 phi_ref[buf, part, z, PADR + EY:PADR + EY + PADR] = zero
+    sub = iota((H, CX), 0)
+
+    def arrived(early, late, t, low):
+        def planes(i):
+            depth = H - i if low else i + 1
+            if t in (0, TILES - 1):
+                if i == H:
+                    return late[H - 1 if t == 0 else H]
+                depth = depth if t == 0 else H - depth
+                return late[depth - 1] if 0 < depth < H else zero
+            value = early[i, tile_rows(t - 1)]
+            for k, edge, row in ((0, 1, 0), (1, TILES - 2, H - 1)):
+                if t == edge:
+                    fix = late[H + 3 + k, i:i + 1] if i < H else late[H + 5, k:k + 1]
+                    value = value + jnp.where(sub == row, fix, 0.0)
+            return value
+
+        if t in (0, TILES - 1):
+            fold = late[H + 1 if t == 0 else H + 2]
+        else:
+            fold = early[H + 1, tile_rows(t - 1)]
+            for k, edge, row in ((0, 1, 0), (1, TILES - 2, H - 1)):
+                if t == edge:
+                    fold = fold + jnp.where(sub == row, late[H + 5, 2 + k:3 + k], 0.0)
+        return planes, fold
+
     for t in range(TILES):
         rows = tile_rows(t)
-        folded = (lo_ref[H + 1, rows] * lo_scale, hi_ref[H + 1, rows] * hi_scale)
+        lo_planes, lo_fold = arrived(lo_ref, late_lo_ref, t, True)
+        hi_planes, hi_fold = arrived(hi_ref, late_hi_ref, t, False)
+        folded = (lo_fold * lo_scale, hi_fold * hi_scale)
         for z in outer:
             low = z < EZ // 2
-            halo, fold, factor = (lo_ref, folded[0], lo_scale) if low else (hi_ref, folded[1], hi_scale)
+            halo, fold, factor = (lo_planes, folded[0], lo_scale) if low else (hi_planes, folded[1], hi_scale)
             if z < H or z >= H + CZ:
                 g = z if low else z - H - CZ
-                main = halo[g, rows] * factor
+                main = halo(g) * factor
                 side = jnp.where(near, roll(fold, -(14 * g + 7), 1), 0.0)
                 if z in (H - 1, H + CZ):
                     k = 0 if low else SZ - 1
                     main = main + dm_ref[k, rows] * factor
                     side = side + ds_ref[k, rows] * factor
             else:
-                main = dm_ref[z - H + 1, rows] * scale + halo[H, rows] * factor
+                main = dm_ref[z - H + 1, rows] * scale + halo(H) * factor
                 side = ds_ref[z - H + 1, rows] * scale + jnp.where(ends, roll(fold, -120, 1), 0.0)
             b_ref[0, place[z], rows] = main
             b_ref[1, place[z], rows] = side
@@ -625,7 +693,7 @@
 
         runs = ((level, lo), (hi, EZ - level)) if hi > lo else ((level, EZ - level),)
         for run in runs:
-            relax(range(*run), reader(level - 1), put, rhs, weights)
+            relax(level, range(*run), reader(level - 1), put, rhs, weights)
 
     get = reader(SWEEPS - 1)
     chunk = 4
@@ -734,45 +802,47 @@
     faces = (xlo, xhi, ylo, yhi, zlo, zhi)
 
     pred_base, dual_base = call(
-        functools.partial(base_kernel, dims),
-        (),
-        (fields, index, scale, table, got),
-        (shape(3, CZ, CY, CX), shape(3, CZ, CY, CX)),
-        (pltpu.VMEM((3, CZ, CY, CX), F32),),
-        cost=1 << 30,
-    )
+        stencil_kernel, (), (fields,), (shape(3, CZ, CY, CX), shape(3, CZ, CY, CX)), cost=1 << 30
+    )
+    force = call(
+        functools.partial(force_kernel, dims), (), (index, scale, table, got), (shape(3, CZ, CY, CX),), cost=1 << 30
+    )[0]
     predicted, dm, ds, xr, xl = call(
         functools.partial(flow_kernel, dims),
         (),
-        (pred_base, fields) + faces,
+        (pred_base, force, fields) + faces,
         (shape(3, CZ, CY, CX), shape(SZ, EY, CX), shape(SZ, EY, CX), shape(3, EY, CX), shape(3, EY, CX)),
     )
     adjoint_next, yaw_grad, position_grad = call(
         functools.partial(dual_kernel, dims),
         (in_hbm(yaw), in_hbm(thrust_coef)),
-        (dual_base, fields, got) + faces,
+        (dual_base, force, fields, got) + faces,
         (shape(3, CZ, CY, CX), shape(1, 4), shape(2, 4)),
         (pltpu.VMEM((3, CZ, CY, CX), F32), pltpu.SemaphoreType.DMA((3,))),
         out_specs=[ANY, VMEM, VMEM],
         cost=1 << 30,
     )
     lo, hi = swap(xr, xl, "gx")
-    dm, ds, up, down = call(
+    dm, ds, up, down, above, below = call(
         functools.partial(x_kernel, dims), (), (dm, ds, lo, hi),
-        (shape(SZ, EY, CX), shape(SZ, EY, CX), shape(27, H, CX), shape(27, H, CX)),
+        (
+            shape(SZ, EY, CX), shape(SZ, EY, CX), shape(27, H, CX), shape(27, H, CX),
+            shape(H + 2, CY, CX), shape(H + 2, CY, CX),
+        ),
     )
     lo, hi = swap(up, down, "gy")
+    early_lo, early_hi = swap(above, below, "gz")
     lo, yaw_grad = lax.optimization_barrier((lo, yaw_grad))
-    dm, ds, up, down = call(
+    dm, ds, above, below = call(
         functools.partial(y_kernel, dims), (), (dm, ds, lo, hi),
-        (shape(SZ, EY, CX), shape(SZ, EY, CX), shape(H + 2, EY, CX), shape(H + 2, EY, CX)),
-    )
-    lo, hi = swap(up, down, "gz")
+        (shape(SZ, EY, CX), shape(SZ, EY, CX), shape(LATE, H, CX), shape(LATE, H, CX)),
+    )
+    late_lo, late_hi = swap(above, below, "gz")
     pre = call(
         functools.partial(inner_kernel, dims), (), (dm, ds), (shape(PRE, 2, EY + 2 * PADR, CX),), cost=1 << 30
     )[0]
     velocity_next, pressure_next = call(
-        functools.partial(sweep_kernel, dims), (), (dm, ds, pre, lo, hi, predicted, pressure),
+        functools.partial(sweep_kernel, dims), (), (dm, ds, pre, early_lo, early_hi, late_lo, late_hi, predicted, pressure),
         (shape(3, CZ, CY, CX), shape(CZ, CY, CX)),
         (
             pltpu.VMEM((2, EZ - CZ + 2, EY, CX), F32), pltpu.VMEM((2, 2, EZ, EY + 2 * PADR, CX), F32),

time: 60.5 us -> 60.9 us (level)
  waiting for transfers between devices: 11.1 us -> 8.31 us
  starting transfers between devices: 32.6 us -> 34.4 us
  local copies, waits for them, and re-layouts: 0.01 us -> 0.88 us
    ppermute x12 -> x14, starting transfers between devices: 18.2 us -> 20 us  [swap(): return (lax.ppermute(up, axis, forward), lax.ppermute(down, axis, backward))]
    all_to_all x1, waiting for transfers between devices: 2.04 us -> 0.23 us  [shards(): got = lax.all_to_all(payload, axes, 0, 0, tiled=True)]
    ppermute x12 -> x14, waiting for transfers between devices: 9.06 us -> 8.08 us  [swap(): return (lax.ppermute(up, axis, forward), lax.ppermute(down, axis, backward))]
    unnamed x2 -> x6, local copies, waits for them, and re-layouts: 0.01 us -> 0.88 us
    pallas_call x8 -> x9, Pallas kernels: 15.7 us -> 16.1 us  [call(): pl.pallas_call(functools.partial(kernel, Place()), out_shape=outs, in_spe...]
  transfers between devices with their start and end apart: 13 -> 15, of which waited for: 6 -> 5; matrix products, arithmetic and copies ran while one was open for 0% -> 0% of each run, Pallas kernels for 9% -> 11%
where the time goes in v1:
time: 60.9 us; the launch traced here: 60.7 us
  starting transfers between devices  34.4 us (56%)
  Pallas kernels  16.1 us (26%)
  waiting for transfers between devices  8.31 us (14%)
  between operations  0.95 us (2%)
  local copies, waits for them, and re-layouts  0.88 us (1%)
    ppermute x14, starting transfers between devices, swap(): return (lax.ppermute(up, axis, forward), lax.ppermute(down, axis, backward))  20 us
    pallas_call x9, Pallas kernels, call(): pl.pallas_call(functools.partial(kernel, Place()), out_shape=outs, in_spe...  16.1 us
    all_to_all x1, starting transfers between devices, shards(): got = lax.all_to_all(payload, axes, 0, 0, tiled=True)  14.4 us
    ppermute x14, waiting for transfers between devices, swap(): return (lax.ppermute(up, axis, forward), lax.ppermute(down, axis, backward))  8.08 us
  transfers between devices with their start and end apart: 15, of which 5 were waited for; matrix products, arithmetic and copies ran while one was open for 0% of the time, Pallas kernels for 11%

profile of v1, /device:TPU:24, one launch (start us, length us, event | category | flops | bytes accessed | tf_op | source)
XLA Modules:
  0.0 60.7 jit_solution(14660522644811144724)
XLA Ops:
  0.6 4.1 %shard_map.146 = (f32[256,128]{1,0:T(8,128)}, f32[32,128]{1,0:T(8,128)S(1)}, f32[32,128]{1,0:T(8,128)S(1)}, f32[96,128]{1,0:T(8,128)S(1)}, f32[96,128]{1,0:T(8,1...) custom-call(f32[4]{0:T(128)} %yaw_ref.3, ...), custom_call_target="tpu_custom_call" | custom-call | tf_op jit(solution)/shard_map/pallas_call | solution.py:759
  4.7 14.4 %all-to-all-start = ((f32[256,1,128]{2,1,0:T(1,128)}), f32[256,1,128]{2,1,0:T(1,128)S(1)}, u32[]{:S(2)}, u32[]{:S(2)}) async-start(f32[256,1,128]{2,1,0:T(1,128)} %bitcast.5), calls=%async_computation | async-start | bytes 262144 | tf_op jit(solution)/shard_map/all_to_all | solution.py:797
  19.1 0.2 collective-permute-start
  19.3 4.2 %collective-permute-start.1 = (f32[32,128]{1,0:T(8,128)S(1)}, f32[32,128]{1,0:T(8,128)S(1)}, u32[]{:S(2)}, u32[]{:S(2)}) collective-permute-start(f32[32,128]{1,0:T(8,128)S(1)} %get-tuple-element.51), channel_id=1, source_target_pairs={{16,0},{32,16},{48,32},{64,48},{80,64},{96,80},{112,96},{128,112},... | collective-permute-start | bytes 49160 | tf_op jit(solution)/shard_map/ppermute | solution.py:727
  23.5 1.5 %collective-permute-start.2 = (f32[96,128]{1,0:T(8,128)S(1)}, f32[96,128]{1,0:T(8,128)S(1)}, u32[]{:S(2)}, u32[]{:S(2)}) collective-permute-start(f32[96,128]{1,0:T(8,128)S(1)} %get-tuple-element.52), channel_id=1, source_target_pairs={{0,4},{4,8},{8,12},{12,0},{1,5},{5,9},{9,13},{13,1},{2,6},{6,10},{... | collective-permute-start | bytes 147464 | tf_op jit(solution)/shard_map/ppermute | solution.py:727
  25.0 1.8 %collective-permute-start.3 = (f32[96,128]{1,0:T(8,128)S(1)}, f32[96,128]{1,0:T(8,128)S(1)}, u32[]{:S(2)}, u32[]{:S(2)}) collective-permute-start(f32[96,128]{1,0:T(8,128)S(1)} %get-tuple-element.53), channel_id=1, source_target_pairs={{4,0},{8,4},{12,8},{0,12},{5,1},{9,5},{13,9},{1,13},{6,2},{10,6},{... | collective-permute-start | bytes 147464 | tf_op jit(solution)/shard_map/ppermute | solution.py:727
  26.7 0.7 %collective-permute-start.4 = (f32[6,32,128]{2,1,0:T(8,128)S(1)}, f32[6,32,128]{2,1,0:T(8,128)S(1)}, u32[]{:S(2)}, u32[]{:S(2)}) collective-permute-start(f32[6,32,128]{2,1,0:T(8,128)S(1)} %get-tuple-element.54), channel_id=1, source_target_pairs={{0,1},{1,2},{2,3},{3,0},{4,5},{5,6},{6,7},{7,4},{8,9},{9,10},{10,1... | collective-permute-start | bytes 294920 | tf_op jit(solution)/shard_map/ppermute | solution.py:727
  27.4 0.9 %shard_map.147 = (f32[3,16,32,128]{3,2,1,0:T(8,128)S(1)}, f32[3,16,32,128]{3,2,1,0:T(8,128)S(1)}) custom-call(f32[7,16,32,128]{3,2,1,0:T(8,128)S(1)} %get-tuple-element.42.fld_ref), custom_call_target="tpu_custom_call" | custom-call | flops 1073741824 | bytes 16777216 | tf_op jit(solution)/shard_map/pallas_call | solution.py:759
  28.4 0.0 copy-start.1
  28.4 0.9 %copy-done.1 = f32[3,16,32,128]{3,2,1,0:T(8,128)} copy-done((f32[3,16,32,128]{3,2,1,0:T(8,128)}, f32[3,16,32,128]{3,2,1,0:T(8,128)S(1)}, u32[]{:S(2)}) %copy-start.1) | copy-done | bytes 786456
  29.3 0.0 collective-permute-done.xlo_ref
  29.3 1.3 %collective-permute-start.5 = (f32[6,32,128]{2,1,0:T(8,128)S(1)}, f32[6,32,128]{2,1,0:T(8,128)S(1)}, u32[]{:S(2)}, u32[]{:S(2)}) collective-permute-start(f32[6,32,128]{2,1,0:T(8,128)S(1)} %get-tuple-element.55), channel_id=1, source_target_pairs={{1,0},{2,1},{3,2},{0,3},{5,4},{6,5},{7,6},{4,7},{9,8},{10,9},{11,1... | collective-permute-start | bytes 294920 | tf_op jit(solution)/shard_map/ppermute | solution.py:727
  30.6 0.2 all-to-all-done
  30.8 0.0 copy-start.2
  30.8 1.6 %shard_map.148.field_ref = f32[3,16,32,128]{3,2,1,0:T(8,128)S(1)} custom-call(s32[2,512]{1,0:T(2,128)S(1)} %get-tuple-element.44.index_ref, f32[1,512]{1,0:T(1,128)S(1)} %get-tuple-element.45.scale_ref, s32[8,128]{1,0:T(8,128)S(1)} %get-tuple-element.46.owner_ref, f32[256,128]{1,0:T(8,128)S(1)} %bitcast.9), custom_call_target="tpu_custom_call" | custom-call | flops 1073741824 | bytes 16777216 | tf_op jit(solution)/shard_map/pallas_call | solution.py:759
  32.4 0.0 collective-permute-done.1.xhi_ref
  32.4 0.0 collective-permute-done.2.ylo_ref
  32.4 0.0 collective-permute-done.3.yhi_ref
  32.4 0.0 collective-permute-done.4.zlo_ref
  32.4 2.7 %collective-permute-done.5.zhi_ref = f32[6,32,128]{2,1,0:T(8,128)S(1)} collective-permute-done((f32[6,32,128]{2,1,0:T(8,128)S(1)}, f32[6,32,128]{2,1,0:T(8,128)S(1)}, u32[]{:S(2)}, u32[]{:S(2)}) %collective-permute-start.5) | collective-permute-done | bytes 98336 | tf_op jit(solution)/shard_map/ppermute | solution.py:727
  35.1 0.8 %shard_map.149 = (f32[3,16,32,128]{3,2,1,0:T(8,128)S(1)}, f32[18,48,128]{2,1,0:T(8,128)S(1)}, f32[18,48,128]{2,1,0:T(8,128)S(1)}, f32[3,48,128]{2,1,0:T(8,128)S(1)}, f32[3,48,128]{2,1,0:T(8,128)S(1)}) custom-call(f32[3,16,32,128]{3,2,1,0:T(8,128)S(1)} %get-tuple-element.43.base_ref, f32[3,16,32,128]{3,2,1,0:T(8,128)S(1)} %shard_map.148.field_ref, ...), custom_call_target="tpu_custom_call" | custom-call | tf_op jit(solution)/shard_map/pallas_call | solution.py:759
  35.9 0.0 collective-permute-start.6
  36.0 2.9 %collective-permute-start.7 = (f32[3,48,128]{2,1,0:T(8,128)S(1)}, f32[3,48,128]{2,1,0:T(8,128)S(1)}, u32[]{:S(2)}, u32[]{:S(2)}) collective-permute-start(f32[3,48,128]{2,1,0:T(8,128)S(1)} %get-tuple-element.59), channel_id=1, source_target_pairs={{16,0},{32,16},{48,32},{64,48},{80,64},{96,80},{112,96},{128,112},... | collective-permute-start | bytes 221192 | tf_op jit(solution)/shard_map/ppermute | solution.py:727
  38.9 2.0 %collective-permute-done.6.lo_ref = f32[3,48,128]{2,1,0:T(8,128)S(1)} collective-permute-done((f32[3,48,128]{2,1,0:T(8,128)S(1)}, f32[3,48,128]{2,1,0:T(8,128)S(1)}, u32[]{:S(2)}, u32[]{:S(2)}) %collective-permute-start.6) | collective-permute-done | bytes 73760 | tf_op jit(solution)/shard_map/ppermute | solution.py:727
  40.9 0.0 collective-permute-done.7.hi_ref
  40.9 0.5 shard_map.150
  41.4 0.1 collective-permute-start.8
  41.5 3.2 %collective-permute-start.9 = (f32[27,8,128]{2,1,0:T(8,128)S(1)}, f32[27,8,128]{2,1,0:T(8,128)S(1)}, u32[]{:S(2)}, u32[]{:S(2)}) collective-permute-start(f32[27,8,128]{2,1,0:T(8,128)S(1)} %get-tuple-element.66), channel_id=1, source_target_pairs={{4,0},{8,4},{12,8},{0,12},{5,1},{9,5},{13,9},{1,13},{6,2},{10,6},{... | collective-permute-start | bytes 331784 | tf_op jit(solution)/shard_map/ppermute | solution.py:727
  44.7 0.0 collective-permute-start.10
  44.7 2.0 %collective-permute-start.11 = (f32[10,32,128]{2,1,0:T(8,128)S(1)}, f32[10,32,128]{2,1,0:T(8,128)S(1)}, u32[]{:S(2)}, u32[]{:S(2)}) collective-permute-start(f32[10,32,128]{2,1,0:T(8,128)S(1)} %get-tuple-element.70), channel_id=1, source_target_pairs={{1,0},{2,1},{3,2},{0,3},{5,4},{6,5},{7,6},{4,7},{9,8},{10,9},{11,1... | collective-permute-start | bytes 491528 | tf_op jit(solution)/shard_map/ppermute | solution.py:727
  46.7 0.0 copy-done.2
  46.7 2.5 %shard_map.151 = (f32[3,16,32,128]{3,2,1,0:T(8,128)}, f32[1,4]{1,0:T(1,128)}, f32[2,4]{1,0:T(2,128)}) custom-call(f32[4]{0:T(128)} %yaw_ref.3, f32[4]{0:T(128)} %ct_ref.3, f32[3,16,32,128]{3,2,1,0:T(8,128)S(1)} %copy-done.2, f32[3,16,32,128]{3,2,1,0:T(8,128)S(1)} %shard_map.148.field_ref, f32[7,16,32,128]{3,2,1,0:T(8,128)S(1)} %get-tuple-element.42.fld_ref, ...), custom_call_target="tpu_custom_call" | custom-call | flops 1073741824 | bytes 16777216 | tf_op jit(solution)/shard_map/pallas_call | solution.py:759
  49.2 0.0 copy-start
  49.2 0.0 collective-permute-done.8.lo_ref
  49.2 0.0 collective-permute-done.9.hi_ref
  49.2 0.2 shard_map.152
  49.5 1.3 %collective-permute-start.12 = (f32[14,8,128]{2,1,0:T(8,128)S(1)}, f32[14,8,128]{2,1,0:T(8,128)S(1)}, u32[]{:S(2)}, u32[]{:S(2)}) collective-permute-start(f32[14,8,128]{2,1,0:T(8,128)S(1)} %get-tuple-element.71), channel_id=1, source_target_pairs={{0,1},{1,2},{2,3},{3,0},{4,5},{5,6},{6,7},{7,4},{8,9},{9,10},{10,1... | collective-permute-start | bytes 172040 | tf_op jit(solution)/shard_map/ppermute | solution.py:727
  50.8 0.8 %collective-permute-start.13 = (f32[14,8,128]{2,1,0:T(8,128)S(1)}, f32[14,8,128]{2,1,0:T(8,128)S(1)}, u32[]{:S(2)}, u32[]{:S(2)}) collective-permute-start(f32[14,8,128]{2,1,0:T(8,128)S(1)} %get-tuple-element.72), channel_id=1, source_target_pairs={{1,0},{2,1},{3,2},{0,3},{5,4},{6,5},{7,6},{4,7},{9,8},{10,9},{11,1... | collective-permute-start | bytes 172040 | tf_op jit(solution)/shard_map/ppermute | solution.py:727
  51.6 1.2 %shard_map.153.pre_ref = f32[56,2,64,128]{3,2,1,0:T(8,128)S(1)} custom-call(f32[18,48,128]{2,1,0:T(8,128)S(1)} %get-tuple-element.67.dm_ref, f32[18,48,128]{2,1,0:T(8,128)S(1)} %get-tuple-element.68.ds_ref), custom_call_target="tpu_custom_call" | custom-call | flops 1073741824 | bytes 16777216 | tf_op jit(solution)/shard_map/pallas_call | solution.py:759
  52.8 0.0 collective-permute-done.10.lo_ref
  52.8 0.0 collective-permute-done.11.hi_ref
  52.8 0.9 %collective-permute-done.12.late_lo_ref = f32[14,8,128]{2,1,0:T(8,128)S(1)} collective-permute-done((f32[14,8,128]{2,1,0:T(8,128)S(1)}, f32[14,8,128]{2,1,0:T(8,128)S(1)}, u32[]{:S(2)}, u32[]{:S(2)}) %collective-permute-start.12) | collective-permute-done | bytes 57376 | tf_op jit(solution)/shard_map/ppermute | solution.py:727
  53.7 2.4 %collective-permute-done.13.late_hi_ref = f32[14,8,128]{2,1,0:T(8,128)S(1)} collective-permute-done((f32[14,8,128]{2,1,0:T(8,128)S(1)}, f32[14,8,128]{2,1,0:T(8,128)S(1)}, u32[]{:S(2)}, u32[]{:S(2)}) %collective-permute-start.13) | collective-permute-done | bytes 57376 | tf_op jit(solution)/shard_map/ppermute | solution.py:727
  56.2 0.0 copy-done
  56.2 4.4 %shard_map.154 = (f32[3,16,32,128]{3,2,1,0:T(8,128)}, f32[16,32,128]{2,1,0:T(8,128)}) custom-call(f32[18,48,128]{2,1,0:T(8,128)S(1)} %get-tuple-element.67.dm_ref, f32[18,48,128]{2,1,0:T(8,128)S(1)} %get-tuple-element.68.ds_ref, f32[56,2,64,128]{3,2,1,0:T(8,128)S(1)} %shard_map.153.pre_ref, f32[10,32,128]{2,1,0:T(8,128)S(1)} %collective-permute-done.10.lo_ref, ...), custom_call_target="tpu_custom_call" | custom-call | tf_op jit(solution)/shard_map/pallas_call | solution.py:759
Async XLA Ops:
  4.7 26.1 %all-to-all-start = ((f32[256,1,128]{2,1,0:T(1,128)}), f32[256,1,128]{2,1,0:T(1,128)S(1)}, u32[]{:S(2)}, u32[]{:S(2)}) async-start(f32[256,1,128]{2,1,0:T(1,128)} %bitcast.5), calls=%async_computation | async-start | bytes 262144 | tf_op jit(solution)/shard_map/all_to_all | solution.py:797
  19.1 10.1 %collective-permute-start = (f32[32,128]{1,0:T(8,128)S(1)}, f32[32,128]{1,0:T(8,128)S(1)}, u32[]{:S(2)}, u32[]{:S(2)}) collective-permute-start(f32[32,128]{1,0:T(8,128)S(1)} %get-tuple-element.48), channel_id=1, source_target_pairs={{0,16},{16,32},{32,48},{48,64},{64,80},{80,96},{96,112},{112,128},... | collective-permute-start | bytes 49160 | tf_op jit(solution)/shard_map/ppermute | solution.py:727
  19.3 13.1 %collective-permute-start.1 = (f32[32,128]{1,0:T(8,128)S(1)}, f32[32,128]{1,0:T(8,128)S(1)}, u32[]{:S(2)}, u32[]{:S(2)}) collective-permute-start(f32[32,128]{1,0:T(8,128)S(1)} %get-tuple-element.51), channel_id=1, source_target_pairs={{16,0},{32,16},{48,32},{64,48},{80,64},{96,80},{112,96},{128,112},... | collective-permute-start | bytes 49160 | tf_op jit(solution)/shard_map/ppermute | solution.py:727
  23.5 8.9 %collective-permute-start.2 = (f32[96,128]{1,0:T(8,128)S(1)}, f32[96,128]{1,0:T(8,128)S(1)}, u32[]{:S(2)}, u32[]{:S(2)}) collective-permute-start(f32[96,128]{1,0:T(8,128)S(1)} %get-tuple-element.52), channel_id=1, source_target_pairs={{0,4},{4,8},{8,12},{12,0},{1,5},{5,9},{9,13},{13,1},{2,6},{6,10},{... | collective-permute-start | bytes 147464 | tf_op jit(solution)/shard_map/ppermute | solution.py:727
  25.0 7.4 %collective-permute-start.3 = (f32[96,128]{1,0:T(8,128)S(1)}, f32[96,128]{1,0:T(8,128)S(1)}, u32[]{:S(2)}, u32[]{:S(2)}) collective-permute-start(f32[96,128]{1,0:T(8,128)S(1)} %get-tuple-element.53), channel_id=1, source_target_pairs={{4,0},{8,4},{12,8},{0,12},{5,1},{9,5},{13,9},{1,13},{6,2},{10,6},{... | collective-permute-start | bytes 147464 | tf_op jit(solution)/shard_map/ppermute | solution.py:727
  26.7 5.7 %collective-permute-start.4 = (f32[6,32,128]{2,1,0:T(8,128)S(1)}, f32[6,32,128]{2,1,0:T(8,128)S(1)}, u32[]{:S(2)}, u32[]{:S(2)}) collective-permute-start(f32[6,32,128]{2,1,0:T(8,128)S(1)} %get-tuple-element.54), channel_id=1, source_target_pairs={{0,1},{1,2},{2,3},{3,0},{4,5},{5,6},{6,7},{7,4},{8,9},{9,10},{10,1... | collective-permute-start | bytes 294920 | tf_op jit(solution)/shard_map/ppermute | solution.py:727
  28.4 0.9 %copy-start.1 = (f32[3,16,32,128]{3,2,1,0:T(8,128)}, f32[3,16,32,128]{3,2,1,0:T(8,128)S(1)}, u32[]{:S(2)}) copy-start(f32[3,16,32,128]{3,2,1,0:T(8,128)S(1)} %get-tuple-element.63.base_ref) | copy-start | bytes 2359300
  29.3 5.8 %collective-permute-start.5 = (f32[6,32,128]{2,1,0:T(8,128)S(1)}, f32[6,32,128]{2,1,0:T(8,128)S(1)}, u32[]{:S(2)}, u32[]{:S(2)}) collective-permute-start(f32[6,32,128]{2,1,0:T(8,128)S(1)} %get-tuple-element.55), channel_id=1, source_target_pairs={{1,0},{2,1},{3,2},{0,3},{5,4},{6,5},{7,6},{4,7},{9,8},{10,9},{11,1... | collective-permute-start | bytes 294920 | tf_op jit(solution)/shard_map/ppermute | solution.py:727
  30.8 15.9 %copy-start.2 = (f32[3,16,32,128]{3,2,1,0:T(8,128)S(1)}, f32[3,16,32,128]{3,2,1,0:T(8,128)}, u32[]{:S(2)}) copy-start(f32[3,16,32,128]{3,2,1,0:T(8,128)} %copy-done.1) | copy-start | bytes 2359300
  35.9 5.0 %collective-permute-start.6 = (f32[3,48,128]{2,1,0:T(8,128)S(1)}, f32[3,48,128]{2,1,0:T(8,128)S(1)}, u32[]{:S(2)}, u32[]{:S(2)}) collective-permute-start(f32[3,48,128]{2,1,0:T(8,128)S(1)} %get-tuple-element.58), channel_id=1, source_target_pairs={{0,16},{16,32},{32,48},{48,64},{64,80},{80,96},{96,112},{112,128},... | collective-permute-start | bytes 221192 | tf_op jit(solution)/shard_map/ppermute | solution.py:727
  36.0 5.0 %collective-permute-start.7 = (f32[3,48,128]{2,1,0:T(8,128)S(1)}, f32[3,48,128]{2,1,0:T(8,128)S(1)}, u32[]{:S(2)}, u32[]{:S(2)}) collective-permute-start(f32[3,48,128]{2,1,0:T(8,128)S(1)} %get-tuple-element.59), channel_id=1, source_target_pairs={{16,0},{32,16},{48,32},{64,48},{80,64},{96,80},{112,96},{128,112},... | collective-permute-start | bytes 221192 | tf_op jit(solution)/shard_map/ppermute | solution.py:727
  41.4 7.8 %collective-permute-start.8 = (f32[27,8,128]{2,1,0:T(8,128)S(1)}, f32[27,8,128]{2,1,0:T(8,128)S(1)}, u32[]{:S(2)}, u32[]{:S(2)}) collective-permute-start(f32[27,8,128]{2,1,0:T(8,128)S(1)} %get-tuple-element.62), channel_id=1, source_target_pairs={{0,4},{4,8},{8,12},{12,0},{1,5},{5,9},{9,13},{13,1},{2,6},{6,10},{... | collective-permute-start | bytes 331784 | tf_op jit(solution)/shard_map/ppermute | solution.py:727
  41.5 7.8 %collective-permute-start.9 = (f32[27,8,128]{2,1,0:T(8,128)S(1)}, f32[27,8,128]{2,1,0:T(8,128)S(1)}, u32[]{:S(2)}, u32[]{:S(2)}) collective-permute-start(f32[27,8,128]{2,1,0:T(8,128)S(1)} %get-tuple-element.66), channel_id=1, source_target_pairs={{4,0},{8,4},{12,8},{0,12},{5,1},{9,5},{13,9},{1,13},{6,2},{10,6},{... | collective-permute-start | bytes 331784 | tf_op jit(solution)/shard_map/ppermute | solution.py:727
  44.7 8.1 %collective-permute-start.10 = (f32[10,32,128]{2,1,0:T(8,128)S(1)}, f32[10,32,128]{2,1,0:T(8,128)S(1)}, u32[]{:S(2)}, u32[]{:S(2)}) collective-permute-start(f32[10,32,128]{2,1,0:T(8,128)S(1)} %get-tuple-element.69), channel_id=1, source_target_pairs={{0,1},{1,2},{2,3},{3,0},{4,5},{5,6},{6,7},{7,4},{8,9},{9,10},{10,1... | collective-permute-start | bytes 491528 | tf_op jit(solution)/shard_map/ppermute | solution.py:727
  44.7 8.1 %collective-permute-start.11 = (f32[10,32,128]{2,1,0:T(8,128)S(1)}, f32[10,32,128]{2,1,0:T(8,128)S(1)}, u32[]{:S(2)}, u32[]{:S(2)}) collective-permute-start(f32[10,32,128]{2,1,0:T(8,128)S(1)} %get-tuple-element.70), channel_id=1, source_target_pairs={{1,0},{2,1},{3,2},{0,3},{5,4},{6,5},{7,6},{4,7},{9,8},{10,9},{11,1... | collective-permute-start | bytes 491528 | tf_op jit(solution)/shard_map/ppermute | solution.py:727
  49.2 6.9 %copy-start = (f32[16,32,128]{2,1,0:T(8,128)S(1)}, f32[16,32,128]{2,1,0:T(8,128)}, u32[]{:S(2)}) copy-start(f32[16,32,128]{2,1,0:T(8,128)} %pres_ref.1) | copy-start | bytes 786436
  49.5 4.3 %collective-permute-start.12 = (f32[14,8,128]{2,1,0:T(8,128)S(1)}, f32[14,8,128]{2,1,0:T(8,128)S(1)}, u32[]{:S(2)}, u32[]{:S(2)}) collective-permute-start(f32[14,8,128]{2,1,0:T(8,128)S(1)} %get-tuple-element.71), channel_id=1, source_target_pairs={{0,1},{1,2},{2,3},{3,0},{4,5},{5,6},{6,7},{7,4},{8,9},{9,10},{10,1... | collective-permute-start | bytes 172040 | tf_op jit(solution)/shard_map/ppermute | solution.py:727
  50.8 5.4 %collective-permute-start.13 = (f32[14,8,128]{2,1,0:T(8,128)S(1)}, f32[14,8,128]{2,1,0:T(8,128)S(1)}, u32[]{:S(2)}, u32[]{:S(2)}) collective-permute-start(f32[14,8,128]{2,1,0:T(8,128)S(1)} %get-tuple-element.72), channel_id=1, source_target_pairs={{1,0},{2,1},{3,2},{0,3},{5,4},{6,5},{7,6},{4,7},{9,8},{10,9},{11,1... | collective-permute-start | bytes 172040 | tf_op jit(solution)/shard_map/ppermute | solution.py:727

commit v2 on v1

--- a/solution.py
+++ b/solution.py
@@ -145,16 +145,17 @@
     lane = iota((H, CX), 1)
     for t in range(CY // H):
         at = slice(H * t, H * t + H)
-        right = jnp.zeros((H, CX), F32)
-        left = jnp.zeros((H, CX), F32)
-        for f in range(6):
-            for z in range(CZ):
-                tile = fld_ref[f, z, at]
-                spot = lane == f * CZ + z
-                right = jnp.where(spot, roll(tile, f * CZ + z + 1, 1), right)
-                left = jnp.where(spot, roll(tile, f * CZ + z, 1), left)
-        xr_ref[at] = right
-        xl_ref[at] = left
+        for half in range(2):
+            right = jnp.zeros((H, CX), F32)
+            left = jnp.zeros((H, CX), F32)
+            for f in range(3):
+                for z in range(CZ):
+                    spot = 2 * (f * CZ + z) + 1
+                    moved = roll(fld_ref[3 * half + f, z, at], spot + 1, 1)
+                    right = jnp.where(lane == spot, moved, right)
+                    left = jnp.where(lane == spot + 1, moved, left)
+            xr_ref[half, at] = right
+            xl_ref[half, at] = left
     for f in range(6):
         yr_ref[f * CZ:(f + 1) * CZ, :] = fld_ref[f, :, CY - 1, :]
         yl_ref[f * CZ:(f + 1) * CZ, :] = fld_ref[f, :, 0, :]
@@ -312,11 +313,13 @@
     comp = f - first
     for t in range(CY // H):
         at = tile_rows(t)
-        face_lo, face_hi = xlo_ref[at] * lo_x, xhi_ref[at] * hi_x
+        odd = jnp.bitwise_and(lane, 1) == 1
+        face = jnp.where(odd, xlo_ref[f // 3, at] * lo_x, roll(xhi_ref[f // 3, at] * hi_x, -2, 1))
         for z in range(CZ):
             spot = f * CZ + z
-            west = jnp.where(lane == 0, roll(face_lo, -spot, 1), 0.0)
-            east = jnp.where(lane == CX - 1, roll(face_hi, CX - 1 - spot, 1), 0.0)
+            moved = roll(face, -(2 * (spot % (3 * CZ)) + 1), 1)
+            west = jnp.where(lane == 0, moved, 0.0)
+            east = jnp.where(lane == CX - 1, moved, 0.0)
             lap = west + east
             if t == 0:
                 lap = lap + jnp.where(sub == 0, ylo_ref[spot:spot + 1, :] * lo_y, 0.0)
@@ -785,7 +788,7 @@
         (in_hbm(yaw), in_hbm(thrust_coef)),
         tuple(in_hbm(a) for a in (velocity, adjoint, viscosity, cells, turbine, weight, disk_dweight, owner)),
         (
-            shape(n_dev, CX), in_vmem(CY, CX), in_vmem(CY, CX), in_vmem(6 * CZ, CX), in_vmem(6 * CZ, CX),
+            shape(n_dev, CX), in_vmem(2, CY, CX), in_vmem(2, CY, CX), in_vmem(6 * CZ, CX), in_vmem(6 * CZ, CX),
             in_vmem(6, CY, CX), in_vmem(6, CY, CX), in_vmem(7, CZ, CY, CX), in_vmem(2, cells.shape[1], dtype=jnp.int32),
             in_vmem(*weight.shape), in_vmem(*owner.shape, dtype=jnp.int32),
         ),
@@ -795,14 +798,16 @@
         limit=ENTRY_LIMIT,
     )
     got = lax.all_to_all(payload, axes, 0, 0, tiled=True)
-    xlo, xhi = swap(xr, xl, "gx")
     ylo, yhi = swap(yr, yl, "gy")
-    xlo, zl = lax.optimization_barrier((xlo, zl))
     zlo, zhi = swap(zr, zl, "gz")
+    count = n_gx
+    xlo = lax.ppermute(xr, "gx", [(i, (i + 1) % count) for i in range(count)])
+    xlo, xl = lax.optimization_barrier((xlo, xl))
+    xhi = lax.ppermute(xl, "gx", [((i + 1) % count, i) for i in range(count)])
     faces = (xlo, xhi, ylo, yhi, zlo, zhi)
 
     pred_base, dual_base = call(
-        stencil_kernel, (), (fields,), (shape(3, CZ, CY, CX), shape(3, CZ, CY, CX)), cost=1 << 30
+        stencil_kernel, (), (fields,), (in_vmem(3, CZ, CY, CX), in_vmem(3, CZ, CY, CX)), cost=1 << 30
     )
     force = call(
         functools.partial(force_kernel, dims), (), (index, scale, table, got), (shape(3, CZ, CY, CX),), cost=1 << 30

time: 60.9 us -> 60.4 us (level)
  waiting for transfers between devices: 8.31 us -> 7.5 us
    ppermute x14 -> x12, starting transfers between devices: 20 us -> 16.7 us  [swap(): return (lax.ppermute(up, axis, forward), lax.ppermute(down, axis, backward))]
    ppermute x0 -> x2, starting transfers between devices: none -> 3.29 us  [the longest x1 3.13 us: shards(): xhi = lax.ppermute(xl, 'gx', [((i + 1) % count, i) for i in range(count)])]
    ppermute x14 -> x12, waiting for transfers between devices: 8.08 us -> 6.22 us  [swap(): return (lax.ppermute(up, axis, forward), lax.ppermute(down, axis, backward))]
    all_to_all x1, waiting for transfers between devices: 0.23 us -> 1.28 us  [shards(): got = lax.all_to_all(payload, axes, 0, 0, tiled=True)]
  transfers between devices with their start and end apart: 15 -> 15, of which waited for: 5 -> 4; matrix products, arithmetic and copies ran while one was open for 0% -> 0% of each run, Pallas kernels for 11% -> 11%
where the time goes in v2:
time: 60.4 us; the launch traced here: 60.2 us
  starting transfers between devices  34.4 us (57%)
  Pallas kernels  16.5 us (27%)
  waiting for transfers between devices  7.5 us (12%)
  between operations  0.95 us (2%)
  local copies, waits for them, and re-layouts  0.88 us (1%)
    ppermute x12, starting transfers between devices, swap(): return (lax.ppermute(up, axis, forward), lax.ppermute(down, axis, backward))  16.7 us
    pallas_call x9, Pallas kernels, call(): pl.pallas_call(functools.partial(kernel, Place()), out_shape=outs, in_spe...  16.5 us
    all_to_all x1, starting transfers between devices, shards(): got = lax.all_to_all(payload, axes, 0, 0, tiled=True)  14.4 us
    ppermute x12, waiting for transfers between devices, swap(): return (lax.ppermute(up, axis, forward), lax.ppermute(down, axis, backward))  6.22 us
    ppermute x1, starting transfers between devices, shards(): xhi = lax.ppermute(xl, 'gx', [((i + 1) % count, i) for i in range(count)])  3.13 us
    all_to_all x1, waiting for transfers between devices, shards(): got = lax.all_to_all(payload, axes, 0, 0, tiled=True)  1.28 us
  transfers between devices with their start and end apart: 15, of which 4 were waited for; matrix products, arithmetic and copies ran while one was open for 0% of the time, Pallas kernels for 11%

profile of v2, /device:TPU:24, one launch (start us, length us, event | category | flops | bytes accessed | tf_op | source)
XLA Modules:
  0.0 60.2 jit_solution(3441626448400796424)
XLA Ops:
  0.6 3.8 %shard_map.146 = (f32[256,128]{1,0:T(8,128)}, f32[2,32,128]{2,1,0:T(8,128)S(1)}, f32[2,32,128]{2,1,0:T(8,128)S(1)}, f32[96,128]{1,0:T(8,128)S(1)}, f32[96,128]{1...) custom-call(f32[4]{0:T(128)} %yaw_ref.3, ...), custom_call_target="tpu_custom_call" | custom-call | tf_op jit(solution)/shard_map/pallas_call | solution.py:762
  4.4 14.4 %all-to-all-start = ((f32[256,1,128]{2,1,0:T(1,128)}), f32[256,1,128]{2,1,0:T(1,128)S(1)}, u32[]{:S(2)}, u32[]{:S(2)}) async-start(f32[256,1,128]{2,1,0:T(1,128)} %bitcast.5), calls=%async_computation | async-start | bytes 262144 | tf_op jit(solution)/shard_map/all_to_all | solution.py:800
  18.9 0.2 collective-permute-start
  19.0 1.5 %collective-permute-start.2 = (f32[96,128]{1,0:T(8,128)S(1)}, f32[96,128]{1,0:T(8,128)S(1)}, u32[]{:S(2)}, u32[]{:S(2)}) collective-permute-start(f32[96,128]{1,0:T(8,128)S(1)} %get-tuple-element.52), channel_id=1, source_target_pairs={{0,4},{4,8},{8,12},{12,0},{1,5},{5,9},{9,13},{13,1},{2,6},{6,10},{... | collective-permute-start | bytes 147464 | tf_op jit(solution)/shard_map/ppermute | solution.py:730
  20.5 1.8 %collective-permute-start.3 = (f32[96,128]{1,0:T(8,128)S(1)}, f32[96,128]{1,0:T(8,128)S(1)}, u32[]{:S(2)}, u32[]{:S(2)}) collective-permute-start(f32[96,128]{1,0:T(8,128)S(1)} %get-tuple-element.53), channel_id=1, source_target_pairs={{4,0},{8,4},{12,8},{0,12},{5,1},{9,5},{13,9},{1,13},{6,2},{10,6},{... | collective-permute-start | bytes 147464 | tf_op jit(solution)/shard_map/ppermute | solution.py:730
  22.3 2.0 %collective-permute-start.4 = (f32[6,32,128]{2,1,0:T(8,128)S(1)}, f32[6,32,128]{2,1,0:T(8,128)S(1)}, u32[]{:S(2)}, u32[]{:S(2)}) collective-permute-start(f32[6,32,128]{2,1,0:T(8,128)S(1)} %get-tuple-element.54), channel_id=1, source_target_pairs={{0,1},{1,2},{2,3},{3,0},{4,5},{5,6},{6,7},{7,4},{8,9},{9,10},{10,1... | collective-permute-start | bytes 294920 | tf_op jit(solution)/shard_map/ppermute | solution.py:730
  24.3 0.0 collective-permute-start.5
  24.3 0.9 %shard_map.147 = (f32[3,16,32,128]{3,2,1,0:T(8,128)S(1)}, f32[3,16,32,128]{3,2,1,0:T(8,128)S(1)}) custom-call(f32[7,16,32,128]{3,2,1,0:T(8,128)S(1)} %get-tuple-element.42.fld_ref), custom_call_target="tpu_custom_call" | custom-call | flops 1073741824 | bytes 16777216 | tf_op jit(solution)/shard_map/pallas_call | solution.py:762
  25.2 0.0 copy-start.1
  25.2 0.9 %copy-done.1 = f32[3,16,32,128]{3,2,1,0:T(8,128)} copy-done((f32[3,16,32,128]{3,2,1,0:T(8,128)}, f32[3,16,32,128]{3,2,1,0:T(8,128)S(1)}, u32[]{:S(2)}) %copy-start.1) | copy-done | bytes 786456
  26.1 0.0 collective-permute-done.xlo_ref
  26.1 3.1 %collective-permute-start.1 = (f32[2,32,128]{2,1,0:T(8,128)S(1)}, f32[2,32,128]{2,1,0:T(8,128)S(1)}, u32[]{:S(2)}, u32[]{:S(2)}) collective-permute-start(f32[2,32,128]{2,1,0:T(8,128)S(1)} %get-tuple-element.51), channel_id=1, source_target_pairs={{16,0},{32,16},{48,32},{64,48},{80,64},{96,80},{112,96},{128,112},... | collective-permute-start | bytes 98312 | tf_op jit(solution)/shard_map/ppermute | solution.py:806
  29.2 1.3 %all-to-all-done = f32[256,1,128]{2,1,0:T(1,128)S(1)} async-done(((f32[256,1,128]{2,1,0:T(1,128)}), f32[256,1,128]{2,1,0:T(1,128)S(1)}, u32[]{:S(2)}, u32[]{:S(2)}) %all-to-all-start) | async-done | bytes 131104 | tf_op jit(solution)/shard_map/all_to_all | solution.py:800
  30.5 0.0 copy-start.2
  30.5 1.6 %shard_map.148.field_ref = f32[3,16,32,128]{3,2,1,0:T(8,128)S(1)} custom-call(s32[2,512]{1,0:T(2,128)S(1)} %get-tuple-element.44.index_ref, f32[1,512]{1,0:T(1,128)S(1)} %get-tuple-element.45.scale_ref, s32[8,128]{1,0:T(8,128)S(1)} %get-tuple-element.46.owner_ref, f32[256,128]{1,0:T(8,128)S(1)} %bitcast.9), custom_call_target="tpu_custom_call" | custom-call | flops 1073741824 | bytes 16777216 | tf_op jit(solution)/shard_map/pallas_call | solution.py:762
  32.1 0.0 collective-permute-done.2.ylo_ref
  32.1 0.0 collective-permute-done.3.yhi_ref
  32.1 0.0 collective-permute-done.1.xhi_ref
  32.1 0.0 collective-permute-done.4.zlo_ref
  32.1 0.0 collective-permute-done.5.zhi_ref
  32.2 1.2 %shard_map.149 = (f32[3,16,32,128]{3,2,1,0:T(8,128)S(1)}, f32[18,48,128]{2,1,0:T(8,128)S(1)}, f32[18,48,128]{2,1,0:T(8,128)S(1)}, f32[3,48,128]{2,1,0:T(8,128)S(1)}, f32[3,48,128]{2,1,0:T(8,128)S(1)}) custom-call(f32[3,16,32,128]{3,2,1,0:T(8,128)S(1)} %get-tuple-element.43.base_ref, f32[3,16,32,128]{3,2,1,0:T(8,128)S(1)} %shard_map.148.field_ref, ...), custom_call_target="tpu_custom_call" | custom-call | tf_op jit(solution)/shard_map/pallas_call | solution.py:762
  33.4 0.0 collective-permute-start.6
  33.4 2.9 %collective-permute-start.7 = (f32[3,48,128]{2,1,0:T(8,128)S(1)}, f32[3,48,128]{2,1,0:T(8,128)S(1)}, u32[]{:S(2)}, u32[]{:S(2)}) collective-permute-start(f32[3,48,128]{2,1,0:T(8,128)S(1)} %get-tuple-element.59), channel_id=1, source_target_pairs={{16,0},{32,16},{48,32},{64,48},{80,64},{96,80},{112,96},{128,112},... | collective-permute-start | bytes 221192 | tf_op jit(solution)/shard_map/ppermute | solution.py:730
  36.4 2.0 %collective-permute-done.6.lo_ref = f32[3,48,128]{2,1,0:T(8,128)S(1)} collective-permute-done((f32[3,48,128]{2,1,0:T(8,128)S(1)}, f32[3,48,128]{2,1,0:T(8,128)S(1)}, u32[]{:S(2)}, u32[]{:S(2)}) %collective-permute-start.6) | collective-permute-done | bytes 73760 | tf_op jit(solution)/shard_map/ppermute | solution.py:730
  38.4 0.0 collective-permute-done.7.hi_ref
  38.4 0.5 shard_map.150
  38.8 0.6 %collective-permute-start.8 = (f32[27,8,128]{2,1,0:T(8,128)S(1)}, f32[27,8,128]{2,1,0:T(8,128)S(1)}, u32[]{:S(2)}, u32[]{:S(2)}) collective-permute-start(f32[27,8,128]{2,1,0:T(8,128)S(1)} %get-tuple-element.62), channel_id=1, source_target_pairs={{0,4},{4,8},{8,12},{12,0},{1,5},{5,9},{9,13},{13,1},{2,6},{6,10},{... | collective-permute-start | bytes 331784 | tf_op jit(solution)/shard_map/ppermute | solution.py:730
  39.5 2.7 %collective-permute-start.9 = (f32[27,8,128]{2,1,0:T(8,128)S(1)}, f32[27,8,128]{2,1,0:T(8,128)S(1)}, u32[]{:S(2)}, u32[]{:S(2)}) collective-permute-start(f32[27,8,128]{2,1,0:T(8,128)S(1)} %get-tuple-element.66), channel_id=1, source_target_pairs={{4,0},{8,4},{12,8},{0,12},{5,1},{9,5},{13,9},{1,13},{6,2},{10,6},{... | collective-permute-start | bytes 331784 | tf_op jit(solution)/shard_map/ppermute | solution.py:730
  42.2 1.8 %collective-permute-start.10 = (f32[10,32,128]{2,1,0:T(8,128)S(1)}, f32[10,32,128]{2,1,0:T(8,128)S(1)}, u32[]{:S(2)}, u32[]{:S(2)}) collective-permute-start(f32[10,32,128]{2,1,0:T(8,128)S(1)} %get-tuple-element.69), channel_id=1, source_target_pairs={{0,1},{1,2},{2,3},{3,0},{4,5},{5,6},{6,7},{7,4},{8,9},{9,10},{10,1... | collective-permute-start | bytes 491528 | tf_op jit(solution)/shard_map/ppermute | solution.py:730
  44.0 0.2 collective-permute-start.11
  44.2 0.0 copy-done.2
  44.2 2.7 %shard_map.151 = (f32[3,16,32,128]{3,2,1,0:T(8,128)}, f32[1,4]{1,0:T(1,128)}, f32[2,4]{1,0:T(2,128)}) custom-call(f32[4]{0:T(128)} %yaw_ref.3, f32[4]{0:T(128)} %ct_ref.3, f32[3,16,32,128]{3,2,1,0:T(8,128)S(1)} %copy-done.2, f32[3,16,32,128]{3,2,1,0:T(8,128)S(1)} %shard_map.148.field_ref, f32[7,16,32,128]{3,2,1,0:T(8,128)S(1)} %get-tuple-element.42.fld_ref, ...), custom_call_target="tpu_custom_call" | custom-call | flops 1073741824 | bytes 16777216 | tf_op jit(solution)/shard_map/pallas_call | solution.py:762
  46.9 0.0 copy-start
  46.9 0.0 collective-permute-done.8.lo_ref
  46.9 0.0 collective-permute-done.9.hi_ref
  46.9 0.2 shard_map.152
  47.1 3.1 %collective-permute-start.12 = (f32[14,8,128]{2,1,0:T(8,128)S(1)}, f32[14,8,128]{2,1,0:T(8,128)S(1)}, u32[]{:S(2)}, u32[]{:S(2)}) collective-permute-start(f32[14,8,128]{2,1,0:T(8,128)S(1)} %get-tuple-element.71), channel_id=1, source_target_pairs={{0,1},{1,2},{2,3},{3,0},{4,5},{5,6},{6,7},{7,4},{8,9},{9,10},{10,1... | collective-permute-start | bytes 172040 | tf_op jit(solution)/shard_map/ppermute | solution.py:730
  50.2 0.0 collective-permute-start.13
  50.2 1.2 %shard_map.153.pre_ref = f32[56,2,64,128]{3,2,1,0:T(8,128)S(1)} custom-call(f32[18,48,128]{2,1,0:T(8,128)S(1)} %get-tuple-element.67.dm_ref, f32[18,48,128]{2,1,0:T(8,128)S(1)} %get-tuple-element.68.ds_ref), custom_call_target="tpu_custom_call" | custom-call | flops 1073741824 | bytes 16777216 | tf_op jit(solution)/shard_map/pallas_call | solution.py:762
  51.4 0.0 collective-permute-done.10.lo_ref
  51.4 0.0 collective-permute-done.11.hi_ref
  51.4 0.6 %collective-permute-done.12.late_lo_ref = f32[14,8,128]{2,1,0:T(8,128)S(1)} collective-permute-done((f32[14,8,128]{2,1,0:T(8,128)S(1)}, f32[14,8,128]{2,1,0:T(8,128)S(1)}, u32[]{:S(2)}, u32[]{:S(2)}) %collective-permute-start.12) | collective-permute-done | bytes 57376 | tf_op jit(solution)/shard_map/ppermute | solution.py:730
  52.1 3.6 %collective-permute-done.13.late_hi_ref = f32[14,8,128]{2,1,0:T(8,128)S(1)} collective-permute-done((f32[14,8,128]{2,1,0:T(8,128)S(1)}, f32[14,8,128]{2,1,0:T(8,128)S(1)}, u32[]{:S(2)}, u32[]{:S(2)}) %collective-permute-start.13) | collective-permute-done | bytes 57376 | tf_op jit(solution)/shard_map/ppermute | solution.py:730
  55.6 0.0 copy-done
  55.6 4.4 %shard_map.154 = (f32[3,16,32,128]{3,2,1,0:T(8,128)}, f32[16,32,128]{2,1,0:T(8,128)}) custom-call(f32[18,48,128]{2,1,0:T(8,128)S(1)} %get-tuple-element.67.dm_ref, f32[18,48,128]{2,1,0:T(8,128)S(1)} %get-tuple-element.68.ds_ref, f32[56,2,64,128]{3,2,1,0:T(8,128)S(1)} %shard_map.153.pre_ref, f32[10,32,128]{2,1,0:T(8,128)S(1)} %collective-permute-done.10.lo_ref, ...), custom_call_target="tpu_custom_call" | custom-call | tf_op jit(solution)/shard_map/pallas_call | solution.py:762
Async XLA Ops:
  4.4 26.1 %all-to-all-start = ((f32[256,1,128]{2,1,0:T(1,128)}), f32[256,1,128]{2,1,0:T(1,128)S(1)}, u32[]{:S(2)}, u32[]{:S(2)}) async-start(f32[256,1,128]{2,1,0:T(1,128)} %bitcast.5), calls=%async_computation | async-start | bytes 262144 | tf_op jit(solution)/shard_map/all_to_all | solution.py:800
  18.9 7.3 %collective-permute-start = (f32[2,32,128]{2,1,0:T(8,128)S(1)}, f32[2,32,128]{2,1,0:T(8,128)S(1)}, u32[]{:S(2)}, u32[]{:S(2)}) collective-permute-start(f32[2,32,128]{2,1,0:T(8,128)S(1)} %get-tuple-element.48), channel_id=1, source_target_pairs={{0,16},{16,32},{32,48},{48,64},{64,80},{80,96},{96,112},{112,128},... | collective-permute-start | bytes 98312 | tf_op jit(solution)/shard_map/ppermute | solution.py:804
  19.0 13.1 %collective-permute-start.2 = (f32[96,128]{1,0:T(8,128)S(1)}, f32[96,128]{1,0:T(8,128)S(1)}, u32[]{:S(2)}, u32[]{:S(2)}) collective-permute-start(f32[96,128]{1,0:T(8,128)S(1)} %get-tuple-element.52), channel_id=1, source_target_pairs={{0,4},{4,8},{8,12},{12,0},{1,5},{5,9},{9,13},{13,1},{2,6},{6,10},{... | collective-permute-start | bytes 147464 | tf_op jit(solution)/shard_map/ppermute | solution.py:730
  20.5 11.6 %collective-permute-start.3 = (f32[96,128]{1,0:T(8,128)S(1)}, f32[96,128]{1,0:T(8,128)S(1)}, u32[]{:S(2)}, u32[]{:S(2)}) collective-permute-start(f32[96,128]{1,0:T(8,128)S(1)} %get-tuple-element.53), channel_id=1, source_target_pairs={{4,0},{8,4},{12,8},{0,12},{5,1},{9,5},{13,9},{1,13},{6,2},{10,6},{... | collective-permute-start | bytes 147464 | tf_op jit(solution)/shard_map/ppermute | solution.py:730
  22.3 9.9 %collective-permute-start.4 = (f32[6,32,128]{2,1,0:T(8,128)S(1)}, f32[6,32,128]{2,1,0:T(8,128)S(1)}, u32[]{:S(2)}, u32[]{:S(2)}) collective-permute-start(f32[6,32,128]{2,1,0:T(8,128)S(1)} %get-tuple-element.54), channel_id=1, source_target_pairs={{0,1},{1,2},{2,3},{3,0},{4,5},{5,6},{6,7},{7,4},{8,9},{9,10},{10,1... | collective-permute-start | bytes 294920 | tf_op jit(solution)/shard_map/ppermute | solution.py:730
  24.3 7.9 %collective-permute-start.5 = (f32[6,32,128]{2,1,0:T(8,128)S(1)}, f32[6,32,128]{2,1,0:T(8,128)S(1)}, u32[]{:S(2)}, u32[]{:S(2)}) collective-permute-start(f32[6,32,128]{2,1,0:T(8,128)S(1)} %get-tuple-element.55), channel_id=1, source_target_pairs={{1,0},{2,1},{3,2},{0,3},{5,4},{6,5},{7,6},{4,7},{9,8},{10,9},{11,1... | collective-permute-start | bytes 294920 | tf_op jit(solution)/shard_map/ppermute | solution.py:730
  25.2 0.9 %copy-start.1 = (f32[3,16,32,128]{3,2,1,0:T(8,128)}, f32[3,16,32,128]{3,2,1,0:T(8,128)S(1)}, u32[]{:S(2)}) copy-start(f32[3,16,32,128]{3,2,1,0:T(8,128)S(1)} %get-tuple-element.63.base_ref) | copy-start | bytes 2359300
  26.1 6.0 %collective-permute-start.1 = (f32[2,32,128]{2,1,0:T(8,128)S(1)}, f32[2,32,128]{2,1,0:T(8,128)S(1)}, u32[]{:S(2)}, u32[]{:S(2)}) collective-permute-start(f32[2,32,128]{2,1,0:T(8,128)S(1)} %get-tuple-element.51), channel_id=1, source_target_pairs={{16,0},{32,16},{48,32},{64,48},{80,64},{96,80},{112,96},{128,112},... | collective-permute-start | bytes 98312 | tf_op jit(solution)/shard_map/ppermute | solution.py:806
  30.5 13.7 %copy-start.2 = (f32[3,16,32,128]{3,2,1,0:T(8,128)S(1)}, f32[3,16,32,128]{3,2,1,0:T(8,128)}, u32[]{:S(2)}) copy-start(f32[3,16,32,128]{3,2,1,0:T(8,128)} %copy-done.1) | copy-start | bytes 2359300
  33.4 5.0 %collective-permute-start.6 = (f32[3,48,128]{2,1,0:T(8,128)S(1)}, f32[3,48,128]{2,1,0:T(8,128)S(1)}, u32[]{:S(2)}, u32[]{:S(2)}) collective-permute-start(f32[3,48,128]{2,1,0:T(8,128)S(1)} %get-tuple-element.58), channel_id=1, source_target_pairs={{0,16},{16,32},{32,48},{48,64},{64,80},{80,96},{96,112},{112,128},... | collective-permute-start | bytes 221192 | tf_op jit(solution)/shard_map/ppermute | solution.py:730
  33.4 5.0 %collective-permute-start.7 = (f32[3,48,128]{2,1,0:T(8,128)S(1)}, f32[3,48,128]{2,1,0:T(8,128)S(1)}, u32[]{:S(2)}, u32[]{:S(2)}) collective-permute-start(f32[3,48,128]{2,1,0:T(8,128)S(1)} %get-tuple-element.59), channel_id=1, source_target_pairs={{16,0},{32,16},{48,32},{64,48},{80,64},{96,80},{112,96},{128,112},... | collective-permute-start | bytes 221192 | tf_op jit(solution)/shard_map/ppermute | solution.py:730
  38.8 8.0 %collective-permute-start.8 = (f32[27,8,128]{2,1,0:T(8,128)S(1)}, f32[27,8,128]{2,1,0:T(8,128)S(1)}, u32[]{:S(2)}, u32[]{:S(2)}) collective-permute-start(f32[27,8,128]{2,1,0:T(8,128)S(1)} %get-tuple-element.62), channel_id=1, source_target_pairs={{0,4},{4,8},{8,12},{12,0},{1,5},{5,9},{9,13},{13,1},{2,6},{6,10},{... | collective-permute-start | bytes 331784 | tf_op jit(solution)/shard_map/ppermute | solution.py:730
  39.5 7.4 %collective-permute-start.9 = (f32[27,8,128]{2,1,0:T(8,128)S(1)}, f32[27,8,128]{2,1,0:T(8,128)S(1)}, u32[]{:S(2)}, u32[]{:S(2)}) collective-permute-start(f32[27,8,128]{2,1,0:T(8,128)S(1)} %get-tuple-element.66), channel_id=1, source_target_pairs={{4,0},{8,4},{12,8},{0,12},{5,1},{9,5},{13,9},{1,13},{6,2},{10,6},{... | collective-permute-start | bytes 331784 | tf_op jit(solution)/shard_map/ppermute | solution.py:730
  42.2 9.3 %collective-permute-start.10 = (f32[10,32,128]{2,1,0:T(8,128)S(1)}, f32[10,32,128]{2,1,0:T(8,128)S(1)}, u32[]{:S(2)}, u32[]{:S(2)}) collective-permute-start(f32[10,32,128]{2,1,0:T(8,128)S(1)} %get-tuple-element.69), channel_id=1, source_target_pairs={{0,1},{1,2},{2,3},{3,0},{4,5},{5,6},{6,7},{7,4},{8,9},{9,10},{10,1... | collective-permute-start | bytes 491528 | tf_op jit(solution)/shard_map/ppermute | solution.py:730
  44.0 7.5 %collective-permute-start.11 = (f32[10,32,128]{2,1,0:T(8,128)S(1)}, f32[10,32,128]{2,1,0:T(8,128)S(1)}, u32[]{:S(2)}, u32[]{:S(2)}) collective-permute-start(f32[10,32,128]{2,1,0:T(8,128)S(1)} %get-tuple-element.70), channel_id=1, source_target_pairs={{1,0},{2,1},{3,2},{0,3},{5,4},{6,5},{7,6},{4,7},{9,8},{10,9},{11,1... | collective-permute-start | bytes 491528 | tf_op jit(solution)/shard_map/ppermute | solution.py:730
  46.9 8.7 %copy-start = (f32[16,32,128]{2,1,0:T(8,128)S(1)}, f32[16,32,128]{2,1,0:T(8,128)}, u32[]{:S(2)}) copy-start(f32[16,32,128]{2,1,0:T(8,128)} %pres_ref.1) | copy-start | bytes 786436
  47.1 4.9 %collective-permute-start.12 = (f32[14,8,128]{2,1,0:T(8,128)S(1)}, f32[14,8,128]{2,1,0:T(8,128)S(1)}, u32[]{:S(2)}, u32[]{:S(2)}) collective-permute-start(f32[14,8,128]{2,1,0:T(8,128)S(1)} %get-tuple-element.71), channel_id=1, source_target_pairs={{0,1},{1,2},{2,3},{3,0},{4,5},{5,6},{6,7},{7,4},{8,9},{9,10},{10,1... | collective-permute-start | bytes 172040 | tf_op jit(solution)/shard_map/ppermute | solution.py:730
  50.2 5.4 %collective-permute-start.13 = (f32[14,8,128]{2,1,0:T(8,128)S(1)}, f32[14,8,128]{2,1,0:T(8,128)S(1)}, u32[]{:S(2)}, u32[]{:S(2)}) collective-permute-start(f32[14,8,128]{2,1,0:T(8,128)S(1)} %get-tuple-element.72), channel_id=1, source_target_pairs={{1,0},{2,1},{3,2},{0,3},{5,4},{6,5},{7,6},{4,7},{9,8},{10,9},{11,1... | collective-permute-start | bytes 172040 | tf_op jit(solution)/shard_map/ppermute | solution.py:730

commit v3 on v2

--- a/solution.py
+++ b/solution.py
@@ -285,27 +285,37 @@
         field_ref[c] = dots([rows], pieces(spread, 2), NT).reshape(CZ, CY, CX)
 
 
-def stencil_kernel(pos_ref, fld_ref, pred_ref, dual_ref):
+def stencil(fld_ref, f, out, comp):
     lane = iota((H, CX), 1)
     sub = iota((H, CX), 0)
     zero = jnp.zeros((H, CX), F32)
     for t in range(CY // H):
         at = tile_rows(t)
-        for f in range(6):
-            out, comp = (pred_ref, f) if f < 3 else (dual_ref, f - 3)
-            below, tile = zero, fld_ref[f, 0, at]
-            for z in range(CZ):
-                above = fld_ref[f, z + 1, at] if z < CZ - 1 else zero
-                south, north = south_of(fld_ref, (f, z), t, sub), north_of(fld_ref, (f, z), t, sub)
-                west = jnp.where(lane == 0, 0.0, roll(tile, 1, 1))
-                east = jnp.where(lane == CX - 1, 0.0, roll(tile, -1, 1))
-                lap = (above + below) + (north + south) + (east + west) - 6.0 * tile
-                rate = fld_ref[6, z, at] * lap + (west - tile if f < 3 else east - tile)
-                out[comp, z, at] = tile + DT * rate
-                below, tile = tile, above
-
-
-def add_faces(f, first, out, given, field_ref, fld_ref, bounds, xlo_ref, xhi_ref, ylo_ref, yhi_ref, zlo_ref, zhi_ref):
+        below, tile = zero, fld_ref[f, 0, at]
+        for z in range(CZ):
+            above = fld_ref[f, z + 1, at] if z < CZ - 1 else zero
+            south, north = south_of(fld_ref, (f, z), t, sub), north_of(fld_ref, (f, z), t, sub)
+            west = jnp.where(lane == 0, 0.0, roll(tile, 1, 1))
+            east = jnp.where(lane == CX - 1, 0.0, roll(tile, -1, 1))
+            lap = (above + below) + (north + south) + (east + west) - 6.0 * tile
+            rate = fld_ref[6, z, at] * lap + (west - tile if f < 3 else east - tile)
+            out[comp, z, at] = tile + DT * rate
+            below, tile = tile, above
+
+
+def stencil_kernel(pos_ref, fld_ref, pred_ref):
+    for f in range(3):
+        stencil(fld_ref, f, pred_ref, f)
+
+
+def merge_faces(face_ref, half, xlo_ref, xhi_ref, bounds):
+    odd = jnp.bitwise_and(iota((H, CX), 1), 1) == 1
+    for t in range(CY // H):
+        at = tile_rows(t)
+        face_ref[at] = jnp.where(odd, xlo_ref[half, at] * bounds[0], roll(xhi_ref[half, at] * bounds[1], -2, 1))
+
+
+def add_faces(f, first, out, given, field_ref, fld_ref, bounds, face_ref, ylo_ref, yhi_ref, zlo_ref, zhi_ref):
     lo_x, hi_x, lo_y, hi_y, lo_z, hi_z = bounds
     lane = iota((H, CX), 1)
     sub = iota((H, CX), 0)
@@ -313,11 +323,9 @@
     comp = f - first
     for t in range(CY // H):
         at = tile_rows(t)
-        odd = jnp.bitwise_and(lane, 1) == 1
-        face = jnp.where(odd, xlo_ref[f // 3, at] * lo_x, roll(xhi_ref[f // 3, at] * hi_x, -2, 1))
         for z in range(CZ):
             spot = f * CZ + z
-            moved = roll(face, -(2 * (spot % (3 * CZ)) + 1), 1)
+            moved = roll(face_ref[at], -(2 * (spot % (3 * CZ)) + 1), 1)
             west = jnp.where(lane == 0, moved, 0.0)
             east = jnp.where(lane == CX - 1, moved, 0.0)
             lap = west + east
@@ -343,11 +351,12 @@
 
 def flow_kernel(
     dims, pos_ref, base_ref, field_ref, fld_ref, xlo_ref, xhi_ref, ylo_ref, yhi_ref, zlo_ref, zhi_ref,
-    pred_ref, dm_ref, ds_ref, xr_ref, xl_ref,
+    pred_ref, dm_ref, ds_ref, xr_ref, xl_ref, face_ref,
 ):
     bounds = edges(pos_ref, dims)
+    merge_faces(face_ref, 0, xlo_ref, xhi_ref, bounds)
     for f in range(3):
-        add_faces(f, 0, pred_ref, base_ref, field_ref, fld_ref, bounds, xlo_ref, xhi_ref, ylo_ref, yhi_ref, zlo_ref, zhi_ref)
+        add_faces(f, 0, pred_ref, base_ref, field_ref, fld_ref, bounds, face_ref, ylo_ref, yhi_ref, zlo_ref, zhi_ref)
     lane = iota((H, CX), 1)
     sub = iota((H, CX), 0)
     zero = jnp.zeros((H, CX), F32)
@@ -395,18 +404,23 @@
 
 
 def dual_kernel(
-    dims, pos_ref, yaw_ref, ct_ref, base_ref, field_ref, fld_ref, got_ref, xlo_ref, xhi_ref, ylo_ref, yhi_ref, zlo_ref, zhi_ref,
-    dual_out, yaw_out, pos_out, dual_ref, sems,
+    dims, pos_ref, field_ref, fld_ref, xlo_ref, xhi_ref, ylo_ref, yhi_ref, zlo_ref, zhi_ref,
+    dual_out, dual_ref, face_ref, sems,
 ):
     bounds = edges(pos_ref, dims)
+    merge_faces(face_ref, 1, xlo_ref, xhi_ref, bounds)
     copies = []
     for f in range(3, 6):
-        add_faces(f, 3, dual_ref, base_ref, field_ref, fld_ref, bounds, xlo_ref, xhi_ref, ylo_ref, yhi_ref, zlo_ref, zhi_ref)
+        stencil(fld_ref, f, dual_ref, f - 3)
+        add_faces(f, 3, dual_ref, dual_ref, field_ref, fld_ref, bounds, face_ref, ylo_ref, yhi_ref, zlo_ref, zhi_ref)
         copies.append(pltpu.make_async_copy(dual_ref.at[f - 3], dual_out.at[f - 3], sems.at[f - 3]))
         copies[-1].start()
-    owner_outputs(got_ref[...], yaw_ref, ct_ref, yaw_out, pos_out)
     for copy in copies:
         copy.wait()
+
+
+def owner_kernel(pos_ref, yaw_ref, ct_ref, got_ref, yaw_out, pos_out):
+    owner_outputs(got_ref[...], yaw_ref, ct_ref, yaw_out, pos_out)
 
 
 def x_kernel(
@@ -806,9 +820,9 @@
     xhi = lax.ppermute(xl, "gx", [((i + 1) % count, i) for i in range(count)])
     faces = (xlo, xhi, ylo, yhi, zlo, zhi)
 
-    pred_base, dual_base = call(
-        stencil_kernel, (), (fields,), (in_vmem(3, CZ, CY, CX), in_vmem(3, CZ, CY, CX)), cost=1 << 30
-    )
+    pred_base = call(
+        stencil_kernel, (), (fields,), (in_vmem(3, CZ, CY, CX),), cost=1 << 30
+    )[0]
     force = call(
         functools.partial(force_kernel, dims), (), (index, scale, table, got), (shape(3, CZ, CY, CX),), cost=1 << 30
     )[0]
@@ -817,17 +831,13 @@
         (),
         (pred_base, force, fields) + faces,
         (shape(3, CZ, CY, CX), shape(SZ, EY, CX), shape(SZ, EY, CX), shape(3, EY, CX), shape(3, EY, CX)),
-    )
-    adjoint_next, yaw_grad, position_grad = call(
-        functools.partial(dual_kernel, dims),
-        (in_hbm(yaw), in_hbm(thrust_coef)),
-        (dual_base, force, fields, got) + faces,
-        (shape(3, CZ, CY, CX), shape(1, 4), shape(2, 4)),
-        (pltpu.VMEM((3, CZ, CY, CX), F32), pltpu.SemaphoreType.DMA((3,))),
-        out_specs=[ANY, VMEM, VMEM],
-        cost=1 << 30,
+        (pltpu.VMEM((CY, CX), F32),),
     )
     lo, hi = swap(xr, xl, "gx")
+    yaw_grad, position_grad = call(
+        owner_kernel, (in_hbm(yaw), in_hbm(thrust_coef)), (got,), (shape(1, 4), shape(2, 4)), cost=1 << 29
+    )
+    lo, yaw_grad = lax.optimization_barrier((lo, yaw_grad))
     dm, ds, up, down, above, below = call(
         functools.partial(x_kernel, dims), (), (dm, ds, lo, hi),
         (
@@ -837,7 +847,6 @@
     )
     lo, hi = swap(up, down, "gy")
     early_lo, early_hi = swap(above, below, "gz")
-    lo, yaw_grad = lax.optimization_barrier((lo, yaw_grad))
     dm, ds, above, below = call(
         functools.partial(y_kernel, dims), (), (dm, ds, lo, hi),
         (shape(SZ, EY, CX), shape(SZ, EY, CX), shape(LATE, H, CX), shape(LATE, H, CX)),
@@ -846,6 +855,17 @@
     pre = call(
         functools.partial(inner_kernel, dims), (), (dm, ds), (shape(PRE, 2, EY + 2 * PADR, CX),), cost=1 << 30
     )[0]
+    pre, force = lax.optimization_barrier((pre, force))
+    adjoint_next = call(
+        functools.partial(dual_kernel, dims),
+        (),
+        (force, fields) + faces,
+        (shape(3, CZ, CY, CX),),
+        (pltpu.VMEM((3, CZ, CY, CX), F32), pltpu.VMEM((CY, CX), F32), pltpu.SemaphoreType.DMA((3,))),
+        out_specs=[ANY],
+        cost=1 << 30,
+    )[0]
+    predicted, adjoint_next = lax.optimization_barrier((predicted, adjoint_next))
     velocity_next, pressure_next = call(
         functools.partial(sweep_kernel, dims), (), (dm, ds, pre, early_lo, early_hi, late_lo, late_hi, predicted, pressure),
         (shape(3, CZ, CY, CX), shape(CZ, CY, CX)),

time: 60.4 us -> 57.5 us (0.952)
  starting transfers between devices: 34.4 us -> 32.1 us
  local copies, waits for them, and re-layouts: 0.88 us -> 0.01 us
  Pallas kernels: 16.5 us -> 15.8 us
  waiting for transfers between devices: 7.5 us -> 8.2 us
    ppermute x12, waiting for transfers between devices: 6.22 us -> 4.32 us  [swap(): return (lax.ppermute(up, axis, forward), lax.ppermute(down, axis, backward))]
    all_to_all x1, waiting for transfers between devices: 1.28 us -> 2.6 us  [shards(): got = lax.all_to_all(payload, axes, 0, 0, tiled=True)]
    ppermute x1, waiting for transfers between devices: 0.01 us -> 1.27 us  [shards(): xlo = lax.ppermute(xr, 'gx', [(i, (i + 1) % count) for i in range(count)])]
    ppermute x1, starting transfers between devices: 3.13 us -> 1.87 us  [shards(): xhi = lax.ppermute(xl, 'gx', [((i + 1) % count, i) for i in range(count)])]
    ppermute x12, starting transfers between devices: 16.7 us -> 15.7 us  [swap(): return (lax.ppermute(up, axis, forward), lax.ppermute(down, axis, backward))]
    unnamed x6 -> x2, local copies, waits for them, and re-layouts: 0.88 us -> 0.01 us
    pallas_call x9 -> x10, Pallas kernels: 16.5 us -> 15.8 us  [call(): pl.pallas_call(functools.partial(kernel, Place()), out_shape=outs, in_spe...]
  transfers between devices with their start and end apart: 15 -> 15, of which waited for: 4 -> 6; matrix products, arithmetic and copies ran while one was open for 0% -> 0% of each run, Pallas kernels for 11% -> 11%
where the time goes in v3:
time: 57.5 us; the launch traced here: 57 us
  starting transfers between devices  32.1 us (56%)
  Pallas kernels  15.8 us (27%)
  waiting for transfers between devices  8.2 us (14%)
  between operations  0.91 us (2%)
    pallas_call x10, Pallas kernels, call(): pl.pallas_call(functools.partial(kernel, Place()), out_shape=outs, in_spe...  15.8 us
    ppermute x12, starting transfers between devices, swap(): return (lax.ppermute(up, axis, forward), lax.ppermute(down, axis, backward))  15.7 us
    all_to_all x1, starting transfers between devices, shards(): got = lax.all_to_all(payload, axes, 0, 0, tiled=True)  14.4 us
    ppermute x12, waiting for transfers between devices, swap(): return (lax.ppermute(up, axis, forward), lax.ppermute(down, axis, backward))  4.32 us
    all_to_all x1, waiting for transfers between devices, shards(): got = lax.all_to_all(payload, axes, 0, 0, tiled=True)  2.6 us
    ppermute x1, starting transfers between devices, shards(): xhi = lax.ppermute(xl, 'gx', [((i + 1) % count, i) for i in range(count)])  1.87 us
    ppermute x1, waiting for transfers between devices, shards(): xlo = lax.ppermute(xr, 'gx', [(i, (i + 1) % count) for i in range(count)])  1.27 us
  transfers between devices with their start and end apart: 15, of which 6 were waited for; matrix products, arithmetic and copies ran while one was open for 0% of the time, Pallas kernels for 11%

profile of v3, /device:TPU:24, one launch (start us, length us, event | category | flops | bytes accessed | tf_op | source)
XLA Modules:
  0.0 57.0 jit_solution(9899149302171030797)
XLA Ops:
  0.6 3.8 %shard_map.146 = (f32[256,128]{1,0:T(8,128)}, f32[2,32,128]{2,1,0:T(8,128)S(1)}, f32[2,32,128]{2,1,0:T(8,128)S(1)}, f32[96,128]{1,0:T(8,128)S(1)}, f32[96,128]{1...) custom-call(f32[4]{0:T(128)} %yaw_ref.3, ...), custom_call_target="tpu_custom_call" | custom-call | tf_op jit(solution)/shard_map/pallas_call | solution.py:776
  4.4 14.4 %all-to-all-start = ((f32[256,1,128]{2,1,0:T(1,128)}), f32[256,1,128]{2,1,0:T(1,128)S(1)}, u32[]{:S(2)}, u32[]{:S(2)}) async-start(f32[256,1,128]{2,1,0:T(1,128)} %bitcast.5), calls=%async_computation | async-start | bytes 262144 | tf_op jit(solution)/shard_map/all_to_all | solution.py:814
  18.9 0.2 collective-permute-start
  19.0 1.5 %collective-permute-start.2 = (f32[96,128]{1,0:T(8,128)S(1)}, f32[96,128]{1,0:T(8,128)S(1)}, u32[]{:S(2)}, u32[]{:S(2)}) collective-permute-start(f32[96,128]{1,0:T(8,128)S(1)} %get-tuple-element.52), channel_id=1, source_target_pairs={{0,4},{4,8},{8,12},{12,0},{1,5},{5,9},{9,13},{13,1},{2,6},{6,10},{... | collective-permute-start | bytes 147464 | tf_op jit(solution)/shard_map/ppermute | solution.py:744
  20.5 1.8 %collective-permute-start.3 = (f32[96,128]{1,0:T(8,128)S(1)}, f32[96,128]{1,0:T(8,128)S(1)}, u32[]{:S(2)}, u32[]{:S(2)}) collective-permute-start(f32[96,128]{1,0:T(8,128)S(1)} %get-tuple-element.53), channel_id=1, source_target_pairs={{4,0},{8,4},{12,8},{0,12},{5,1},{9,5},{13,9},{1,13},{6,2},{10,6},{... | collective-permute-start | bytes 147464 | tf_op jit(solution)/shard_map/ppermute | solution.py:744
  22.3 2.0 %collective-permute-start.4 = (f32[6,32,128]{2,1,0:T(8,128)S(1)}, f32[6,32,128]{2,1,0:T(8,128)S(1)}, u32[]{:S(2)}, u32[]{:S(2)}) collective-permute-start(f32[6,32,128]{2,1,0:T(8,128)S(1)} %get-tuple-element.54), channel_id=1, source_target_pairs={{0,1},{1,2},{2,3},{3,0},{4,5},{5,6},{6,7},{7,4},{8,9},{9,10},{10,1... | collective-permute-start | bytes 294920 | tf_op jit(solution)/shard_map/ppermute | solution.py:744
  24.3 0.0 collective-permute-start.5
  24.3 0.5 shard_map.147.base_ref
  24.8 1.3 %collective-permute-done.xlo_ref = f32[2,32,128]{2,1,0:T(8,128)S(1)} collective-permute-done((f32[2,32,128]{2,1,0:T(8,128)S(1)}, f32[2,32,128]{2,1,0:T(8,128)S(1)}, u32[]{:S(2)}, u32[]{:S(2)}) %collective-permute-start) | collective-permute-done | bytes 32800 | tf_op jit(solution)/shard_map/ppermute | solution.py:818
  26.1 1.9 %collective-permute-start.1 = (f32[2,32,128]{2,1,0:T(8,128)S(1)}, f32[2,32,128]{2,1,0:T(8,128)S(1)}, u32[]{:S(2)}, u32[]{:S(2)}) collective-permute-start(f32[2,32,128]{2,1,0:T(8,128)S(1)} %get-tuple-element.51), channel_id=1, source_target_pairs={{16,0},{32,16},{48,32},{64,48},{80,64},{96,80},{112,96},{128,112},... | collective-permute-start | bytes 98312 | tf_op jit(solution)/shard_map/ppermute | solution.py:820
  27.9 2.6 %all-to-all-done = f32[256,1,128]{2,1,0:T(1,128)S(1)} async-done(((f32[256,1,128]{2,1,0:T(1,128)}), f32[256,1,128]{2,1,0:T(1,128)S(1)}, u32[]{:S(2)}, u32[]{:S(2)}) %all-to-all-start) | async-done | bytes 131104 | tf_op jit(solution)/shard_map/all_to_all | solution.py:814
  30.5 1.6 %shard_map.148.field_ref = f32[3,16,32,128]{3,2,1,0:T(8,128)S(1)} custom-call(s32[2,512]{1,0:T(2,128)S(1)} %get-tuple-element.44.index_ref, f32[1,512]{1,0:T(1,128)S(1)} %get-tuple-element.45.scale_ref, s32[8,128]{1,0:T(8,128)S(1)} %get-tuple-element.46.owner_ref, f32[256,128]{1,0:T(8,128)S(1)} %bitcast.9), custom_call_target="tpu_custom_call" | custom-call | flops 1073741824 | bytes 16777216 | tf_op jit(solution)/shard_map/pallas_call | solution.py:776
  32.1 0.0 collective-permute-done.2.ylo_ref
  32.1 0.0 collective-permute-done.3.yhi_ref
  32.1 0.0 collective-permute-done.1.xhi_ref
  32.1 0.0 collective-permute-done.4.zlo_ref
  32.1 0.0 collective-permute-done.5.zhi_ref
  32.2 0.8 %shard_map.149 = (f32[3,16,32,128]{3,2,1,0:T(8,128)S(1)}, f32[18,48,128]{2,1,0:T(8,128)S(1)}, f32[18,48,128]{2,1,0:T(8,128)S(1)}, f32[3,48,128]{2,1,0:T(8,128)S(1)}, f32[3,48,128]{2,1,0:T(8,128)S(1)}) custom-call(f32[3,16,32,128]{3,2,1,0:T(8,128)S(1)} %shard_map.147.base_ref, f32[3,16,32,128]{3,2,1,0:T(8,128)S(1)} %shard_map.148.field_ref, ...), custom_call_target="tpu_custom_call" | custom-call | tf_op jit(solution)/shard_map/pallas_call | solution.py:776
  32.9 0.0 collective-permute-start.6
  33.0 2.9 %collective-permute-start.7 = (f32[3,48,128]{2,1,0:T(8,128)S(1)}, f32[3,48,128]{2,1,0:T(8,128)S(1)}, u32[]{:S(2)}, u32[]{:S(2)}) collective-permute-start(f32[3,48,128]{2,1,0:T(8,128)S(1)} %get-tuple-element.61), channel_id=1, source_target_pairs={{16,0},{32,16},{48,32},{64,48},{80,64},{96,80},{112,96},{128,112},... | collective-permute-start | bytes 221192 | tf_op jit(solution)/shard_map/ppermute | solution.py:744
  35.9 1.4 %shard_map.150 = (f32[1,4]{1,0:T(1,128)}, f32[2,4]{1,0:T(2,128)}) custom-call(f32[4]{0:T(128)} %yaw_ref.3, f32[4]{0:T(128)} %ct_ref.3, f32[256,128]{1,0:T(8,128)S(1)} %bitcast.10), custom_call_target="tpu_custom_call" | custom-call | flops 536870912 | bytes 8388608 | tf_op jit(solution)/shard_map/pallas_call | solution.py:776
  37.3 0.6 %collective-permute-done.6.lo_ref = f32[3,48,128]{2,1,0:T(8,128)S(1)} collective-permute-done((f32[3,48,128]{2,1,0:T(8,128)S(1)}, f32[3,48,128]{2,1,0:T(8,128)S(1)}, u32[]{:S(2)}, u32[]{:S(2)}) %collective-permute-start.6) | collective-permute-done | bytes 73760 | tf_op jit(solution)/shard_map/ppermute | solution.py:744
  37.9 0.0 collective-permute-done.7.hi_ref
  37.9 0.5 shard_map.151
  38.4 0.6 %collective-permute-start.8 = (f32[27,8,128]{2,1,0:T(8,128)S(1)}, f32[27,8,128]{2,1,0:T(8,128)S(1)}, u32[]{:S(2)}, u32[]{:S(2)}) collective-permute-start(f32[27,8,128]{2,1,0:T(8,128)S(1)} %get-tuple-element.64), channel_id=1, source_target_pairs={{0,4},{4,8},{8,12},{12,0},{1,5},{5,9},{9,13},{13,1},{2,6},{6,10},{... | collective-permute-start | bytes 331784 | tf_op jit(solution)/shard_map/ppermute | solution.py:744
  39.0 2.7 %collective-permute-start.9 = (f32[27,8,128]{2,1,0:T(8,128)S(1)}, f32[27,8,128]{2,1,0:T(8,128)S(1)}, u32[]{:S(2)}, u32[]{:S(2)}) collective-permute-start(f32[27,8,128]{2,1,0:T(8,128)S(1)} %get-tuple-element.65), channel_id=1, source_target_pairs={{4,0},{8,4},{12,8},{0,12},{5,1},{9,5},{13,9},{1,13},{6,2},{10,6},{... | collective-permute-start | bytes 331784 | tf_op jit(solution)/shard_map/ppermute | solution.py:744
  41.7 1.8 %collective-permute-start.10 = (f32[10,32,128]{2,1,0:T(8,128)S(1)}, f32[10,32,128]{2,1,0:T(8,128)S(1)}, u32[]{:S(2)}, u32[]{:S(2)}) collective-permute-start(f32[10,32,128]{2,1,0:T(8,128)S(1)} %get-tuple-element.69), channel_id=1, source_target_pairs={{0,1},{1,2},{2,3},{3,0},{4,5},{5,6},{6,7},{7,4},{8,9},{9,10},{10,1... | collective-permute-start | bytes 491528 | tf_op jit(solution)/shard_map/ppermute | solution.py:744
  43.5 0.2 collective-permute-start.11
  43.7 1.0 %collective-permute-done.8.lo_ref = f32[27,8,128]{2,1,0:T(8,128)S(1)} collective-permute-done((f32[27,8,128]{2,1,0:T(8,128)S(1)}, f32[27,8,128]{2,1,0:T(8,128)S(1)}, u32[]{:S(2)}, u32[]{:S(2)}) %collective-permute-start.8) | collective-permute-done | bytes 110624 | tf_op jit(solution)/shard_map/ppermute | solution.py:744
  44.8 0.0 collective-permute-done.9.hi_ref
  44.8 0.2 shard_map.152
  45.0 2.1 %collective-permute-start.12 = (f32[14,8,128]{2,1,0:T(8,128)S(1)}, f32[14,8,128]{2,1,0:T(8,128)S(1)}, u32[]{:S(2)}, u32[]{:S(2)}) collective-permute-start(f32[14,8,128]{2,1,0:T(8,128)S(1)} %get-tuple-element.71), channel_id=1, source_target_pairs={{0,1},{1,2},{2,3},{3,0},{4,5},{5,6},{6,7},{7,4},{8,9},{9,10},{10,1... | collective-permute-start | bytes 172040 | tf_op jit(solution)/shard_map/ppermute | solution.py:744
  47.0 0.0 collective-permute-start.13
  47.1 0.0 copy-start
  47.1 1.2 %shard_map.153.pre_ref = f32[56,2,64,128]{3,2,1,0:T(8,128)S(1)} custom-call(f32[18,48,128]{2,1,0:T(8,128)S(1)} %get-tuple-element.66.dm_ref, f32[18,48,128]{2,1,0:T(8,128)S(1)} %get-tuple-element.67.ds_ref), custom_call_target="tpu_custom_call" | custom-call | flops 1073741824 | bytes 16777216 | tf_op jit(solution)/shard_map/pallas_call | solution.py:776
  48.3 1.5 %shard_map.154 = f32[3,16,32,128]{3,2,1,0:T(8,128)} custom-call(f32[3,16,32,128]{3,2,1,0:T(8,128)S(1)} %shard_map.148.field_ref, f32[7,16,32,128]{3,2,1,0:T(8,128)S(1)} %get-tuple-element.43.fld_ref, f32[2,32,128]{2,1,0:T(8,128)S(1)} %collective-permute-done.xlo_ref, f32[2,32,128]{2,1,0:T(8,128)S(1)} %collective-permute-done.1.xhi_ref, ...), custom_call_target="tpu_custom_call" | custom-call | flops 1073741824 | bytes 16777216 | tf_op jit(solution)/shard_map/pallas_call | solution.py:776
  49.7 0.0 collective-permute-done.10.lo_ref
  49.8 0.8 %collective-permute-done.11.hi_ref = f32[10,32,128]{2,1,0:T(8,128)S(1)} collective-permute-done((f32[10,32,128]{2,1,0:T(8,128)S(1)}, f32[10,32,128]{2,1,0:T(8,128)S(1)}, u32[]{:S(2)}, u32[]{:S(2)}) %collective-permute-start.11) | collective-permute-done | bytes 163872 | tf_op jit(solution)/shard_map/ppermute | solution.py:744
  50.6 0.0 collective-permute-done.12.late_lo_ref
  50.6 1.8 %collective-permute-done.13.late_hi_ref = f32[14,8,128]{2,1,0:T(8,128)S(1)} collective-permute-done((f32[14,8,128]{2,1,0:T(8,128)S(1)}, f32[14,8,128]{2,1,0:T(8,128)S(1)}, u32[]{:S(2)}, u32[]{:S(2)}) %collective-permute-start.13) | collective-permute-done | bytes 57376 | tf_op jit(solution)/shard_map/ppermute | solution.py:744
  52.4 0.0 copy-done
  52.4 4.4 %shard_map.155 = (f32[3,16,32,128]{3,2,1,0:T(8,128)}, f32[16,32,128]{2,1,0:T(8,128)}) custom-call(f32[18,48,128]{2,1,0:T(8,128)S(1)} %get-tuple-element.66.dm_ref, f32[18,48,128]{2,1,0:T(8,128)S(1)} %get-tuple-element.67.ds_ref, f32[56,2,64,128]{3,2,1,0:T(8,128)S(1)} %shard_map.153.pre_ref, f32[10,32,128]{2,1,0:T(8,128)S(1)} %collective-permute-done.10.lo_ref, ...), custom_call_target="tpu_custom_call" | custom-call | tf_op jit(solution)/shard_map/pallas_call | solution.py:776
Async XLA Ops:
  4.4 26.1 %all-to-all-start = ((f32[256,1,128]{2,1,0:T(1,128)}), f32[256,1,128]{2,1,0:T(1,128)S(1)}, u32[]{:S(2)}, u32[]{:S(2)}) async-start(f32[256,1,128]{2,1,0:T(1,128)} %bitcast.5), calls=%async_computation | async-start | bytes 262144 | tf_op jit(solution)/shard_map/all_to_all | solution.py:814
  18.9 7.2 %collective-permute-start = (f32[2,32,128]{2,1,0:T(8,128)S(1)}, f32[2,32,128]{2,1,0:T(8,128)S(1)}, u32[]{:S(2)}, u32[]{:S(2)}) collective-permute-start(f32[2,32,128]{2,1,0:T(8,128)S(1)} %get-tuple-element.48), channel_id=1, source_target_pairs={{0,16},{16,32},{32,48},{48,64},{64,80},{80,96},{96,112},{112,128},... | collective-permute-start | bytes 98312 | tf_op jit(solution)/shard_map/ppermute | solution.py:818
  19.0 13.1 %collective-permute-start.2 = (f32[96,128]{1,0:T(8,128)S(1)}, f32[96,128]{1,0:T(8,128)S(1)}, u32[]{:S(2)}, u32[]{:S(2)}) collective-permute-start(f32[96,128]{1,0:T(8,128)S(1)} %get-tuple-element.52), channel_id=1, source_target_pairs={{0,4},{4,8},{8,12},{12,0},{1,5},{5,9},{9,13},{13,1},{2,6},{6,10},{... | collective-permute-start | bytes 147464 | tf_op jit(solution)/shard_map/ppermute | solution.py:744
  20.5 11.6 %collective-permute-start.3 = (f32[96,128]{1,0:T(8,128)S(1)}, f32[96,128]{1,0:T(8,128)S(1)}, u32[]{:S(2)}, u32[]{:S(2)}) collective-permute-start(f32[96,128]{1,0:T(8,128)S(1)} %get-tuple-element.53), channel_id=1, source_target_pairs={{4,0},{8,4},{12,8},{0,12},{5,1},{9,5},{13,9},{1,13},{6,2},{10,6},{... | collective-permute-start | bytes 147464 | tf_op jit(solution)/shard_map/ppermute | solution.py:744
  22.3 9.9 %collective-permute-start.4 = (f32[6,32,128]{2,1,0:T(8,128)S(1)}, f32[6,32,128]{2,1,0:T(8,128)S(1)}, u32[]{:S(2)}, u32[]{:S(2)}) collective-permute-start(f32[6,32,128]{2,1,0:T(8,128)S(1)} %get-tuple-element.54), channel_id=1, source_target_pairs={{0,1},{1,2},{2,3},{3,0},{4,5},{5,6},{6,7},{7,4},{8,9},{9,10},{10,1... | collective-permute-start | bytes 294920 | tf_op jit(solution)/shard_map/ppermute | solution.py:744
  24.3 7.9 %collective-permute-start.5 = (f32[6,32,128]{2,1,0:T(8,128)S(1)}, f32[6,32,128]{2,1,0:T(8,128)S(1)}, u32[]{:S(2)}, u32[]{:S(2)}) collective-permute-start(f32[6,32,128]{2,1,0:T(8,128)S(1)} %get-tuple-element.55), channel_id=1, source_target_pairs={{1,0},{2,1},{3,2},{0,3},{5,4},{6,5},{7,6},{4,7},{9,8},{10,9},{11,1... | collective-permute-start | bytes 294920 | tf_op jit(solution)/shard_map/ppermute | solution.py:744
  26.1 6.1 %collective-permute-start.1 = (f32[2,32,128]{2,1,0:T(8,128)S(1)}, f32[2,32,128]{2,1,0:T(8,128)S(1)}, u32[]{:S(2)}, u32[]{:S(2)}) collective-permute-start(f32[2,32,128]{2,1,0:T(8,128)S(1)} %get-tuple-element.51), channel_id=1, source_target_pairs={{16,0},{32,16},{48,32},{64,48},{80,64},{96,80},{112,96},{128,112},... | collective-permute-start | bytes 98312 | tf_op jit(solution)/shard_map/ppermute | solution.py:820
  32.9 5.0 %collective-permute-start.6 = (f32[3,48,128]{2,1,0:T(8,128)S(1)}, f32[3,48,128]{2,1,0:T(8,128)S(1)}, u32[]{:S(2)}, u32[]{:S(2)}) collective-permute-start(f32[3,48,128]{2,1,0:T(8,128)S(1)} %get-tuple-element.58), channel_id=1, source_target_pairs={{0,16},{16,32},{32,48},{48,64},{64,80},{80,96},{96,112},{112,128},... | collective-permute-start | bytes 221192 | tf_op jit(solution)/shard_map/ppermute | solution.py:744
  33.0 5.0 %collective-permute-start.7 = (f32[3,48,128]{2,1,0:T(8,128)S(1)}, f32[3,48,128]{2,1,0:T(8,128)S(1)}, u32[]{:S(2)}, u32[]{:S(2)}) collective-permute-start(f32[3,48,128]{2,1,0:T(8,128)S(1)} %get-tuple-element.61), channel_id=1, source_target_pairs={{16,0},{32,16},{48,32},{64,48},{80,64},{96,80},{112,96},{128,112},... | collective-permute-start | bytes 221192 | tf_op jit(solution)/shard_map/ppermute | solution.py:744
  38.4 6.4 %collective-permute-start.8 = (f32[27,8,128]{2,1,0:T(8,128)S(1)}, f32[27,8,128]{2,1,0:T(8,128)S(1)}, u32[]{:S(2)}, u32[]{:S(2)}) collective-permute-start(f32[27,8,128]{2,1,0:T(8,128)S(1)} %get-tuple-element.64), channel_id=1, source_target_pairs={{0,4},{4,8},{8,12},{12,0},{1,5},{5,9},{9,13},{13,1},{2,6},{6,10},{... | collective-permute-start | bytes 331784 | tf_op jit(solution)/shard_map/ppermute | solution.py:744
  39.0 5.7 %collective-permute-start.9 = (f32[27,8,128]{2,1,0:T(8,128)S(1)}, f32[27,8,128]{2,1,0:T(8,128)S(1)}, u32[]{:S(2)}, u32[]{:S(2)}) collective-permute-start(f32[27,8,128]{2,1,0:T(8,128)S(1)} %get-tuple-element.65), channel_id=1, source_target_pairs={{4,0},{8,4},{12,8},{0,12},{5,1},{9,5},{13,9},{1,13},{6,2},{10,6},{... | collective-permute-start | bytes 331784 | tf_op jit(solution)/shard_map/ppermute | solution.py:744
  41.7 8.0 %collective-permute-start.10 = (f32[10,32,128]{2,1,0:T(8,128)S(1)}, f32[10,32,128]{2,1,0:T(8,128)S(1)}, u32[]{:S(2)}, u32[]{:S(2)}) collective-permute-start(f32[10,32,128]{2,1,0:T(8,128)S(1)} %get-tuple-element.69), channel_id=1, source_target_pairs={{0,1},{1,2},{2,3},{3,0},{4,5},{5,6},{6,7},{7,4},{8,9},{9,10},{10,1... | collective-permute-start | bytes 491528 | tf_op jit(solution)/shard_map/ppermute | solution.py:744
  43.5 7.1 %collective-permute-start.11 = (f32[10,32,128]{2,1,0:T(8,128)S(1)}, f32[10,32,128]{2,1,0:T(8,128)S(1)}, u32[]{:S(2)}, u32[]{:S(2)}) collective-permute-start(f32[10,32,128]{2,1,0:T(8,128)S(1)} %get-tuple-element.70), channel_id=1, source_target_pairs={{1,0},{2,1},{3,2},{0,3},{5,4},{6,5},{7,6},{4,7},{9,8},{10,9},{11,1... | collective-permute-start | bytes 491528 | tf_op jit(solution)/shard_map/ppermute | solution.py:744
  45.0 5.6 %collective-permute-start.12 = (f32[14,8,128]{2,1,0:T(8,128)S(1)}, f32[14,8,128]{2,1,0:T(8,128)S(1)}, u32[]{:S(2)}, u32[]{:S(2)}) collective-permute-start(f32[14,8,128]{2,1,0:T(8,128)S(1)} %get-tuple-element.71), channel_id=1, source_target_pairs={{0,1},{1,2},{2,3},{3,0},{4,5},{5,6},{6,7},{7,4},{8,9},{9,10},{10,1... | collective-permute-start | bytes 172040 | tf_op jit(solution)/shard_map/ppermute | solution.py:744
  47.0 5.4 %collective-permute-start.13 = (f32[14,8,128]{2,1,0:T(8,128)S(1)}, f32[14,8,128]{2,1,0:T(8,128)S(1)}, u32[]{:S(2)}, u32[]{:S(2)}) collective-permute-start(f32[14,8,128]{2,1,0:T(8,128)S(1)} %get-tuple-element.72), channel_id=1, source_target_pairs={{1,0},{2,1},{3,2},{0,3},{5,4},{6,5},{7,6},{4,7},{9,8},{10,9},{11,1... | collective-permute-start | bytes 172040 | tf_op jit(solution)/shard_map/ppermute | solution.py:744
  47.1 5.4 %copy-start = (f32[16,32,128]{2,1,0:T(8,128)S(1)}, f32[16,32,128]{2,1,0:T(8,128)}, u32[]{:S(2)}) copy-start(f32[16,32,128]{2,1,0:T(8,128)} %pres_ref.1) | copy-start | bytes 786436

commit v4 on v3

--- a/solution.py
+++ b/solution.py
@@ -702,20 +702,26 @@
 
         return get
 
-    for level in range(1, SWEEPS):
+    for level in range(1, SWEEPS - 1):
         lo, hi = pre_planes(level)
 
         def put(part, z, rows, value, level=level):
             phi_ref[level % 2, part, z, rows] = value
 
-        runs = ((level, lo), (hi, EZ - level)) if hi > lo else ((level, EZ - level),)
-        for run in runs:
+        for run in ((level, lo), (hi, EZ - level)):
             relax(level, range(*run), reader(level - 1), put, rhs, weights)
+
+    def put_last(part, z, rows, value):
+        phi_ref[(SWEEPS - 1) % 2, part, z, rows] = value
 
     get = reader(SWEEPS - 1)
     chunk = 4
     copies = []
     for c in range(CZ // chunk):
+        begin = H - 1 if c == 0 else H + 1 + c * chunk
+        relax(
+            SWEEPS - 1, range(begin, H + 1 + (c + 1) * chunk), reader(SWEEPS - 2), put_last, rhs, weights
+        )
         for z in range(c * chunk, (c + 1) * chunk):
             for t in range(CY // H):
                 rows = tile_rows(t)

time: 57.5 us -> 57.5 us (level)
  no operation moved by 1% of the time
where the time goes in v4:
time: 57.5 us; the launch traced here: 57 us
  starting transfers between devices  32.1 us (56%)
  Pallas kernels  15.8 us (27%)
  waiting for transfers between devices  8.2 us (14%)
  between operations  0.91 us (2%)
    pallas_call x10, Pallas kernels, call(): pl.pallas_call(functools.partial(kernel, Place()), out_shape=outs, in_spe...  15.8 us
    ppermute x12, starting transfers between devices, swap(): return (lax.ppermute(up, axis, forward), lax.ppermute(down, axis, backward))  15.7 us
    all_to_all x1, starting transfers between devices, shards(): got = lax.all_to_all(payload, axes, 0, 0, tiled=True)  14.4 us
    ppermute x12, waiting for transfers between devices, swap(): return (lax.ppermute(up, axis, forward), lax.ppermute(down, axis, backward))  4.32 us
    all_to_all x1, waiting for transfers between devices, shards(): got = lax.all_to_all(payload, axes, 0, 0, tiled=True)  2.6 us
    ppermute x1, starting transfers between devices, shards(): xhi = lax.ppermute(xl, 'gx', [((i + 1) % count, i) for i in range(count)])  1.87 us
    ppermute x1, waiting for transfers between devices, shards(): xlo = lax.ppermute(xr, 'gx', [(i, (i + 1) % count) for i in range(count)])  1.27 us
  transfers between devices with their start and end apart: 15, of which 6 were waited for; matrix products, arithmetic and copies ran while one was open for 0% of the time, Pallas kernels for 11%

profile of v4, /device:TPU:24, one launch (start us, length us, event | category | flops | bytes accessed | tf_op | source)
XLA Modules:
  0.0 57.0 jit_solution(13700234524473171639)
XLA Ops:
  0.6 3.8 %shard_map.146 = (f32[256,128]{1,0:T(8,128)}, f32[2,32,128]{2,1,0:T(8,128)S(1)}, f32[2,32,128]{2,1,0:T(8,128)S(1)}, f32[96,128]{1,0:T(8,128)S(1)}, f32[96,128]{1...) custom-call(f32[4]{0:T(128)} %yaw_ref.3, ...), custom_call_target="tpu_custom_call" | custom-call | tf_op jit(solution)/shard_map/pallas_call | solution.py:782
  4.4 14.4 %all-to-all-start = ((f32[256,1,128]{2,1,0:T(1,128)}), f32[256,1,128]{2,1,0:T(1,128)S(1)}, u32[]{:S(2)}, u32[]{:S(2)}) async-start(f32[256,1,128]{2,1,0:T(1,128)} %bitcast.5), calls=%async_computation | async-start | bytes 262144 | tf_op jit(solution)/shard_map/all_to_all | solution.py:820
  18.9 0.2 collective-permute-start
  19.0 1.5 %collective-permute-start.2 = (f32[96,128]{1,0:T(8,128)S(1)}, f32[96,128]{1,0:T(8,128)S(1)}, u32[]{:S(2)}, u32[]{:S(2)}) collective-permute-start(f32[96,128]{1,0:T(8,128)S(1)} %get-tuple-element.52), channel_id=1, source_target_pairs={{0,4},{4,8},{8,12},{12,0},{1,5},{5,9},{9,13},{13,1},{2,6},{6,10},{... | collective-permute-start | bytes 147464 | tf_op jit(solution)/shard_map/ppermute | solution.py:750
  20.5 1.8 %collective-permute-start.3 = (f32[96,128]{1,0:T(8,128)S(1)}, f32[96,128]{1,0:T(8,128)S(1)}, u32[]{:S(2)}, u32[]{:S(2)}) collective-permute-start(f32[96,128]{1,0:T(8,128)S(1)} %get-tuple-element.53), channel_id=1, source_target_pairs={{4,0},{8,4},{12,8},{0,12},{5,1},{9,5},{13,9},{1,13},{6,2},{10,6},{... | collective-permute-start | bytes 147464 | tf_op jit(solution)/shard_map/ppermute | solution.py:750
  22.3 2.0 %collective-permute-start.4 = (f32[6,32,128]{2,1,0:T(8,128)S(1)}, f32[6,32,128]{2,1,0:T(8,128)S(1)}, u32[]{:S(2)}, u32[]{:S(2)}) collective-permute-start(f32[6,32,128]{2,1,0:T(8,128)S(1)} %get-tuple-element.54), channel_id=1, source_target_pairs={{0,1},{1,2},{2,3},{3,0},{4,5},{5,6},{6,7},{7,4},{8,9},{9,10},{10,1... | collective-permute-start | bytes 294920 | tf_op jit(solution)/shard_map/ppermute | solution.py:750
  24.3 0.0 collective-permute-start.5
  24.3 0.5 shard_map.147.base_ref
  24.8 1.3 %collective-permute-done.xlo_ref = f32[2,32,128]{2,1,0:T(8,128)S(1)} collective-permute-done((f32[2,32,128]{2,1,0:T(8,128)S(1)}, f32[2,32,128]{2,1,0:T(8,128)S(1)}, u32[]{:S(2)}, u32[]{:S(2)}) %collective-permute-start) | collective-permute-done | bytes 32800 | tf_op jit(solution)/shard_map/ppermute | solution.py:824
  26.1 1.9 %collective-permute-start.1 = (f32[2,32,128]{2,1,0:T(8,128)S(1)}, f32[2,32,128]{2,1,0:T(8,128)S(1)}, u32[]{:S(2)}, u32[]{:S(2)}) collective-permute-start(f32[2,32,128]{2,1,0:T(8,128)S(1)} %get-tuple-element.51), channel_id=1, source_target_pairs={{16,0},{32,16},{48,32},{64,48},{80,64},{96,80},{112,96},{128,112},... | collective-permute-start | bytes 98312 | tf_op jit(solution)/shard_map/ppermute | solution.py:826
  27.9 2.6 %all-to-all-done = f32[256,1,128]{2,1,0:T(1,128)S(1)} async-done(((f32[256,1,128]{2,1,0:T(1,128)}), f32[256,1,128]{2,1,0:T(1,128)S(1)}, u32[]{:S(2)}, u32[]{:S(2)}) %all-to-all-start) | async-done | bytes 131104 | tf_op jit(solution)/shard_map/all_to_all | solution.py:820
  30.5 1.6 %shard_map.148.field_ref = f32[3,16,32,128]{3,2,1,0:T(8,128)S(1)} custom-call(s32[2,512]{1,0:T(2,128)S(1)} %get-tuple-element.44.index_ref, f32[1,512]{1,0:T(1,128)S(1)} %get-tuple-element.45.scale_ref, s32[8,128]{1,0:T(8,128)S(1)} %get-tuple-element.46.owner_ref, f32[256,128]{1,0:T(8,128)S(1)} %bitcast.9), custom_call_target="tpu_custom_call" | custom-call | flops 1073741824 | bytes 16777216 | tf_op jit(solution)/shard_map/pallas_call | solution.py:782
  32.1 0.0 collective-permute-done.2.ylo_ref
  32.1 0.0 collective-permute-done.3.yhi_ref
  32.1 0.0 collective-permute-done.1.xhi_ref
  32.1 0.0 collective-permute-done.4.zlo_ref
  32.1 0.0 collective-permute-done.5.zhi_ref
  32.2 0.8 %shard_map.149 = (f32[3,16,32,128]{3,2,1,0:T(8,128)S(1)}, f32[18,48,128]{2,1,0:T(8,128)S(1)}, f32[18,48,128]{2,1,0:T(8,128)S(1)}, f32[3,48,128]{2,1,0:T(8,128)S(1)}, f32[3,48,128]{2,1,0:T(8,128)S(1)}) custom-call(f32[3,16,32,128]{3,2,1,0:T(8,128)S(1)} %shard_map.147.base_ref, f32[3,16,32,128]{3,2,1,0:T(8,128)S(1)} %shard_map.148.field_ref, ...), custom_call_target="tpu_custom_call" | custom-call | tf_op jit(solution)/shard_map/pallas_call | solution.py:782
  32.9 0.0 collective-permute-start.6
  33.0 2.9 %collective-permute-start.7 = (f32[3,48,128]{2,1,0:T(8,128)S(1)}, f32[3,48,128]{2,1,0:T(8,128)S(1)}, u32[]{:S(2)}, u32[]{:S(2)}) collective-permute-start(f32[3,48,128]{2,1,0:T(8,128)S(1)} %get-tuple-element.61), channel_id=1, source_target_pairs={{16,0},{32,16},{48,32},{64,48},{80,64},{96,80},{112,96},{128,112},... | collective-permute-start | bytes 221192 | tf_op jit(solution)/shard_map/ppermute | solution.py:750
  35.9 1.4 %shard_map.150 = (f32[1,4]{1,0:T(1,128)}, f32[2,4]{1,0:T(2,128)}) custom-call(f32[4]{0:T(128)} %yaw_ref.3, f32[4]{0:T(128)} %ct_ref.3, f32[256,128]{1,0:T(8,128)S(1)} %bitcast.10), custom_call_target="tpu_custom_call" | custom-call | flops 536870912 | bytes 8388608 | tf_op jit(solution)/shard_map/pallas_call | solution.py:782
  37.3 0.6 %collective-permute-done.6.lo_ref = f32[3,48,128]{2,1,0:T(8,128)S(1)} collective-permute-done((f32[3,48,128]{2,1,0:T(8,128)S(1)}, f32[3,48,128]{2,1,0:T(8,128)S(1)}, u32[]{:S(2)}, u32[]{:S(2)}) %collective-permute-start.6) | collective-permute-done | bytes 73760 | tf_op jit(solution)/shard_map/ppermute | solution.py:750
  37.9 0.0 collective-permute-done.7.hi_ref
  37.9 0.5 shard_map.151
  38.4 0.6 %collective-permute-start.8 = (f32[27,8,128]{2,1,0:T(8,128)S(1)}, f32[27,8,128]{2,1,0:T(8,128)S(1)}, u32[]{:S(2)}, u32[]{:S(2)}) collective-permute-start(f32[27,8,128]{2,1,0:T(8,128)S(1)} %get-tuple-element.64), channel_id=1, source_target_pairs={{0,4},{4,8},{8,12},{12,0},{1,5},{5,9},{9,13},{13,1},{2,6},{6,10},{... | collective-permute-start | bytes 331784 | tf_op jit(solution)/shard_map/ppermute | solution.py:750
  39.0 2.7 %collective-permute-start.9 = (f32[27,8,128]{2,1,0:T(8,128)S(1)}, f32[27,8,128]{2,1,0:T(8,128)S(1)}, u32[]{:S(2)}, u32[]{:S(2)}) collective-permute-start(f32[27,8,128]{2,1,0:T(8,128)S(1)} %get-tuple-element.65), channel_id=1, source_target_pairs={{4,0},{8,4},{12,8},{0,12},{5,1},{9,5},{13,9},{1,13},{6,2},{10,6},{... | collective-permute-start | bytes 331784 | tf_op jit(solution)/shard_map/ppermute | solution.py:750
  41.7 1.8 %collective-permute-start.10 = (f32[10,32,128]{2,1,0:T(8,128)S(1)}, f32[10,32,128]{2,1,0:T(8,128)S(1)}, u32[]{:S(2)}, u32[]{:S(2)}) collective-permute-start(f32[10,32,128]{2,1,0:T(8,128)S(1)} %get-tuple-element.69), channel_id=1, source_target_pairs={{0,1},{1,2},{2,3},{3,0},{4,5},{5,6},{6,7},{7,4},{8,9},{9,10},{10,1... | collective-permute-start | bytes 491528 | tf_op jit(solution)/shard_map/ppermute | solution.py:750
  43.5 0.2 collective-permute-start.11
  43.7 1.0 %collective-permute-done.8.lo_ref = f32[27,8,128]{2,1,0:T(8,128)S(1)} collective-permute-done((f32[27,8,128]{2,1,0:T(8,128)S(1)}, f32[27,8,128]{2,1,0:T(8,128)S(1)}, u32[]{:S(2)}, u32[]{:S(2)}) %collective-permute-start.8) | collective-permute-done | bytes 110624 | tf_op jit(solution)/shard_map/ppermute | solution.py:750
  44.8 0.0 collective-permute-done.9.hi_ref
  44.8 0.2 shard_map.152
  45.0 2.1 %collective-permute-start.12 = (f32[14,8,128]{2,1,0:T(8,128)S(1)}, f32[14,8,128]{2,1,0:T(8,128)S(1)}, u32[]{:S(2)}, u32[]{:S(2)}) collective-permute-start(f32[14,8,128]{2,1,0:T(8,128)S(1)} %get-tuple-element.71), channel_id=1, source_target_pairs={{0,1},{1,2},{2,3},{3,0},{4,5},{5,6},{6,7},{7,4},{8,9},{9,10},{10,1... | collective-permute-start | bytes 172040 | tf_op jit(solution)/shard_map/ppermute | solution.py:750
  47.0 0.0 collective-permute-start.13
  47.1 0.0 copy-start
  47.1 1.2 %shard_map.153.pre_ref = f32[56,2,64,128]{3,2,1,0:T(8,128)S(1)} custom-call(f32[18,48,128]{2,1,0:T(8,128)S(1)} %get-tuple-element.66.dm_ref, f32[18,48,128]{2,1,0:T(8,128)S(1)} %get-tuple-element.67.ds_ref), custom_call_target="tpu_custom_call" | custom-call | flops 1073741824 | bytes 16777216 | tf_op jit(solution)/shard_map/pallas_call | solution.py:782
  48.3 1.5 %shard_map.154 = f32[3,16,32,128]{3,2,1,0:T(8,128)} custom-call(f32[3,16,32,128]{3,2,1,0:T(8,128)S(1)} %shard_map.148.field_ref, f32[7,16,32,128]{3,2,1,0:T(8,128)S(1)} %get-tuple-element.43.fld_ref, f32[2,32,128]{2,1,0:T(8,128)S(1)} %collective-permute-done.xlo_ref, f32[2,32,128]{2,1,0:T(8,128)S(1)} %collective-permute-done.1.xhi_ref, ...), custom_call_target="tpu_custom_call" | custom-call | flops 1073741824 | bytes 16777216 | tf_op jit(solution)/shard_map/pallas_call | solution.py:782
  49.7 0.0 collective-permute-done.10.lo_ref
  49.8 0.8 %collective-permute-done.11.hi_ref = f32[10,32,128]{2,1,0:T(8,128)S(1)} collective-permute-done((f32[10,32,128]{2,1,0:T(8,128)S(1)}, f32[10,32,128]{2,1,0:T(8,128)S(1)}, u32[]{:S(2)}, u32[]{:S(2)}) %collective-permute-start.11) | collective-permute-done | bytes 163872 | tf_op jit(solution)/shard_map/ppermute | solution.py:750
  50.6 0.0 collective-permute-done.12.late_lo_ref
  50.6 1.8 %collective-permute-done.13.late_hi_ref = f32[14,8,128]{2,1,0:T(8,128)S(1)} collective-permute-done((f32[14,8,128]{2,1,0:T(8,128)S(1)}, f32[14,8,128]{2,1,0:T(8,128)S(1)}, u32[]{:S(2)}, u32[]{:S(2)}) %collective-permute-start.13) | collective-permute-done | bytes 57376 | tf_op jit(solution)/shard_map/ppermute | solution.py:750
  52.4 0.0 copy-done
  52.4 4.4 %shard_map.155 = (f32[3,16,32,128]{3,2,1,0:T(8,128)}, f32[16,32,128]{2,1,0:T(8,128)}) custom-call(f32[18,48,128]{2,1,0:T(8,128)S(1)} %get-tuple-element.66.dm_ref, f32[18,48,128]{2,1,0:T(8,128)S(1)} %get-tuple-element.67.ds_ref, f32[56,2,64,128]{3,2,1,0:T(8,128)S(1)} %shard_map.153.pre_ref, f32[10,32,128]{2,1,0:T(8,128)S(1)} %collective-permute-done.10.lo_ref, ...), custom_call_target="tpu_custom_call" | custom-call | tf_op jit(solution)/shard_map/pallas_call | solution.py:782
Async XLA Ops:
  4.4 26.1 %all-to-all-start = ((f32[256,1,128]{2,1,0:T(1,128)}), f32[256,1,128]{2,1,0:T(1,128)S(1)}, u32[]{:S(2)}, u32[]{:S(2)}) async-start(f32[256,1,128]{2,1,0:T(1,128)} %bitcast.5), calls=%async_computation | async-start | bytes 262144 | tf_op jit(solution)/shard_map/all_to_all | solution.py:820
  18.9 7.2 %collective-permute-start = (f32[2,32,128]{2,1,0:T(8,128)S(1)}, f32[2,32,128]{2,1,0:T(8,128)S(1)}, u32[]{:S(2)}, u32[]{:S(2)}) collective-permute-start(f32[2,32,128]{2,1,0:T(8,128)S(1)} %get-tuple-element.48), channel_id=1, source_target_pairs={{0,16},{16,32},{32,48},{48,64},{64,80},{80,96},{96,112},{112,128},... | collective-permute-start | bytes 98312 | tf_op jit(solution)/shard_map/ppermute | solution.py:824
  19.0 13.1 %collective-permute-start.2 = (f32[96,128]{1,0:T(8,128)S(1)}, f32[96,128]{1,0:T(8,128)S(1)}, u32[]{:S(2)}, u32[]{:S(2)}) collective-permute-start(f32[96,128]{1,0:T(8,128)S(1)} %get-tuple-element.52), channel_id=1, source_target_pairs={{0,4},{4,8},{8,12},{12,0},{1,5},{5,9},{9,13},{13,1},{2,6},{6,10},{... | collective-permute-start | bytes 147464 | tf_op jit(solution)/shard_map/ppermute | solution.py:750
  20.5 11.6 %collective-permute-start.3 = (f32[96,128]{1,0:T(8,128)S(1)}, f32[96,128]{1,0:T(8,128)S(1)}, u32[]{:S(2)}, u32[]{:S(2)}) collective-permute-start(f32[96,128]{1,0:T(8,128)S(1)} %get-tuple-element.53), channel_id=1, source_target_pairs={{4,0},{8,4},{12,8},{0,12},{5,1},{9,5},{13,9},{1,13},{6,2},{10,6},{... | collective-permute-start | bytes 147464 | tf_op jit(solution)/shard_map/ppermute | solution.py:750
  22.3 9.9 %collective-permute-start.4 = (f32[6,32,128]{2,1,0:T(8,128)S(1)}, f32[6,32,128]{2,1,0:T(8,128)S(1)}, u32[]{:S(2)}, u32[]{:S(2)}) collective-permute-start(f32[6,32,128]{2,1,0:T(8,128)S(1)} %get-tuple-element.54), channel_id=1, source_target_pairs={{0,1},{1,2},{2,3},{3,0},{4,5},{5,6},{6,7},{7,4},{8,9},{9,10},{10,1... | collective-permute-start | bytes 294920 | tf_op jit(solution)/shard_map/ppermute | solution.py:750
  24.3 7.9 %collective-permute-start.5 = (f32[6,32,128]{2,1,0:T(8,128)S(1)}, f32[6,32,128]{2,1,0:T(8,128)S(1)}, u32[]{:S(2)}, u32[]{:S(2)}) collective-permute-start(f32[6,32,128]{2,1,0:T(8,128)S(1)} %get-tuple-element.55), channel_id=1, source_target_pairs={{1,0},{2,1},{3,2},{0,3},{5,4},{6,5},{7,6},{4,7},{9,8},{10,9},{11,1... | collective-permute-start | bytes 294920 | tf_op jit(solution)/shard_map/ppermute | solution.py:750
  26.1 6.1 %collective-permute-start.1 = (f32[2,32,128]{2,1,0:T(8,128)S(1)}, f32[2,32,128]{2,1,0:T(8,128)S(1)}, u32[]{:S(2)}, u32[]{:S(2)}) collective-permute-start(f32[2,32,128]{2,1,0:T(8,128)S(1)} %get-tuple-element.51), channel_id=1, source_target_pairs={{16,0},{32,16},{48,32},{64,48},{80,64},{96,80},{112,96},{128,112},... | collective-permute-start | bytes 98312 | tf_op jit(solution)/shard_map/ppermute | solution.py:826
  32.9 5.0 %collective-permute-start.6 = (f32[3,48,128]{2,1,0:T(8,128)S(1)}, f32[3,48,128]{2,1,0:T(8,128)S(1)}, u32[]{:S(2)}, u32[]{:S(2)}) collective-permute-start(f32[3,48,128]{2,1,0:T(8,128)S(1)} %get-tuple-element.58), channel_id=1, source_target_pairs={{0,16},{16,32},{32,48},{48,64},{64,80},{80,96},{96,112},{112,128},... | collective-permute-start | bytes 221192 | tf_op jit(solution)/shard_map/ppermute | solution.py:750
  33.0 5.0 %collective-permute-start.7 = (f32[3,48,128]{2,1,0:T(8,128)S(1)}, f32[3,48,128]{2,1,0:T(8,128)S(1)}, u32[]{:S(2)}, u32[]{:S(2)}) collective-permute-start(f32[3,48,128]{2,1,0:T(8,128)S(1)} %get-tuple-element.61), channel_id=1, source_target_pairs={{16,0},{32,16},{48,32},{64,48},{80,64},{96,80},{112,96},{128,112},... | collective-permute-start | bytes 221192 | tf_op jit(solution)/shard_map/ppermute | solution.py:750
  38.4 6.4 %collective-permute-start.8 = (f32[27,8,128]{2,1,0:T(8,128)S(1)}, f32[27,8,128]{2,1,0:T(8,128)S(1)}, u32[]{:S(2)}, u32[]{:S(2)}) collective-permute-start(f32[27,8,128]{2,1,0:T(8,128)S(1)} %get-tuple-element.64), channel_id=1, source_target_pairs={{0,4},{4,8},{8,12},{12,0},{1,5},{5,9},{9,13},{13,1},{2,6},{6,10},{... | collective-permute-start | bytes 331784 | tf_op jit(solution)/shard_map/ppermute | solution.py:750
  39.0 5.7 %collective-permute-start.9 = (f32[27,8,128]{2,1,0:T(8,128)S(1)}, f32[27,8,128]{2,1,0:T(8,128)S(1)}, u32[]{:S(2)}, u32[]{:S(2)}) collective-permute-start(f32[27,8,128]{2,1,0:T(8,128)S(1)} %get-tuple-element.65), channel_id=1, source_target_pairs={{4,0},{8,4},{12,8},{0,12},{5,1},{9,5},{13,9},{1,13},{6,2},{10,6},{... | collective-permute-start | bytes 331784 | tf_op jit(solution)/shard_map/ppermute | solution.py:750
  41.7 8.0 %collective-permute-start.10 = (f32[10,32,128]{2,1,0:T(8,128)S(1)}, f32[10,32,128]{2,1,0:T(8,128)S(1)}, u32[]{:S(2)}, u32[]{:S(2)}) collective-permute-start(f32[10,32,128]{2,1,0:T(8,128)S(1)} %get-tuple-element.69), channel_id=1, source_target_pairs={{0,1},{1,2},{2,3},{3,0},{4,5},{5,6},{6,7},{7,4},{8,9},{9,10},{10,1... | collective-permute-start | bytes 491528 | tf_op jit(solution)/shard_map/ppermute | solution.py:750
  43.5 7.1 %collective-permute-start.11 = (f32[10,32,128]{2,1,0:T(8,128)S(1)}, f32[10,32,128]{2,1,0:T(8,128)S(1)}, u32[]{:S(2)}, u32[]{:S(2)}) collective-permute-start(f32[10,32,128]{2,1,0:T(8,128)S(1)} %get-tuple-element.70), channel_id=1, source_target_pairs={{1,0},{2,1},{3,2},{0,3},{5,4},{6,5},{7,6},{4,7},{9,8},{10,9},{11,1... | collective-permute-start | bytes 491528 | tf_op jit(solution)/shard_map/ppermute | solution.py:750
  45.0 5.6 %collective-permute-start.12 = (f32[14,8,128]{2,1,0:T(8,128)S(1)}, f32[14,8,128]{2,1,0:T(8,128)S(1)}, u32[]{:S(2)}, u32[]{:S(2)}) collective-permute-start(f32[14,8,128]{2,1,0:T(8,128)S(1)} %get-tuple-element.71), channel_id=1, source_target_pairs={{0,1},{1,2},{2,3},{3,0},{4,5},{5,6},{6,7},{7,4},{8,9},{9,10},{10,1... | collective-permute-start | bytes 172040 | tf_op jit(solution)/shard_map/ppermute | solution.py:750
  47.0 5.4 %collective-permute-start.13 = (f32[14,8,128]{2,1,0:T(8,128)S(1)}, f32[14,8,128]{2,1,0:T(8,128)S(1)}, u32[]{:S(2)}, u32[]{:S(2)}) collective-permute-start(f32[14,8,128]{2,1,0:T(8,128)S(1)} %get-tuple-element.72), channel_id=1, source_target_pairs={{1,0},{2,1},{3,2},{0,3},{5,4},{6,5},{7,6},{4,7},{9,8},{10,9},{11,1... | collective-permute-start | bytes 172040 | tf_op jit(solution)/shard_map/ppermute | solution.py:750
  47.1 5.4 %copy-start = (f32[16,32,128]{2,1,0:T(8,128)S(1)}, f32[16,32,128]{2,1,0:T(8,128)}, u32[]{:S(2)}) copy-start(f32[16,32,128]{2,1,0:T(8,128)} %pres_ref.1) | copy-start | bytes 786436
